TPU v7x, 32 devices: a whole 2x2x4 slice. The times are simulated.
32 devices in a mesh: gx: 4 (over z), gy: 4 (over x, core), ha: 2 (over y).
Axes of the slice: x: 2, y: 2, z: 4, core: 2. Of those that a mesh axis runs over, the one named last changes fastest.
Arguments:
- wavefield: float32 [4, 4, 2, 32, 9, 512], P('gx', 'gy', 'ha'), may hold values from -6 to 6
- deriv_ops: float32 [3, 512, 512], replicated, may hold values from -0.25 to 0.25
- density: float32 [4, 4, 2, 32], P('gx', 'gy', 'ha'), may hold values from 1 to 3
- lame_first: float32 [4, 4, 2, 32], P('gx', 'gy', 'ha'), may hold values from 0.5 to 2
- shear_modulus: float32 [4, 4, 2, 32], P('gx', 'gy', 'ha'), may hold values from 0.3 to 1
- high_order: int32 [4, 4, 2, 32], P('gx', 'gy', 'ha'), may hold values from 0 to 1, as said below
- element_cell: int32 [4, 4, 2, 32], P('gx', 'gy', 'ha'), may hold values from 0 to 31, each once within a row
- face_orient: int32 [4, 4, 2, 6, 32], P('gx', 'gy', 'ha'), may hold values from 0 to 7
Outputs:
- advanced: float32 [4, 4, 2, 32, 9, 512], P('gx', 'gy', 'ha')
Inputs may be any that keep to these rules, and one draw needn't show every extreme that they name: `high_order`: within each group of devices along ha that share gx and gy, exactly half of the devices have 16 flagged elements and the others none; which devices and which elements are drawn. `element_cell`: on every device a permutation of the cells 0 to 31.
All inputs are finite; a program needn't handle non-finite values.
Results may differ from a plain program's by a relative error of at most 0.0001.
Values sent between devices are 32-bit elements; how exact they have to be, the bound alone decides.
No kernel may reach another device: no remote copies, remote signals or barrier semaphores. Data moves between devices by JAX's collectives and lax.ppermute only.
A program may use at most 128 MiB of HBM per device.

v0:
```python
import functools
import math

import jax
import jax.numpy as jnp
from jax import lax
from jax.experimental import pallas as pl
from jax.experimental.pallas import tpu as pltpu
from jax.sharding import PartitionSpec as P

STEPS = 2
DT = 0.8
LIFT = 2.0
PICKED = ((0, 1, 2, 3, 6, 8), (0, 1, 2, 6, 4, 7), (0, 1, 2, 8, 7, 5))
F32 = jnp.float32
BF16 = jnp.bfloat16
VMEM_LIMIT = 48 << 20


def wide(column, count):
    return jnp.concatenate([column] * count, axis=1)


def get(field, rows, cols):
    return jnp.concatenate([field[t, rows, :] for t in range(cols.start // 128, cols.stop // 128)], axis=1)


def put(field, rows, cols, value):
    for t in range(cols.start // 128, cols.stop // 128):
        field[t, rows, :] = value[:, t * 128 - cols.start : (t + 1) * 128 - cols.start]


def add(field, rows, cols, value):
    put(field, rows, cols, get(field, rows, cols) + value)


def split(value):
    high = value.astype(BF16)
    return high, (value - high.astype(F32)).astype(BF16)


def dot(left, right):
    return jnp.dot(left, right, preferred_element_type=F32)


def lanes_of(rows):
    return lax.broadcasted_iota(jnp.int32, (rows, 128), 1)


def rate(high, low, w_high, w_low, par, stride, rows, emit, block=256):
    nodes = w_high.shape[-1]
    inv_rho = wide(par[0:rows], block // 128)
    lame = wide(par[stride : stride + rows], block // 128)
    shear = wide(par[2 * stride : 2 * stride + rows], block // 128)
    shear2 = 2.0 * shear
    for start in range(0, nodes, block):
        cols = slice(start, start + block)
        deriv = []
        for dim in range(3):
            top = jnp.concatenate([high[f * stride : f * stride + rows] for f in PICKED[dim]], axis=0)
            rest = jnp.concatenate([low[f * stride : f * stride + rows] for f in PICKED[dim]], axis=0)
            both = dot(jnp.concatenate([top, rest], axis=0), w_high[dim, :, cols])
            deriv.append(both[: 6 * rows] + both[6 * rows :] + dot(top, w_low[dim, :, cols]))
        part = lambda dim, row: deriv[dim][row * rows : (row + 1) * rows]
        div = lame * (part(0, 0) + part(1, 1) + part(2, 2))
        emit(0, cols, inv_rho * (part(0, 3) + part(1, 3) + part(2, 3)))
        emit(1, cols, inv_rho * (part(0, 4) + part(1, 4) + part(2, 4)))
        emit(2, cols, inv_rho * (part(0, 5) + part(1, 5) + part(2, 5)))
        emit(3, cols, div + shear2 * part(0, 0))
        emit(4, cols, div + shear2 * part(1, 1))
        emit(5, cols, div + shear2 * part(2, 2))
        emit(6, cols, shear * (part(0, 1) + part(1, 0)))
        emit(7, cols, shear * (part(1, 2) + part(2, 1)))
        emit(8, cols, shear * (part(0, 2) + part(2, 0)))


def correction(jump, par, count, dim, rows):
    take = lambda k: par[k * count : k * count + rows] if not isinstance(rows, slice) else par[
        k * count + rows.start : k * count + rows.stop
    ]
    inv_rho, lame, shear, half_speed = take(0), take(1), take(2), take(3)
    size = jump[0].shape[0]
    sign = jnp.where(lanes_of(size) < 64, -0.5, 0.5)
    inv_rho, lame, shear = sign * inv_rho, sign * lame, sign * shear
    stiff = lame + 2.0 * shear
    if dim == 0:
        flux = [inv_rho * jump[3], inv_rho * jump[6], inv_rho * jump[8]]
        flux += [stiff * jump[0], lame * jump[0], lame * jump[0]]
        flux += [shear * jump[1], None, shear * jump[2]]
    elif dim == 1:
        flux = [inv_rho * jump[6], inv_rho * jump[4], inv_rho * jump[7]]
        flux += [lame * jump[1], stiff * jump[1], lame * jump[1]]
        flux += [shear * jump[0], shear * jump[2], None]
    else:
        flux = [inv_rho * jump[8], inv_rho * jump[7], inv_rho * jump[5]]
        flux += [lame * jump[2], lame * jump[2], stiff * jump[2]]
        flux += [None, shear * jump[1], shear * jump[0]]
    return [
        half_speed * jump[f] if flux[f] is None else half_speed * jump[f] + flux[f] for f in range(len(jump))
    ]


def orient(value, index):
    return jnp.take_along_axis(value, index, axis=1, mode="promise_in_bounds")


def lift_edges(target, face, f, rows, count):
    lanes = lanes_of(face.shape[0])
    scaled = DT * LIFT * face
    top = slice(f * count + rows.start, f * count + rows.stop)
    last = target.shape[0] - 1
    target[0, top] = target[0, top] + jnp.where(lanes < 64, scaled, 0.0)
    target[last, top] = target[last, top] + jnp.where(lanes < 64, 0.0, scaled)


def lift_inner(target, face_high, face_low, lift_table):
    rows, nodes = target.shape[1], lift_table.shape[1]
    for start in range(0, nodes, 256):
        cols = slice(start, start + 256)
        lifted = dot(face_high[...], lift_table[:, cols]) + dot(face_low[...], lift_table[:, cols])
        add(target, slice(0, rows), cols, DT * LIFT * lifted)


def predict(count, fields, q, par, w_high, w_low, face_table, cell_sm, flag_sm, outs, scratch):
    int_high, int_low, trace_x, trace_y, trace_z, edge_x, edge_y, edge_z = outs
    h0, l0, h1, l1, total, second, packed, packed_par, series, hot_rows = scratch
    nodes = h0.shape[1]
    tiles_of_node = nodes // 128
    every = slice(0, nodes)
    for f in range(fields):
        rows = slice(f * count, (f + 1) * count)
        h0[rows], l0[rows] = split(get(q, rows, every))

    def first(f, cols, value):
        rows = slice(f * count, (f + 1) * count)
        put(total, rows, cols, get(q, rows, cols) + DT / 2.0 * value)
        h1[rows, cols], l1[rows, cols] = split(value)

    rate(h0, l0, w_high, w_low, par, count, count, first)

    def then(f, cols, value):
        rows = slice(f * count, (f + 1) * count)
        add(total, rows, cols, DT**2 / 6.0 * value)
        put(second, rows, cols, value)

    rate(h1, l1, w_high, w_low, par, count, count, then)

    slot = jnp.int32(0)
    for e in range(count):
        hot_rows[slot] = cell_sm[e]
        slot = slot + flag_sm[e]
    half = count // 2

    @pl.when(slot > 0)
    def _():
        for k in range(half):
            row = hot_rows[k]
            for t in range(tiles_of_node):
                packed[t, pl.ds(k, fields, stride=count), :] = second[t, pl.ds(row, fields, stride=count), :]
            packed_par[pl.ds(k, 3, stride=count), :] = par[pl.ds(row, 3, stride=count), :]
        for f in range(fields):
            rows = slice(f * count, f * count + half)
            h0[rows], l0[rows] = split(get(packed, rows, every))
        buffers = [(h0, l0), (h1, l1)]
        for order in (3, 4, 5):
            weight = DT**order / math.factorial(order + 1)
            source, target = buffers[(order - 3) % 2], buffers[(order - 2) % 2]

            def more(f, cols, value, order=order, weight=weight, target=target):
                rows = slice(f * count, f * count + half)
                (put if order == 3 else add)(series, rows, cols, weight * value)
                if order < 5:
                    target[0][rows, cols], target[1][rows, cols] = split(value)

            rate(source[0], source[1], w_high, w_low, packed_par, count, half, more)
        for k in range(half):
            row = hot_rows[k]
            spot = pl.ds(row, fields, stride=count)
            for t in range(tiles_of_node):
                total[t, spot, :] = total[t, spot, :] + series[t, pl.ds(k, fields, stride=count), :]

    for f in range(fields):
        rows = slice(f * count, (f + 1) * count)
        int_high[rows], int_low[rows] = split(get(total, rows, every))
        trace_x[rows] = jnp.where(lanes_of(count) < 64, total[0, rows], total[tiles_of_node - 1, rows])
    faces = dot(int_high[...], face_table[...]) + dot(int_low[...], face_table[...])
    trace_y[...] = faces[:, 0:128]
    trace_z[...] = faces[:, 128:256]
    for f in range(fields):
        edge_x[f * 8 : f * 8 + 8] = jnp.where(
            lanes_of(8) < 64, trace_x[f * count : f * count + 8], trace_x[(f + 1) * count - 8 : (f + 1) * count]
        )
    tiles = fields * count // 8
    minus = lanes_of(tiles) < 64
    pad = edge_y.shape[0] // 2
    for m in range(2):
        edge_y[m * pad : m * pad + tiles] = jnp.where(
            minus, trace_y[pl.ds(m, tiles, stride=8), :], trace_y[pl.ds(6 + m, tiles, stride=8), :]
        )
        if pad > tiles:
            edge_y[m * pad + tiles : (m + 1) * pad] = jnp.zeros((pad - tiles, 128), F32)
    pairs = fields * count // 2
    edge_z[...] = jnp.where(
        lanes_of(pairs) < 64, trace_z[pl.ds(0, pairs, stride=2), :], trace_z[pl.ds(1, pairs, stride=2), :]
    )


def inner(count, fields, q, int_high, int_low, trace_x, trace_y, trace_z, par, index, w_high, w_low, lift_table,
          base, face_high, face_low):
    def volume(f, cols, value):
        rows = slice(f * count, (f + 1) * count)
        put(base, rows, cols, get(q, rows, cols) + DT * value)

    rate(int_high, int_low, w_high, w_low, par, count, count, volume)
    lanes = lanes_of(count)
    sub = lax.broadcasted_iota(jnp.int32, (count, 128), 0)
    minus = lanes < 64
    zero = jnp.zeros((8, 128), F32)
    for dim, trace in enumerate((trace_x, trace_y, trace_z)):
        jump = []
        for f in range(fields):
            own = trace[f * count : (f + 1) * count]
            if dim == 0:
                above = jnp.concatenate([own[8:], zero], axis=0)
                below = jnp.concatenate([zero, own[:-8]], axis=0)
            elif dim == 1:
                above = jnp.where(sub % 8 < 6, pltpu.roll(own, count - 2, 0), 0.0)
                below = jnp.where(sub % 8 < 2, 0.0, pltpu.roll(own, 2, 0))
            else:
                above = jnp.where(sub % 2 < 1, pltpu.roll(own, count - 1, 0), 0.0)
                below = jnp.where(sub % 2 < 1, 0.0, pltpu.roll(own, 1, 0))
            beside = jnp.where(minus, above, below)
            jump.append(orient(beside, index[dim * count : (dim + 1) * count]) - own)
        fixed = correction(jump, par, count, dim, count)
        for f in range(fields):
            if dim == 0:
                lift_edges(base, fixed[f], f, slice(0, count), count)
            else:
                cols = slice((dim - 1) * 128, dim * 128)
                rows = slice(f * count, (f + 1) * count)
                face_high[rows, cols], face_low[rows, cols] = split(fixed[f])
    lift_inner(base, face_high, face_low, lift_table)


def outer(count, fields, sizes, got, base, par, index, lift_table, out, halo, face_high, face_low):
    lower, upper = [], []
    for dim, (axis, size) in enumerate(sizes):
        here = lax.axis_index(axis)
        odd = here % 2 == 1
        first, second = got[dim]
        second = first if second is None else second
        lower.append((jnp.logical_and(odd, here > 0) if size == 2 else None, odd, here > 0, first, second))
        upper.append((None, odd, here < size - 1, first, second))

    def from_lower(dim, rows, minus):
        _, odd, there, first, second = lower[dim]
        value = jnp.where(odd, first[rows], second[rows])
        return jnp.where(jnp.logical_and(there, jnp.logical_not(minus)), value, 0.0)

    def from_upper(dim, rows, minus):
        _, odd, there, first, second = upper[dim]
        value = jnp.where(odd, second[rows], first[rows])
        return jnp.where(jnp.logical_and(there, minus), value, 0.0)

    out[...] = base[...]
    minus8 = lanes_of(8) < 64
    for end in range(2):
        rows = slice(0, 8) if end == 0 else slice(count - 8, count)
        jump = []
        for f in range(fields):
            here = slice(f * 8, f * 8 + 8)
            value = from_lower(0, here, minus8) if end == 0 else from_upper(0, here, minus8)
            jump.append(orient(value, index[rows]))
        fixed = correction(jump, par, count, 0, rows)
        for f in range(fields):
            lift_edges(out, fixed[f], f, rows, count)
    tiles = fields * count // 8
    pad = got[1][0].shape[0] // 2
    pairs = fields * count // 2
    for dim in (1, 2):
        if dim == 1:
            halo[...] = jnp.zeros_like(halo)
            minus = lanes_of(tiles) < 64
            for m in range(2):
                here = slice(m * pad, m * pad + tiles)
                halo[pl.ds(m, tiles, stride=8), :] = from_lower(1, here, minus)
                halo[pl.ds(6 + m, tiles, stride=8), :] = from_upper(1, here, minus)
        else:
            minus = lanes_of(pairs) < 64
            halo[pl.ds(0, pairs, stride=2), :] = from_lower(2, slice(0, pairs), minus)
            halo[pl.ds(1, pairs, stride=2), :] = from_upper(2, slice(0, pairs), minus)
        jump = [
            orient(halo[f * count : (f + 1) * count], index[dim * count : (dim + 1) * count]) for f in range(fields)
        ]
        fixed = correction(jump, par, count, dim, count)
        for f in range(fields):
            cols = slice((dim - 1) * 128, dim * 128)
            rows = slice(f * count, (f + 1) * count)
            face_high[rows, cols], face_low[rows, cols] = split(fixed[f])
    lift_inner(out, face_high, face_low, lift_table)


def first_kernel(count, fields, wave, ops, density, lame, shear, cell, orient_code, cell_sm, flag_sm,
                 q, w_high, w_low, par, index, face_table, lift_table, *rest):
    outs, scratch = rest[:8], rest[8:]
    staged = scratch[4]
    put(staged, slice(0, fields * count), slice(0, wave.shape[1]), wave[...])
    for e in range(count):
        for t in range(q.shape[0]):
            q[t, pl.ds(cell_sm[e], fields, stride=count), :] = staged[t, pl.ds(e, fields, stride=count), :]
    for dim in range(3):
        for start in range(0, ops.shape[1], 128):
            rows = slice(start, start + 128)
            w_high[dim, rows, :], w_low[dim, rows, :] = split(ops[dim, rows, :])
    fills = cell[...] == lax.broadcasted_iota(jnp.int32, (count, count), 0)
    in_cell = lambda row: jnp.broadcast_to(
        jnp.sum(jnp.where(fills, row, 0.0), axis=1, keepdims=True), (count, 128)
    )
    inv_rho = in_cell(1.0 / density[...])
    lame_col = in_cell(lame[...])
    shear_col = in_cell(shear[...])
    par[0:count] = inv_rho
    par[count : 2 * count] = lame_col
    par[2 * count : 3 * count] = shear_col
    par[3 * count : 4 * count] = 0.5 * jnp.sqrt((lame_col + 2.0 * shear_col) * inv_rho)
    lanes = lanes_of(count)
    p_lane, r_lane = lanes % 64 // 8, lanes % 8
    for dim in range(3):
        code = jnp.where(
            lanes < 64,
            in_cell(orient_code[2 * dim].astype(F32)),
            in_cell(orient_code[2 * dim + 1].astype(F32)),
        ).astype(jnp.int32)
        p_from = jnp.where(code % 2 == 1, 7 - p_lane, p_lane)
        r_from = jnp.where(code // 2 % 2 == 1, 7 - r_lane, r_lane)
        source = jnp.where(code >= 4, r_from * 8 + p_from, p_from * 8 + r_from)
        index[dim * count : (dim + 1) * count] = source + jnp.where(lanes < 64, 64, 0)

    def on_face(node, column):
        i, j, k = node // 64, node // 8 % 8, node % 8
        plus = column // 64 % 2 * 7
        p, r = column % 64 // 8, column % 8
        along_y = (column < 128) & (j == plus) & (i == p) & (k == r)
        along_z = (column >= 128) & (k == plus) & (i == p) & (j == r)
        return jnp.where(along_y | along_z, 1.0, 0.0).astype(BF16)

    table = (face_table.shape[0], face_table.shape[1])
    face_table[...] = on_face(lax.broadcasted_iota(jnp.int32, table, 0), lax.broadcasted_iota(jnp.int32, table, 1))
    table = table[::-1]
    lift_table[...] = on_face(lax.broadcasted_iota(jnp.int32, table, 1), lax.broadcasted_iota(jnp.int32, table, 0))
    predict(count, fields, q, par, w_high, w_low, face_table, cell_sm, flag_sm, outs, scratch)


def inner_kernel(count, fields, *refs):
    inner(count, fields, *refs)


def unpack_got(sizes, refs):
    got, at = [], 0
    for _, size in sizes:
        pair = [None, None]
        for k in range(1 if size == 2 else 2):
            pair[k] = refs[at]
            at += 1
        got.append(pair)
    return got, refs[at:]


def middle_kernel(count, fields, sizes, *refs):
    got, refs = unpack_got(sizes, refs)
    base, par, index, w_high, w_low, face_table, lift_table, cell_sm, flag_sm = refs[:9]
    q, outs = refs[9], refs[10:18]
    halo, face_high, face_low = refs[18:21]
    outer(count, fields, sizes, got, base, par, index, lift_table, q, halo, face_high, face_low)
    predict(count, fields, q, par, w_high, w_low, face_table, cell_sm, flag_sm, outs, refs[21:])


def last_kernel(count, fields, sizes, *refs):
    got, refs = unpack_got(sizes, refs)
    base, par, index, lift_table, cell_sm, out, q, staged, halo, face_high, face_low = refs
    outer(count, fields, sizes, got, base, par, index, lift_table, q, halo, face_high, face_low)
    for e in range(count):
        for t in range(q.shape[0]):
            staged[t, pl.ds(e, fields, stride=count), :] = q[t, pl.ds(cell_sm[e], fields, stride=count), :]
    out[...] = get(staged, slice(0, fields * count), slice(0, out.shape[1]))


def exchange(edges, sizes):
    got = []
    for edge, (axis, size) in zip(edges, sizes):
        first, second = [], []
        for low in range(size):
            high = (low + 1) % size
            if high == 0 and (size % 2 or size == 2):
                continue
            (second if low % 2 else first).extend([(low, high), (high, low)])
        got.append(lax.ppermute(edge, axis, first))
        if size > 2:
            got.append(lax.ppermute(edge, axis, second))
    return got


def shards(sizes, wavefield, deriv_ops, density, lame_first, shear_modulus, high_order, element_cell, face_orient):
    count, fields, nodes = wavefield.shape[-3:]
    rows = fields * count
    wave = wavefield[0, 0, 0].swapaxes(0, 1).reshape(rows, nodes)
    row = lambda value: value.reshape(1, count)
    cell_sm = element_cell.reshape(count)
    flag_sm = high_order.reshape(count)
    codes = face_orient.reshape(6, 1, count)
    vmem = pl.BlockSpec(memory_space=pltpu.VMEM)
    smem = pl.BlockSpec(memory_space=pltpu.SMEM)
    shape = jax.ShapeDtypeStruct
    field_shape = shape((nodes // 128, rows, 128), F32)
    pad = -(-(rows // 8) // 8) * 8
    predicted = [
        shape((rows, nodes), BF16),
        shape((rows, nodes), BF16),
        shape((rows, 128), F32),
        shape((rows, 128), F32),
        shape((rows, 128), F32),
        shape((fields * 8, 128), F32),
        shape((2 * pad, 128), F32),
        shape((rows // 2, 128), F32),
    ]
    predict_scratch = [
        pltpu.VMEM((rows, nodes), BF16),
        pltpu.VMEM((rows, nodes), BF16),
        pltpu.VMEM((rows, nodes), BF16),
        pltpu.VMEM((rows, nodes), BF16),
        pltpu.VMEM(field_shape.shape, F32),
        pltpu.VMEM(field_shape.shape, F32),
        pltpu.VMEM(field_shape.shape, F32),
        pltpu.VMEM((3 * count, 128), F32),
        pltpu.VMEM(field_shape.shape, F32),
        pltpu.SMEM((count + 1,), jnp.int32),
    ]
    face_scratch = [pltpu.VMEM((rows, 256), BF16), pltpu.VMEM((rows, 256), BF16)]
    halo_scratch = [pltpu.VMEM((rows, 128), F32)] + face_scratch
    params = pltpu.CompilerParams(vmem_limit_bytes=VMEM_LIMIT)

    def call(kernel, operands, in_specs, out_shape, scratch, products, name):
        single = not isinstance(out_shape, list)
        return pl.pallas_call(
            kernel,
            out_shape=out_shape,
            in_specs=in_specs,
            out_specs=vmem if single else [vmem] * len(out_shape),
            scratch_shapes=scratch,
            compiler_params=params,
            cost_estimate=pl.CostEstimate(
                flops=products * 6 * rows * nodes * nodes * 4, bytes_accessed=4 * rows * nodes * 4, transcendentals=0
            ),
            name=name,
        )(*operands)

    q, w_high, w_low, par, index, face_table, lift_table, *ahead = call(
        functools.partial(first_kernel, count, fields),
        [wave, deriv_ops, row(density), row(lame_first), row(shear_modulus), row(element_cell), codes, cell_sm, flag_sm],
        [vmem] * 7 + [smem] * 2,
        [
            field_shape,
            shape(deriv_ops.shape, BF16),
            shape(deriv_ops.shape, BF16),
            shape((4 * count, 128), F32),
            shape((3 * count, 128), jnp.int32),
            shape((nodes, 256), BF16),
            shape((256, nodes), BF16),
        ]
        + predicted,
        predict_scratch,
        4,
        "first_predictor",
    )
    for step in range(STEPS):
        traces, edges = ahead[:5], ahead[5:]
        got = exchange(edges, sizes)
        base = call(
            functools.partial(inner_kernel, count, fields),
            [q, *traces, par, index, w_high, w_low, lift_table],
            [vmem] * 11,
            field_shape,
            face_scratch,
            1,
            "inner_update",
        )
        if step < STEPS - 1:
            q, *ahead = call(
                functools.partial(middle_kernel, count, fields, sizes),
                [*got, base, par, index, w_high, w_low, face_table, lift_table, cell_sm, flag_sm],
                [vmem] * (len(got) + 7) + [smem] * 2,
                [field_shape] + predicted,
                halo_scratch + predict_scratch,
                4,
                "outer_update_predictor",
            )
        else:
            out = call(
                functools.partial(last_kernel, count, fields, sizes),
                [*got, base, par, index, lift_table, cell_sm],
                [vmem] * (len(got) + 4) + [smem],
                shape((rows, nodes), F32),
                [pltpu.VMEM(field_shape.shape, F32)] * 2 + halo_scratch,
                1,
                "outer_update",
            )
    return out.reshape(fields, count, nodes).swapaxes(0, 1)[None, None, None]


def solution(mesh):
    sizes = tuple((axis, mesh.shape[axis]) for axis in mesh.axis_names)
    lead = ("gx", "gy", "ha")
    placed = (
        P(*lead, None, None, None),
        P(),
        P(*lead, None),
        P(*lead, None),
        P(*lead, None),
        P(*lead, None),
        P(*lead, None),
        P(*lead, None, None),
    )
    return jax.shard_map(
        functools.partial(shards, sizes),
        mesh=mesh,
        in_specs=placed,
        out_specs=P(*lead, None, None, None),
        check_vma=False,
    )
```

profile of v0, /device:TPU:0, one launch (start us, length us, event | category | flops | bytes accessed | tf_op | source)
XLA Modules:
  0.0 41.9 jit_solution(17018099291143251644)
XLA Ops:
  0.0 0.0 copy-start
  0.0 1.1 %copy-done = f32[1,1,1,32,9,512]{5,3,4,2,1,0:T(8,128)S(1)} copy-done((f32[1,1,1,32,9,512]{5,3,4,2,1,0:T(8,128)S(1)}, f32[1,1,1,32,9,512]{5,3,4,2,1,0:T(8,128)}, u32[]{:S(2)}) %copy-start) | copy-done | bytes 589848
  1.1 0.0 copy-start.1
  1.1 0.7 %copy-done.1 = s32[1,1,1,6,32]{4,2,3,1,0:T(1,128)S(1)} copy-done((s32[1,1,1,6,32]{4,2,3,1,0:T(1,128)S(1)}, s32[1,1,1,6,32]{4,2,3,1,0:T(1,128)}, u32[]{:S(2)}) %copy-start.1) | copy-done | bytes 792
  1.8 0.0 copy-start.2
  1.8 0.7 %copy-done.2 = f32[1,1,1,32]{3,2,1,0:T(1,128)S(1)} copy-done((f32[1,1,1,32]{3,2,1,0:T(1,128)S(1)}, f32[1,1,1,32]{3,2,1,0:T(1,128)}, u32[]{:S(2)}) %copy-start.2) | copy-done | bytes 152
  2.4 0.0 copy-start.3
  2.4 0.7 %copy-done.3 = f32[1,1,1,32]{3,2,1,0:T(1,128)S(1)} copy-done((f32[1,1,1,32]{3,2,1,0:T(1,128)S(1)}, f32[1,1,1,32]{3,2,1,0:T(1,128)}, u32[]{:S(2)}) %copy-start.3) | copy-done | bytes 152
  3.1 0.0 copy-start.4
  3.1 0.7 %copy-done.4 = f32[1,1,1,32]{3,2,1,0:T(1,128)S(1)} copy-done((f32[1,1,1,32]{3,2,1,0:T(1,128)S(1)}, f32[1,1,1,32]{3,2,1,0:T(1,128)}, u32[]{:S(2)}) %copy-start.4) | copy-done | bytes 152
  3.7 0.0 copy-start.5
  3.7 0.7 %copy-done.5 = s32[1,1,1,32]{3,2,1,0:T(1,128)S(1)} copy-done((s32[1,1,1,32]{3,2,1,0:T(1,128)S(1)}, s32[1,1,1,32]{3,2,1,0:T(1,128)}, u32[]{:S(2)}) %copy-start.5) | copy-done | bytes 152
  4.4 0.0 copy-start.7
  4.4 0.7 %copy-done.7 = s32[1,1,1,32]{3,2,1,0:T(1,128)S(1)} copy-done((s32[1,1,1,32]{3,2,1,0:T(1,128)S(1)}, s32[1,1,1,32]{3,2,1,0:T(1,128)}, u32[]{:S(2)}) %copy-start.7) | copy-done | bytes 152
  5.0 8.8 %first_predictor.1 = (f32[4,288,128]{2,1,0:T(8,128)S(1)}, bf16[3,512,512]{2,1,0:T(8,128)(2,1)S(1)}, bf16[3,512,512]{2,1,0:T(8,128)(2,1)S(1)}, f32[128,128]{1,0:T...) custom-call(f32[288,512]{1,0:T(8,128)S(1)} %bitcast.17, ...), custom_call_target="tpu_custom_call" | custom-call | flops 7247757312 | bytes 2359296 | tf_op jit(solution)/shard_map/first_predictor/pallas_call | solution.py:444
  13.8 0.0 copy-start.9
  13.8 5.1 %collective-permute-start.1 = (f32[72,128]{1,0:T(8,128)S(1)}, f32[72,128]{1,0:T(8,128)S(1)}, u32[]{:S(2)}, u32[]{:S(2)}) collective-permute-start(f32[72,128]{1,0:T(8,128)S(1)} %get-tuple-element.29), channel_id=1, source_target_pairs={{8,16},{16,8},{24,0},{0,24},{9,17},{17,9},{25,1},{1,25},{10,18},{1... | collective-permute-start | bytes 110600 | tf_op jit(solution)/shard_map/ppermute | solution.py:399
  19.0 0.0 collective-permute-start
  19.0 0.7 %collective-permute-start.3 = (f32[80,128]{1,0:T(8,128)S(1)}, f32[80,128]{1,0:T(8,128)S(1)}, u32[]{:S(2)}, u32[]{:S(2)}) collective-permute-start(f32[80,128]{1,0:T(8,128)S(1)} %get-tuple-element.30), channel_id=1, source_target_pairs={{2,4},{4,2},{6,0},{0,6},{3,5},{5,3},{7,1},{1,7},{10,12},{12,10},{1... | collective-permute-start | bytes 122888 | tf_op jit(solution)/shard_map/ppermute | solution.py:399
  19.6 0.5 %collective-permute-start.2 = (f32[80,128]{1,0:T(8,128)S(1)}, f32[80,128]{1,0:T(8,128)S(1)}, u32[]{:S(2)}, u32[]{:S(2)}) collective-permute-start(f32[80,128]{1,0:T(8,128)S(1)} %get-tuple-element.30), channel_id=1, source_target_pairs={{0,2},{2,0},{4,6},{6,4},{1,3},{3,1},{5,7},{7,5},{8,10},{10,8},{12,... | collective-permute-start | bytes 122888 | tf_op jit(solution)/shard_map/ppermute | solution.py:397
  20.1 2.0 %collective-permute-start.4 = (f32[144,128]{1,0:T(8,128)S(1)}, f32[144,128]{1,0:T(8,128)S(1)}, u32[]{:S(2)}, u32[]{:S(2)}) collective-permute-start(f32[144,128]{1,0:T(8,128)S(1)} %get-tuple-element.31), channel_id=1, source_target_pairs={{0,1},{1,0},{2,3},{3,2},{4,5},{5,4},{6,7},{7,6},{8,9},{9,8},{10,11... | collective-permute-start | bytes 221192 | tf_op jit(solution)/shard_map/ppermute | solution.py:397
  22.1 0.0 copy-start.6
  22.1 0.0 copy-start.8
  22.1 1.3 %inner_update.2.refs_5_ = f32[4,288,128]{2,1,0:T(8,128)S(1)} custom-call(f32[4,288,128]{2,1,0:T(8,128)S(1)} %get-tuple-element.32.refs_0_, bf16[288,512]{1,0:T(8,128)(2,1)S(1)} %get-tuple-element.33.refs_1_, bf16[288,512]{1,0:T(8,128)(2,1)S(1)} %get-tuple-element.34.refs_2_, f32[288,128]{1,0:T(8,128)S(1)} %get-tuple-element.35.refs_3_, ...), custom_call_target="tpu_custom_call" | custom-call | flops 1811939328 | bytes 2359296 | tf_op jit(solution)/shard_map/inner_update/pallas_call | solution.py:444
  23.3 0.0 copy-done.9
  23.3 0.0 collective-permute-done.1.refs_1_
  23.4 0.0 collective-permute-done.refs_0_
  23.4 0.0 collective-permute-done.3.refs_3_
  23.4 0.0 collective-permute-done.2.refs_2_
  23.4 1.1 %collective-permute-done.4.refs_4_ = f32[144,128]{1,0:T(8,128)S(1)} collective-permute-done((f32[144,128]{1,0:T(8,128)S(1)}, f32[144,128]{1,0:T(8,128)S(1)}, u32[]{:S(2)}, u32[]{:S(2)}) %collective-permute-start.4) | collective-permute-done | bytes 73760 | tf_op jit(solution)/shard_map/ppermute | solution.py:397
  24.5 0.0 copy-done.6
  24.5 0.0 copy-done.8
  24.5 0.0 copy-start.10
  24.5 7.8 %outer_update_predictor.1 = (f32[4,288,128]{2,1,0:T(8,128)S(1)}, bf16[288,512]{1,0:T(8,128)(2,1)S(1)}, bf16[288,512]{1,0:T(8,128)(2,1)S(1)}, f32[288,128]{1,0:T(...) custom-call(f32[72,128]{1,0:T(8,128)S(1)} %collective-permute-done.r, ...), custom_call_target="tpu_custom_call" | custom-call | flops 7247757312 | bytes 2359296 | tf_op jit(solution)/shard_map/outer_update_predictor/pallas_call | solution.py:444
  32.3 1.0 %collective-permute-start.6 = (f32[72,128]{1,0:T(8,128)S(1)}, f32[72,128]{1,0:T(8,128)S(1)}, u32[]{:S(2)}, u32[]{:S(2)}) collective-permute-start(f32[72,128]{1,0:T(8,128)S(1)} %get-tuple-element.44), channel_id=1, source_target_pairs={{8,16},{16,8},{24,0},{0,24},{9,17},{17,9},{25,1},{1,25},{10,18},{1... | collective-permute-start | bytes 110600 | tf_op jit(solution)/shard_map/ppermute | solution.py:399
  33.3 1.2 %collective-permute-start.5 = (f32[72,128]{1,0:T(8,128)S(1)}, f32[72,128]{1,0:T(8,128)S(1)}, u32[]{:S(2)}, u32[]{:S(2)}) collective-permute-start(f32[72,128]{1,0:T(8,128)S(1)} %get-tuple-element.44), channel_id=1, source_target_pairs={{0,8},{8,0},{16,24},{24,16},{1,9},{9,1},{17,25},{25,17},{2,10},{10... | collective-permute-start | bytes 110600 | tf_op jit(solution)/shard_map/ppermute | solution.py:397
  34.5 0.0 collective-permute-start.8
  34.5 0.2 collective-permute-start.7
  34.7 2.1 %collective-permute-start.9 = (f32[144,128]{1,0:T(8,128)S(1)}, f32[144,128]{1,0:T(8,128)S(1)}, u32[]{:S(2)}, u32[]{:S(2)}) collective-permute-start(f32[144,128]{1,0:T(8,128)S(1)} %get-tuple-element.46), channel_id=1, source_target_pairs={{0,1},{1,0},{2,3},{3,2},{4,5},{5,4},{6,7},{7,6},{8,9},{9,8},{10,11... | collective-permute-start | bytes 221192 | tf_op jit(solution)/shard_map/ppermute | solution.py:397
  36.8 0.0 copy-done.10
  36.8 1.3 %inner_update.3.refs_5_ = f32[4,288,128]{2,1,0:T(8,128)S(1)} custom-call(f32[4,288,128]{2,1,0:T(8,128)S(1)} %get-tuple-element.47.refs_0_, bf16[288,512]{1,0:T(8,128)(2,1)S(1)} %get-tuple-element.48.refs_1_, bf16[288,512]{1,0:T(8,128)(2,1)S(1)} %get-tuple-element.49.refs_2_, f32[288,128]{1,0:T(8,128)S(1)} %get-tuple-element.50.refs_3_, ...), custom_call_target="tpu_custom_call" | custom-call | flops 1811939328 | bytes 2359296 | tf_op jit(solution)/shard_map/inner_update/pallas_call | solution.py:444
  38.0 0.2 collective-permute-done.6.refs_1_
  38.2 0.0 collective-permute-done.5.refs_0_
  38.2 0.0 collective-permute-done.8.refs_3_
  38.2 0.0 collective-permute-done.7.refs_2_
  38.2 1.0 %collective-permute-done.9.refs_4_ = f32[144,128]{1,0:T(8,128)S(1)} collective-permute-done((f32[144,128]{1,0:T(8,128)S(1)}, f32[144,128]{1,0:T(8,128)S(1)}, u32[]{:S(2)}, u32[]{:S(2)}) %collective-permute-start.9) | collective-permute-done | bytes 73760 | tf_op jit(solution)/shard_map/ppermute | solution.py:397
  39.2 2.7 %outer_update.1 = f32[288,512]{1,0:T(8,128)} custom-call(f32[72,128]{1,0:T(8,128)S(1)} %collective-permute-done.5.refs_0_, f32[72,128]{1,0:T(8,128)S(1)} %collective-permute-done.6.refs_1_, f32[80,128]{1,0:T(8,128)S(1)} %collective-permute-done.7.refs_2_, f32[80,128]{1,0:T(8,128)S(1)} %collective-permute-done.8.refs_3_, ...), custom_call_target="tpu_custom_call" | custom-call | flops 1811939328 | bytes 2359296 | tf_op jit(solution)/shard_map/outer_update/pallas_call | solution.py:444
Async XLA Ops:
  0.0 1.1 %copy-start = (f32[1,1,1,32,9,512]{5,3,4,2,1,0:T(8,128)S(1)}, f32[1,1,1,32,9,512]{5,3,4,2,1,0:T(8,128)}, u32[]{:S(2)}) copy-start(f32[1,1,1,32,9,512]{5,3,4,2,1,0:T(8,128)} %param.8) | copy-start | bytes 1769476
  1.1 0.7 %copy-start.1 = (s32[1,1,1,6,32]{4,2,3,1,0:T(1,128)S(1)}, s32[1,1,1,6,32]{4,2,3,1,0:T(1,128)}, u32[]{:S(2)}) copy-start(s32[1,1,1,6,32]{4,2,3,1,0:T(1,128)} %param.15) | copy-start | bytes 2308
  1.8 0.7 %copy-start.2 = (f32[1,1,1,32]{3,2,1,0:T(1,128)S(1)}, f32[1,1,1,32]{3,2,1,0:T(1,128)}, u32[]{:S(2)}) copy-start(f32[1,1,1,32]{3,2,1,0:T(1,128)} %param.10) | copy-start | bytes 388
  2.4 0.7 %copy-start.3 = (f32[1,1,1,32]{3,2,1,0:T(1,128)S(1)}, f32[1,1,1,32]{3,2,1,0:T(1,128)}, u32[]{:S(2)}) copy-start(f32[1,1,1,32]{3,2,1,0:T(1,128)} %param.11) | copy-start | bytes 388
  3.1 0.7 %copy-start.4 = (f32[1,1,1,32]{3,2,1,0:T(1,128)S(1)}, f32[1,1,1,32]{3,2,1,0:T(1,128)}, u32[]{:S(2)}) copy-start(f32[1,1,1,32]{3,2,1,0:T(1,128)} %param.12) | copy-start | bytes 388
  3.7 0.7 %copy-start.5 = (s32[1,1,1,32]{3,2,1,0:T(1,128)S(1)}, s32[1,1,1,32]{3,2,1,0:T(1,128)}, u32[]{:S(2)}) copy-start(s32[1,1,1,32]{3,2,1,0:T(1,128)} %param.13) | copy-start | bytes 388
  4.4 0.7 %copy-start.7 = (s32[1,1,1,32]{3,2,1,0:T(1,128)S(1)}, s32[1,1,1,32]{3,2,1,0:T(1,128)}, u32[]{:S(2)}) copy-start(s32[1,1,1,32]{3,2,1,0:T(1,128)} %param.14) | copy-start | bytes 388
  13.8 9.5 %copy-start.9 = (bf16[3,512,512]{2,1,0:T(8,128)(2,1)}, bf16[3,512,512]{2,1,0:T(8,128)(2,1)S(1)}, u32[]{:S(2)}) copy-start(bf16[3,512,512]{2,1,0:T(8,128)(2,1)S(1)} %get-tuple-element.41.refs_9_) | copy-start | bytes 4718596
  13.8 9.5 %collective-permute-start.1 = (f32[72,128]{1,0:T(8,128)S(1)}, f32[72,128]{1,0:T(8,128)S(1)}, u32[]{:S(2)}, u32[]{:S(2)}) collective-permute-start(f32[72,128]{1,0:T(8,128)S(1)} %get-tuple-element.29), channel_id=1, source_target_pairs={{8,16},{16,8},{24,0},{0,24},{9,17},{17,9},{25,1},{1,25},{10,18},{1... | collective-permute-start | bytes 110600 | tf_op jit(solution)/shard_map/ppermute | solution.py:399
  19.0 4.4 %collective-permute-start = (f32[72,128]{1,0:T(8,128)S(1)}, f32[72,128]{1,0:T(8,128)S(1)}, u32[]{:S(2)}, u32[]{:S(2)}) collective-permute-start(f32[72,128]{1,0:T(8,128)S(1)} %get-tuple-element.29), channel_id=1, source_target_pairs={{0,8},{8,0},{16,24},{24,16},{1,9},{9,1},{17,25},{25,17},{2,10},{10... | collective-permute-start | bytes 110600 | tf_op jit(solution)/shard_map/ppermute | solution.py:397
  19.0 4.4 %collective-permute-start.3 = (f32[80,128]{1,0:T(8,128)S(1)}, f32[80,128]{1,0:T(8,128)S(1)}, u32[]{:S(2)}, u32[]{:S(2)}) collective-permute-start(f32[80,128]{1,0:T(8,128)S(1)} %get-tuple-element.30), channel_id=1, source_target_pairs={{2,4},{4,2},{6,0},{0,6},{3,5},{5,3},{7,1},{1,7},{10,12},{12,10},{1... | collective-permute-start | bytes 122888 | tf_op jit(solution)/shard_map/ppermute | solution.py:399
  19.6 3.8 %collective-permute-start.2 = (f32[80,128]{1,0:T(8,128)S(1)}, f32[80,128]{1,0:T(8,128)S(1)}, u32[]{:S(2)}, u32[]{:S(2)}) collective-permute-start(f32[80,128]{1,0:T(8,128)S(1)} %get-tuple-element.30), channel_id=1, source_target_pairs={{0,2},{2,0},{4,6},{6,4},{1,3},{3,1},{5,7},{7,5},{8,10},{10,8},{12,... | collective-permute-start | bytes 122888 | tf_op jit(solution)/shard_map/ppermute | solution.py:397
  20.1 4.4 %collective-permute-start.4 = (f32[144,128]{1,0:T(8,128)S(1)}, f32[144,128]{1,0:T(8,128)S(1)}, u32[]{:S(2)}, u32[]{:S(2)}) collective-permute-start(f32[144,128]{1,0:T(8,128)S(1)} %get-tuple-element.31), channel_id=1, source_target_pairs={{0,1},{1,0},{2,3},{3,2},{4,5},{5,4},{6,7},{7,6},{8,9},{9,8},{10,11... | collective-permute-start | bytes 221192 | tf_op jit(solution)/shard_map/ppermute | solution.py:397
  22.1 2.4 %copy-start.6 = (s32[1,1,1,32]{3,2,1,0:T(1,128)S(1)}, s32[1,1,1,32]{3,2,1,0:T(1,128)}, u32[]{:S(2)}) copy-start(s32[1,1,1,32]{3,2,1,0:T(1,128)} %param.13) | copy-start | bytes 388
  22.1 2.4 %copy-start.8 = (s32[1,1,1,32]{3,2,1,0:T(1,128)S(1)}, s32[1,1,1,32]{3,2,1,0:T(1,128)}, u32[]{:S(2)}) copy-start(s32[1,1,1,32]{3,2,1,0:T(1,128)} %param.14) | copy-start | bytes 388
  24.5 12.3 %copy-start.10 = (bf16[3,512,512]{2,1,0:T(8,128)(2,1)S(1)}, bf16[3,512,512]{2,1,0:T(8,128)(2,1)}, u32[]{:S(2)}) copy-start(bf16[3,512,512]{2,1,0:T(8,128)(2,1)} %copy-done.9) | copy-start | bytes 4718596
  32.3 5.9 %collective-permute-start.6 = (f32[72,128]{1,0:T(8,128)S(1)}, f32[72,128]{1,0:T(8,128)S(1)}, u32[]{:S(2)}, u32[]{:S(2)}) collective-permute-start(f32[72,128]{1,0:T(8,128)S(1)} %get-tuple-element.44), channel_id=1, source_target_pairs={{8,16},{16,8},{24,0},{0,24},{9,17},{17,9},{25,1},{1,25},{10,18},{1... | collective-permute-start | bytes 110600 | tf_op jit(solution)/shard_map/ppermute | solution.py:399
  33.3 4.9 %collective-permute-start.5 = (f32[72,128]{1,0:T(8,128)S(1)}, f32[72,128]{1,0:T(8,128)S(1)}, u32[]{:S(2)}, u32[]{:S(2)}) collective-permute-start(f32[72,128]{1,0:T(8,128)S(1)} %get-tuple-element.44), channel_id=1, source_target_pairs={{0,8},{8,0},{16,24},{24,16},{1,9},{9,1},{17,25},{25,17},{2,10},{10... | collective-permute-start | bytes 110600 | tf_op jit(solution)/shard_map/ppermute | solution.py:397
  34.5 3.7 %collective-permute-start.8 = (f32[80,128]{1,0:T(8,128)S(1)}, f32[80,128]{1,0:T(8,128)S(1)}, u32[]{:S(2)}, u32[]{:S(2)}) collective-permute-start(f32[80,128]{1,0:T(8,128)S(1)} %get-tuple-element.45), channel_id=1, source_target_pairs={{2,4},{4,2},{6,0},{0,6},{3,5},{5,3},{7,1},{1,7},{10,12},{12,10},{1... | collective-permute-start | bytes 122888 | tf_op jit(solution)/shard_map/ppermute | solution.py:399
  34.5 3.7 %collective-permute-start.7 = (f32[80,128]{1,0:T(8,128)S(1)}, f32[80,128]{1,0:T(8,128)S(1)}, u32[]{:S(2)}, u32[]{:S(2)}) collective-permute-start(f32[80,128]{1,0:T(8,128)S(1)} %get-tuple-element.45), channel_id=1, source_target_pairs={{0,2},{2,0},{4,6},{6,4},{1,3},{3,1},{5,7},{7,5},{8,10},{10,8},{12,... | collective-permute-start | bytes 122888 | tf_op jit(solution)/shard_map/ppermute | solution.py:397
  34.7 4.5 %collective-permute-start.9 = (f32[144,128]{1,0:T(8,128)S(1)}, f32[144,128]{1,0:T(8,128)S(1)}, u32[]{:S(2)}, u32[]{:S(2)}) collective-permute-start(f32[144,128]{1,0:T(8,128)S(1)} %get-tuple-element.46), channel_id=1, source_target_pairs={{0,1},{1,0},{2,3},{3,2},{4,5},{5,4},{6,7},{7,6},{8,9},{9,8},{10,11... | collective-permute-start | bytes 221192 | tf_op jit(solution)/shard_map/ppermute | solution.py:397
where the time goes:
time: 42.3 us; the launch traced here: 41.9 us
  Pallas kernels  21.8 us (52%)
  starting transfers between devices  12.7 us (30%)
  local copies, waits for them, and re-layouts  5.04 us (12%)
  waiting for transfers between devices  2.27 us (5%)
    pallas_call x5, Pallas kernels, call(): pl.pallas_call(kernel, out_shape=out_shape, in_specs=in_specs, out_specs=...  21.8 us
    ppermute x4, starting transfers between devices, exchange(): got.append(lax.ppermute(edge, axis, second))  6.82 us
    ppermute x6, starting transfers between devices, exchange(): got.append(lax.ppermute(edge, axis, first))  5.88 us
    unnamed x22, local copies, waits for them, and re-layouts  5.04 us
    ppermute x6, waiting for transfers between devices, exchange(): got.append(lax.ppermute(edge, axis, first))  2.1 us
  transfers between devices with their start and end apart: 10, of which 3 were waited for; matrix products, arithmetic and copies ran while one was open for 0% of the time, Pallas kernels for 6%

commit v1 on v0

--- a/solution.py
+++ b/solution.py
@@ -1,4 +1,5 @@
 import functools
+import itertools
 import math
 
 import jax
@@ -14,7 +15,7 @@
 PICKED = ((0, 1, 2, 3, 6, 8), (0, 1, 2, 6, 4, 7), (0, 1, 2, 8, 7, 5))
 F32 = jnp.float32
 BF16 = jnp.bfloat16
-VMEM_LIMIT = 48 << 20
+VMEM_LIMIT = 24 << 20
 
 
 def wide(column, count):
@@ -119,6 +120,13 @@
         cols = slice(start, start + 256)
         lifted = dot(face_high[...], lift_table[:, cols]) + dot(face_low[...], lift_table[:, cols])
         add(target, slice(0, rows), cols, DT * LIFT * lifted)
+
+
+def fetch(copies):
+    started = [pltpu.make_async_copy(*copy) for copy in copies]
+    for copy in started:
+        copy.start()
+    return started
 
 
 def predict(count, fields, q, par, w_high, w_low, face_table, cell_sm, flag_sm, outs, scratch):
@@ -300,18 +308,19 @@
     lift_inner(out, face_high, face_low, lift_table)
 
 
-def first_kernel(count, fields, wave, ops, density, lame, shear, cell, orient_code, cell_sm, flag_sm,
-                 q, w_high, w_low, par, index, face_table, lift_table, *rest):
-    outs, scratch = rest[:8], rest[8:]
+def first_kernel(count, fields, wave, ops_any, density_any, lame_any, shear_any, cell_any, orient_any, cells_any,
+                 flags_any, q, w_high, w_low, par, index, face_table, lift_table, *rest):
+    outs, scratch = rest[:8], rest[8:18]
+    ops, density, lame, shear, cell, orient_code, cell_sm, flag_sm, sems = rest[18:]
     staged = scratch[4]
-    put(staged, slice(0, fields * count), slice(0, wave.shape[1]), wave[...])
-    for e in range(count):
-        for t in range(q.shape[0]):
-            q[t, pl.ds(cell_sm[e], fields, stride=count), :] = staged[t, pl.ds(e, fields, stride=count), :]
-    for dim in range(3):
-        for start in range(0, ops.shape[1], 128):
-            rows = slice(start, start + 128)
-            w_high[dim, rows, :], w_low[dim, rows, :] = split(ops[dim, rows, :])
+    tiles_of_node = q.shape[0]
+    pairs = [(density_any, density), (lame_any, lame), (shear_any, shear), (cell_any, cell)]
+    pairs += [(orient_any, orient_code), (cells_any, cell_sm), (flags_any, flag_sm)]
+    pairs += [(wave.at[:, t * 128 : (t + 1) * 128], staged.at[t]) for t in range(tiles_of_node)]
+    pairs += [(ops_any.at[dim], ops.at[dim]) for dim in range(3)]
+    waits = fetch([(*pair, sems.at[k]) for k, pair in enumerate(pairs)])
+    for wait in waits[:7]:
+        wait.wait()
     fills = cell[...] == lax.broadcasted_iota(jnp.int32, (count, count), 0)
     in_cell = lambda row: jnp.broadcast_to(
         jnp.sum(jnp.where(fills, row, 0.0), axis=1, keepdims=True), (count, 128)
@@ -348,6 +357,16 @@
     face_table[...] = on_face(lax.broadcasted_iota(jnp.int32, table, 0), lax.broadcasted_iota(jnp.int32, table, 1))
     table = table[::-1]
     lift_table[...] = on_face(lax.broadcasted_iota(jnp.int32, table, 1), lax.broadcasted_iota(jnp.int32, table, 0))
+    for wait in waits[7 : 7 + tiles_of_node]:
+        wait.wait()
+    for e in range(count):
+        for t in range(tiles_of_node):
+            q[t, pl.ds(cell_sm[e], fields, stride=count), :] = staged[t, pl.ds(e, fields, stride=count), :]
+    for dim in range(3):
+        waits[7 + tiles_of_node + dim].wait()
+        for start in range(0, ops.shape[1], 128):
+            rows = slice(start, start + 128)
+            w_high[dim, rows, :], w_low[dim, rows, :] = split(ops[dim, rows, :])
     predict(count, fields, q, par, w_high, w_low, face_table, cell_sm, flag_sm, outs, scratch)
 
 
@@ -368,35 +387,57 @@
 
 def middle_kernel(count, fields, sizes, *refs):
     got, refs = unpack_got(sizes, refs)
-    base, par, index, w_high, w_low, face_table, lift_table, cell_sm, flag_sm = refs[:9]
+    base, par, index, w_high, w_low, face_table, lift_table, cells_any, flags_any = refs[:9]
     q, outs = refs[9], refs[10:18]
     halo, face_high, face_low = refs[18:21]
+    scratch, (cell_sm, flag_sm, sems) = refs[21:31], refs[31:]
+    waits = fetch([(cells_any, cell_sm, sems.at[0]), (flags_any, flag_sm, sems.at[1])])
     outer(count, fields, sizes, got, base, par, index, lift_table, q, halo, face_high, face_low)
-    predict(count, fields, q, par, w_high, w_low, face_table, cell_sm, flag_sm, outs, refs[21:])
+    for wait in waits:
+        wait.wait()
+    predict(count, fields, q, par, w_high, w_low, face_table, cell_sm, flag_sm, outs, scratch)
 
 
 def last_kernel(count, fields, sizes, *refs):
     got, refs = unpack_got(sizes, refs)
-    base, par, index, lift_table, cell_sm, out, q, staged, halo, face_high, face_low = refs
+    base, par, index, lift_table, cells_any, out, q, staged, halo, face_high, face_low, cell_sm, sems = refs
+    tiles_of_node = q.shape[0]
+    waits = fetch([(cells_any, cell_sm, sems.at[tiles_of_node])])
     outer(count, fields, sizes, got, base, par, index, lift_table, q, halo, face_high, face_low)
-    for e in range(count):
-        for t in range(q.shape[0]):
+    waits[0].wait()
+    done = []
+    for t in range(tiles_of_node):
+        for e in range(count):
             staged[t, pl.ds(e, fields, stride=count), :] = q[t, pl.ds(cell_sm[e], fields, stride=count), :]
-    out[...] = get(staged, slice(0, fields * count), slice(0, out.shape[1]))
+        done += fetch([(staged.at[t], out.at[:, t * 128 : (t + 1) * 128], sems.at[t])])
+    for wait in done:
+        wait.wait()
+
+
+def swaps(sizes, dim, parity):
+    lengths = [size for _, size in sizes]
+    size, pairs = lengths[dim], []
+    for place in itertools.product(*[range(length) for length in lengths]):
+        other = list(place)
+        other[dim] += 1 if place[dim] % 2 == parity else -1
+        if not 0 <= other[dim] < size:
+            if dim == 0 and lengths[1] % 2 == 0:
+                other[dim], other[1] = place[dim], place[1] ^ 1
+            else:
+                other[dim] = other[dim] % size if size % 2 == 0 else place[dim]
+        flat = [0, 0]
+        for length, mine, theirs in zip(lengths, place, other):
+            flat = [flat[0] * length + mine, flat[1] * length + theirs]
+        pairs.append(tuple(flat))
+    return pairs
 
 
 def exchange(edges, sizes):
+    axes = tuple(axis for axis, _ in sizes)
     got = []
-    for edge, (axis, size) in zip(edges, sizes):
-        first, second = [], []
-        for low in range(size):
-            high = (low + 1) % size
-            if high == 0 and (size % 2 or size == 2):
-                continue
-            (second if low % 2 else first).extend([(low, high), (high, low)])
-        got.append(lax.ppermute(edge, axis, first))
-        if size > 2:
-            got.append(lax.ppermute(edge, axis, second))
+    for dim, edge in enumerate(edges):
+        for parity in range(1 if sizes[dim][1] == 2 else 2):
+            got.append(lax.ppermute(edge, axes, swaps(sizes, dim, parity)))
     return got
 
 
@@ -409,7 +450,8 @@
     flag_sm = high_order.reshape(count)
     codes = face_orient.reshape(6, 1, count)
     vmem = pl.BlockSpec(memory_space=pltpu.VMEM)
-    smem = pl.BlockSpec(memory_space=pltpu.SMEM)
+    hbm = pl.BlockSpec(memory_space=pltpu.HBM)
+    index_scratch = pltpu.SMEM((count,), jnp.int32)
     shape = jax.ShapeDtypeStruct
     field_shape = shape((nodes // 128, rows, 128), F32)
     pad = -(-(rows // 8) // 8) * 8
@@ -439,13 +481,13 @@
     halo_scratch = [pltpu.VMEM((rows, 128), F32)] + face_scratch
     params = pltpu.CompilerParams(vmem_limit_bytes=VMEM_LIMIT)
 
-    def call(kernel, operands, in_specs, out_shape, scratch, products, name):
+    def call(kernel, operands, in_specs, out_shape, scratch, products, name, out_spec=vmem):
         single = not isinstance(out_shape, list)
         return pl.pallas_call(
             kernel,
             out_shape=out_shape,
             in_specs=in_specs,
-            out_specs=vmem if single else [vmem] * len(out_shape),
+            out_specs=out_spec if single else [out_spec] * len(out_shape),
             scratch_shapes=scratch,
             compiler_params=params,
             cost_estimate=pl.CostEstimate(
@@ -457,7 +499,7 @@
     q, w_high, w_low, par, index, face_table, lift_table, *ahead = call(
         functools.partial(first_kernel, count, fields),
         [wave, deriv_ops, row(density), row(lame_first), row(shear_modulus), row(element_cell), codes, cell_sm, flag_sm],
-        [vmem] * 7 + [smem] * 2,
+        [hbm] * 9,
         [
             field_shape,
             shape(deriv_ops.shape, BF16),
@@ -468,7 +510,18 @@
             shape((256, nodes), BF16),
         ]
         + predicted,
-        predict_scratch,
+        predict_scratch
+        + [
+            pltpu.VMEM(deriv_ops.shape, F32),
+            pltpu.VMEM((1, count), F32),
+            pltpu.VMEM((1, count), F32),
+            pltpu.VMEM((1, count), F32),
+            pltpu.VMEM((1, count), jnp.int32),
+            pltpu.VMEM((6, 1, count), jnp.int32),
+            index_scratch,
+            index_scratch,
+            pltpu.SemaphoreType.DMA((10 + nodes // 128,)),
+        ],
         4,
         "first_predictor",
     )
@@ -488,9 +541,9 @@
             q, *ahead = call(
                 functools.partial(middle_kernel, count, fields, sizes),
                 [*got, base, par, index, w_high, w_low, face_table, lift_table, cell_sm, flag_sm],
-                [vmem] * (len(got) + 7) + [smem] * 2,
+                [vmem] * (len(got) + 7) + [hbm] * 2,
                 [field_shape] + predicted,
-                halo_scratch + predict_scratch,
+                halo_scratch + predict_scratch + [index_scratch, index_scratch, pltpu.SemaphoreType.DMA((2,))],
                 4,
                 "outer_update_predictor",
             )
@@ -498,11 +551,14 @@
             out = call(
                 functools.partial(last_kernel, count, fields, sizes),
                 [*got, base, par, index, lift_table, cell_sm],
-                [vmem] * (len(got) + 4) + [smem],
+                [vmem] * (len(got) + 4) + [hbm],
                 shape((rows, nodes), F32),
-                [pltpu.VMEM(field_shape.shape, F32)] * 2 + halo_scratch,
+                [pltpu.VMEM(field_shape.shape, F32)] * 2
+                + halo_scratch
+                + [index_scratch, pltpu.SemaphoreType.DMA((nodes // 128 + 1,))],
                 1,
                 "outer_update",
+                hbm,
             )
     return out.reshape(fields, count, nodes).swapaxes(0, 1)[None, None, None]
 

time: 42.3 us -> 40.8 us (0.965)
  Pallas kernels: 21.8 us -> 13 us
  starting transfers between devices: 12.7 us -> 18.2 us
  local copies, waits for them, and re-layouts: 5.04 us -> 6.92 us
    pallas_call x5, Pallas kernels: 21.8 us -> 13 us  [call(): pl.pallas_call(kernel, out_shape=out_shape, in_specs=in_specs, out_specs=...]
    ppermute x10, starting transfers between devices: 12.7 us -> 18.2 us  [exchange(): got.append(lax.ppermute(edge, axes, swaps(sizes, dim, parity)))]
    unnamed x22 -> x20, local copies, waits for them, and re-layouts: 5.04 us -> 6.92 us
  transfers between devices with their start and end apart: 10 -> 10, of which waited for: 3 -> 2; matrix products, arithmetic and copies ran while one was open for 0% -> 0% of each run, Pallas kernels for 6% -> 6%
where the time goes in v1:
time: 40.8 us; the launch traced here: 40.6 us
  starting transfers between devices  18.2 us (45%)
  Pallas kernels  13 us (32%)
  local copies, waits for them, and re-layouts  6.92 us (17%)
  waiting for transfers between devices  2.22 us (5%)
    ppermute x10, starting transfers between devices, exchange(): got.append(lax.ppermute(edge, axes, swaps(sizes, dim, parity)))  18.2 us
    pallas_call x5, Pallas kernels, call(): pl.pallas_call(kernel, out_shape=out_shape, in_specs=in_specs, out_specs=...  13 us
    unnamed x20, local copies, waits for them, and re-layouts  6.92 us
    ppermute x10, waiting for transfers between devices, exchange(): got.append(lax.ppermute(edge, axes, swaps(sizes, dim, parity)))  2.22 us
  transfers between devices with their start and end apart: 10, of which 2 were waited for; matrix products, arithmetic and copies ran while one was open for 0% of the time, Pallas kernels for 6%

profile of v1, /device:TPU:0, one launch (start us, length us, event | category | flops | bytes accessed | tf_op | source)
XLA Modules:
  0.0 40.6 jit_solution(15813281362653195717)
XLA Ops:
  0.0 0.0 copy-start
  0.0 1.9 %copy-done = f32[3,512,512]{2,1,0:T(8,128)S(1)} copy-done((f32[3,512,512]{2,1,0:T(8,128)S(1)}, f32[3,512,512]{2,1,0:T(8,128)}, u32[]{:S(2)}) %copy-start) | copy-done | bytes 3145752
  1.9 0.0 copy-start.1
  1.9 1.1 %copy-done.1 = f32[1,1,1,32,9,512]{5,3,4,2,1,0:T(8,128)S(1)} copy-done((f32[1,1,1,32,9,512]{5,3,4,2,1,0:T(8,128)S(1)}, f32[1,1,1,32,9,512]{5,3,4,2,1,0:T(8,128)}, u32[]{:S(2)}) %copy-start.1) | copy-done | bytes 589848
  3.0 0.0 copy-start.2
  3.0 0.7 %copy-done.2 = s32[1,1,1,6,32]{4,2,3,1,0:T(1,128)S(1)} copy-done((s32[1,1,1,6,32]{4,2,3,1,0:T(1,128)S(1)}, s32[1,1,1,6,32]{4,2,3,1,0:T(1,128)}, u32[]{:S(2)}) %copy-start.2) | copy-done | bytes 792
  3.6 0.0 copy-start.3
  3.6 0.7 %copy-done.3 = f32[1,1,1,32]{3,2,1,0:T(1,128)S(1)} copy-done((f32[1,1,1,32]{3,2,1,0:T(1,128)S(1)}, f32[1,1,1,32]{3,2,1,0:T(1,128)}, u32[]{:S(2)}) %copy-start.3) | copy-done | bytes 152
  4.3 0.0 copy-start.4
  4.3 0.7 %copy-done.4 = f32[1,1,1,32]{3,2,1,0:T(1,128)S(1)} copy-done((f32[1,1,1,32]{3,2,1,0:T(1,128)S(1)}, f32[1,1,1,32]{3,2,1,0:T(1,128)}, u32[]{:S(2)}) %copy-start.4) | copy-done | bytes 152
  5.0 0.0 copy-start.5
  5.0 0.7 %copy-done.5 = f32[1,1,1,32]{3,2,1,0:T(1,128)S(1)} copy-done((f32[1,1,1,32]{3,2,1,0:T(1,128)S(1)}, f32[1,1,1,32]{3,2,1,0:T(1,128)}, u32[]{:S(2)}) %copy-start.5) | copy-done | bytes 152
  5.6 0.0 copy-start.6
  5.6 0.7 %copy-done.6 = s32[1,1,1,32]{3,2,1,0:T(1,128)S(1)} copy-done((s32[1,1,1,32]{3,2,1,0:T(1,128)S(1)}, s32[1,1,1,32]{3,2,1,0:T(1,128)}, u32[]{:S(2)}) %copy-start.6) | copy-done | bytes 152
  6.3 0.0 copy-start.8
  6.3 0.7 %copy-done.8 = s32[1,1,1,32]{3,2,1,0:T(1,128)S(1)} copy-done((s32[1,1,1,32]{3,2,1,0:T(1,128)S(1)}, s32[1,1,1,32]{3,2,1,0:T(1,128)}, u32[]{:S(2)}) %copy-start.8) | copy-done | bytes 152
  6.9 4.9 %first_predictor.1 = (f32[4,288,128]{2,1,0:T(8,128)S(1)}, bf16[3,512,512]{2,1,0:T(8,128)(2,1)S(1)}, bf16[3,512,512]{2,1,0:T(8,128)(2,1)S(1)}, f32[128,128]{1,0:T...) custom-call(f32[288,512]{1,0:T(8,128)S(1)} %bitcast.17, ...), custom_call_target="tpu_custom_call" | custom-call | flops 7247757312 | bytes 2359296 | tf_op jit(solution)/shard_map/first_predictor/pallas_call | solution.py:486
  11.9 3.6 %collective-permute-start.1 = (f32[72,128]{1,0:T(8,128)S(1)}, f32[72,128]{1,0:T(8,128)S(1)}, u32[]{:S(2)}, u32[]{:S(2)}) collective-permute-start(f32[72,128]{1,0:T(8,128)S(1)} %get-tuple-element.29), channel_id=1, source_target_pairs={{0,2},{1,3},{2,0},{3,1},{4,6},{5,7},{6,4},{7,5},{8,16},{9,17},{10,... | collective-permute-start | bytes 110600 | tf_op jit(solution)/shard_map/ppermute | solution.py:440
  15.4 4.2 %collective-permute-start = (f32[72,128]{1,0:T(8,128)S(1)}, f32[72,128]{1,0:T(8,128)S(1)}, u32[]{:S(2)}, u32[]{:S(2)}) collective-permute-start(f32[72,128]{1,0:T(8,128)S(1)} %get-tuple-element.29), channel_id=1, source_target_pairs={{0,8},{1,9},{2,10},{3,11},{4,12},{5,13},{6,14},{7,15},{8,0},{9,1},... | collective-permute-start | bytes 110600 | tf_op jit(solution)/shard_map/ppermute | solution.py:440
  19.6 0.4 collective-permute-start.3
  20.0 0.0 collective-permute-start.2
  20.0 2.8 %collective-permute-start.4 = (f32[144,128]{1,0:T(8,128)S(1)}, f32[144,128]{1,0:T(8,128)S(1)}, u32[]{:S(2)}, u32[]{:S(2)}) collective-permute-start(f32[144,128]{1,0:T(8,128)S(1)} %get-tuple-element.31), channel_id=1, source_target_pairs={{0,1},{1,0},{2,3},{3,2},{4,5},{5,4},{6,7},{7,6},{8,9},{9,8},{10,11... | collective-permute-start | bytes 221192 | tf_op jit(solution)/shard_map/ppermute | solution.py:440
  22.7 0.0 copy-start.7
  22.7 0.0 copy-start.9
  22.7 1.3 %inner_update.2.refs_5_ = f32[4,288,128]{2,1,0:T(8,128)S(1)} custom-call(f32[4,288,128]{2,1,0:T(8,128)S(1)} %get-tuple-element.32.refs_0_, bf16[288,512]{1,0:T(8,128)(2,1)S(1)} %get-tuple-element.33.refs_1_, bf16[288,512]{1,0:T(8,128)(2,1)S(1)} %get-tuple-element.34.refs_2_, f32[288,128]{1,0:T(8,128)S(1)} %get-tuple-element.35.refs_3_, ...), custom_call_target="tpu_custom_call" | custom-call | flops 1811939328 | bytes 2359296 | tf_op jit(solution)/shard_map/inner_update/pallas_call | solution.py:486
  24.0 0.0 collective-permute-done.1.refs_1_
  24.0 0.0 collective-permute-done.refs_0_
  24.0 0.0 collective-permute-done.3.refs_3_
  24.0 0.0 collective-permute-done.2.refs_2_
  24.1 1.1 %collective-permute-done.4.refs_4_ = f32[144,128]{1,0:T(8,128)S(1)} collective-permute-done((f32[144,128]{1,0:T(8,128)S(1)}, f32[144,128]{1,0:T(8,128)S(1)}, u32[]{:S(2)}, u32[]{:S(2)}) %collective-permute-start.4) | collective-permute-done | bytes 73760 | tf_op jit(solution)/shard_map/ppermute | solution.py:440
  25.2 0.0 copy-done.7
  25.2 0.0 copy-done.9
  25.2 3.6 %outer_update_predictor.1 = (f32[4,288,128]{2,1,0:T(8,128)S(1)}, bf16[288,512]{1,0:T(8,128)(2,1)S(1)}, bf16[288,512]{1,0:T(8,128)(2,1)S(1)}, f32[288,128]{1,0:T(...) custom-call(f32[72,128]{1,0:T(8,128)S(1)} %collective-permute-done.r, ...), custom_call_target="tpu_custom_call" | custom-call | flops 7247757312 | bytes 2359296 | tf_op jit(solution)/shard_map/outer_update_predictor/pallas_call | solution.py:486
  28.7 2.6 %collective-permute-start.6 = (f32[72,128]{1,0:T(8,128)S(1)}, f32[72,128]{1,0:T(8,128)S(1)}, u32[]{:S(2)}, u32[]{:S(2)}) collective-permute-start(f32[72,128]{1,0:T(8,128)S(1)} %get-tuple-element.44), channel_id=1, source_target_pairs={{0,2},{1,3},{2,0},{3,1},{4,6},{5,7},{6,4},{7,5},{8,16},{9,17},{10,... | collective-permute-start | bytes 110600 | tf_op jit(solution)/shard_map/ppermute | solution.py:440
  31.3 2.4 %collective-permute-start.5 = (f32[72,128]{1,0:T(8,128)S(1)}, f32[72,128]{1,0:T(8,128)S(1)}, u32[]{:S(2)}, u32[]{:S(2)}) collective-permute-start(f32[72,128]{1,0:T(8,128)S(1)} %get-tuple-element.44), channel_id=1, source_target_pairs={{0,8},{1,9},{2,10},{3,11},{4,12},{5,13},{6,14},{7,15},{8,0},{9,1},... | collective-permute-start | bytes 110600 | tf_op jit(solution)/shard_map/ppermute | solution.py:440
  33.7 0.0 collective-permute-start.8
  33.7 0.0 collective-permute-start.7
  33.7 2.4 %collective-permute-start.9 = (f32[144,128]{1,0:T(8,128)S(1)}, f32[144,128]{1,0:T(8,128)S(1)}, u32[]{:S(2)}, u32[]{:S(2)}) collective-permute-start(f32[144,128]{1,0:T(8,128)S(1)} %get-tuple-element.46), channel_id=1, source_target_pairs={{0,1},{1,0},{2,3},{3,2},{4,5},{5,4},{6,7},{7,6},{8,9},{9,8},{10,11... | collective-permute-start | bytes 221192 | tf_op jit(solution)/shard_map/ppermute | solution.py:440
  36.1 1.3 %inner_update.3.refs_5_ = f32[4,288,128]{2,1,0:T(8,128)S(1)} custom-call(f32[4,288,128]{2,1,0:T(8,128)S(1)} %get-tuple-element.47.refs_0_, bf16[288,512]{1,0:T(8,128)(2,1)S(1)} %get-tuple-element.48.refs_1_, bf16[288,512]{1,0:T(8,128)(2,1)S(1)} %get-tuple-element.49.refs_2_, f32[288,128]{1,0:T(8,128)S(1)} %get-tuple-element.50.refs_3_, ...), custom_call_target="tpu_custom_call" | custom-call | flops 1811939328 | bytes 2359296 | tf_op jit(solution)/shard_map/inner_update/pallas_call | solution.py:486
  37.4 0.0 collective-permute-done.6.refs_1_
  37.4 0.0 collective-permute-done.5.refs_0_
  37.4 0.0 collective-permute-done.8.refs_3_
  37.4 0.0 collective-permute-done.7.refs_2_
  37.4 1.1 %collective-permute-done.9.refs_4_ = f32[144,128]{1,0:T(8,128)S(1)} collective-permute-done((f32[144,128]{1,0:T(8,128)S(1)}, f32[144,128]{1,0:T(8,128)S(1)}, u32[]{:S(2)}, u32[]{:S(2)}) %collective-permute-start.9) | collective-permute-done | bytes 73760 | tf_op jit(solution)/shard_map/ppermute | solution.py:440
  38.5 1.9 %outer_update.1 = f32[288,512]{1,0:T(8,128)} custom-call(f32[72,128]{1,0:T(8,128)S(1)} %collective-permute-done.5.refs_0_, f32[72,128]{1,0:T(8,128)S(1)} %collective-permute-done.6.refs_1_, f32[80,128]{1,0:T(8,128)S(1)} %collective-permute-done.7.refs_2_, f32[80,128]{1,0:T(8,128)S(1)} %collective-permute-done.8.refs_3_, ...), custom_call_target="tpu_custom_call" | custom-call | flops 1811939328 | bytes 2359296 | tf_op jit(solution)/shard_map/outer_update/pallas_call | solution.py:486
Async XLA Ops:
  0.0 1.9 %copy-start = (f32[3,512,512]{2,1,0:T(8,128)S(1)}, f32[3,512,512]{2,1,0:T(8,128)}, u32[]{:S(2)}) copy-start(f32[3,512,512]{2,1,0:T(8,128)} %ops_any.1) | copy-start | bytes 9437188
  1.9 1.1 %copy-start.1 = (f32[1,1,1,32,9,512]{5,3,4,2,1,0:T(8,128)S(1)}, f32[1,1,1,32,9,512]{5,3,4,2,1,0:T(8,128)}, u32[]{:S(2)}) copy-start(f32[1,1,1,32,9,512]{5,3,4,2,1,0:T(8,128)} %param.8) | copy-start | bytes 1769476
  3.0 0.7 %copy-start.2 = (s32[1,1,1,6,32]{4,2,3,1,0:T(1,128)S(1)}, s32[1,1,1,6,32]{4,2,3,1,0:T(1,128)}, u32[]{:S(2)}) copy-start(s32[1,1,1,6,32]{4,2,3,1,0:T(1,128)} %param.15) | copy-start | bytes 2308
  3.6 0.7 %copy-start.3 = (f32[1,1,1,32]{3,2,1,0:T(1,128)S(1)}, f32[1,1,1,32]{3,2,1,0:T(1,128)}, u32[]{:S(2)}) copy-start(f32[1,1,1,32]{3,2,1,0:T(1,128)} %param.10) | copy-start | bytes 388
  4.3 0.7 %copy-start.4 = (f32[1,1,1,32]{3,2,1,0:T(1,128)S(1)}, f32[1,1,1,32]{3,2,1,0:T(1,128)}, u32[]{:S(2)}) copy-start(f32[1,1,1,32]{3,2,1,0:T(1,128)} %param.11) | copy-start | bytes 388
  5.0 0.7 %copy-start.5 = (f32[1,1,1,32]{3,2,1,0:T(1,128)S(1)}, f32[1,1,1,32]{3,2,1,0:T(1,128)}, u32[]{:S(2)}) copy-start(f32[1,1,1,32]{3,2,1,0:T(1,128)} %param.12) | copy-start | bytes 388
  5.6 0.7 %copy-start.6 = (s32[1,1,1,32]{3,2,1,0:T(1,128)S(1)}, s32[1,1,1,32]{3,2,1,0:T(1,128)}, u32[]{:S(2)}) copy-start(s32[1,1,1,32]{3,2,1,0:T(1,128)} %param.13) | copy-start | bytes 388
  6.3 0.7 %copy-start.8 = (s32[1,1,1,32]{3,2,1,0:T(1,128)S(1)}, s32[1,1,1,32]{3,2,1,0:T(1,128)}, u32[]{:S(2)}) copy-start(s32[1,1,1,32]{3,2,1,0:T(1,128)} %param.14) | copy-start | bytes 388
  11.9 12.1 %collective-permute-start.1 = (f32[72,128]{1,0:T(8,128)S(1)}, f32[72,128]{1,0:T(8,128)S(1)}, u32[]{:S(2)}, u32[]{:S(2)}) collective-permute-start(f32[72,128]{1,0:T(8,128)S(1)} %get-tuple-element.29), channel_id=1, source_target_pairs={{0,2},{1,3},{2,0},{3,1},{4,6},{5,7},{6,4},{7,5},{8,16},{9,17},{10,... | collective-permute-start | bytes 110600 | tf_op jit(solution)/shard_map/ppermute | solution.py:440
  15.4 8.6 %collective-permute-start = (f32[72,128]{1,0:T(8,128)S(1)}, f32[72,128]{1,0:T(8,128)S(1)}, u32[]{:S(2)}, u32[]{:S(2)}) collective-permute-start(f32[72,128]{1,0:T(8,128)S(1)} %get-tuple-element.29), channel_id=1, source_target_pairs={{0,8},{1,9},{2,10},{3,11},{4,12},{5,13},{6,14},{7,15},{8,0},{9,1},... | collective-permute-start | bytes 110600 | tf_op jit(solution)/shard_map/ppermute | solution.py:440
  19.6 4.4 %collective-permute-start.3 = (f32[80,128]{1,0:T(8,128)S(1)}, f32[80,128]{1,0:T(8,128)S(1)}, u32[]{:S(2)}, u32[]{:S(2)}) collective-permute-start(f32[80,128]{1,0:T(8,128)S(1)} %get-tuple-element.30), channel_id=1, source_target_pairs={{0,6},{1,7},{2,4},{3,5},{4,2},{5,3},{6,0},{7,1},{8,14},{9,15},{10,... | collective-permute-start | bytes 122888 | tf_op jit(solution)/shard_map/ppermute | solution.py:440
  20.0 4.1 %collective-permute-start.2 = (f32[80,128]{1,0:T(8,128)S(1)}, f32[80,128]{1,0:T(8,128)S(1)}, u32[]{:S(2)}, u32[]{:S(2)}) collective-permute-start(f32[80,128]{1,0:T(8,128)S(1)} %get-tuple-element.30), channel_id=1, source_target_pairs={{0,2},{1,3},{2,0},{3,1},{4,6},{5,7},{6,4},{7,5},{8,10},{9,11},{10,... | collective-permute-start | bytes 122888 | tf_op jit(solution)/shard_map/ppermute | solution.py:440
  20.0 5.2 %collective-permute-start.4 = (f32[144,128]{1,0:T(8,128)S(1)}, f32[144,128]{1,0:T(8,128)S(1)}, u32[]{:S(2)}, u32[]{:S(2)}) collective-permute-start(f32[144,128]{1,0:T(8,128)S(1)} %get-tuple-element.31), channel_id=1, source_target_pairs={{0,1},{1,0},{2,3},{3,2},{4,5},{5,4},{6,7},{7,6},{8,9},{9,8},{10,11... | collective-permute-start | bytes 221192 | tf_op jit(solution)/shard_map/ppermute | solution.py:440
  22.7 2.4 %copy-start.7 = (s32[1,1,1,32]{3,2,1,0:T(1,128)S(1)}, s32[1,1,1,32]{3,2,1,0:T(1,128)}, u32[]{:S(2)}) copy-start(s32[1,1,1,32]{3,2,1,0:T(1,128)} %param.13) | copy-start | bytes 388
  22.7 2.4 %copy-start.9 = (s32[1,1,1,32]{3,2,1,0:T(1,128)S(1)}, s32[1,1,1,32]{3,2,1,0:T(1,128)}, u32[]{:S(2)}) copy-start(s32[1,1,1,32]{3,2,1,0:T(1,128)} %param.14) | copy-start | bytes 388
  28.7 8.6 %collective-permute-start.6 = (f32[72,128]{1,0:T(8,128)S(1)}, f32[72,128]{1,0:T(8,128)S(1)}, u32[]{:S(2)}, u32[]{:S(2)}) collective-permute-start(f32[72,128]{1,0:T(8,128)S(1)} %get-tuple-element.44), channel_id=1, source_target_pairs={{0,2},{1,3},{2,0},{3,1},{4,6},{5,7},{6,4},{7,5},{8,16},{9,17},{10,... | collective-permute-start | bytes 110600 | tf_op jit(solution)/shard_map/ppermute | solution.py:440
  31.3 6.1 %collective-permute-start.5 = (f32[72,128]{1,0:T(8,128)S(1)}, f32[72,128]{1,0:T(8,128)S(1)}, u32[]{:S(2)}, u32[]{:S(2)}) collective-permute-start(f32[72,128]{1,0:T(8,128)S(1)} %get-tuple-element.44), channel_id=1, source_target_pairs={{0,8},{1,9},{2,10},{3,11},{4,12},{5,13},{6,14},{7,15},{8,0},{9,1},... | collective-permute-start | bytes 110600 | tf_op jit(solution)/shard_map/ppermute | solution.py:440
  33.7 3.7 %collective-permute-start.8 = (f32[80,128]{1,0:T(8,128)S(1)}, f32[80,128]{1,0:T(8,128)S(1)}, u32[]{:S(2)}, u32[]{:S(2)}) collective-permute-start(f32[80,128]{1,0:T(8,128)S(1)} %get-tuple-element.45), channel_id=1, source_target_pairs={{0,6},{1,7},{2,4},{3,5},{4,2},{5,3},{6,0},{7,1},{8,14},{9,15},{10,... | collective-permute-start | bytes 122888 | tf_op jit(solution)/shard_map/ppermute | solution.py:440
  33.7 3.7 %collective-permute-start.7 = (f32[80,128]{1,0:T(8,128)S(1)}, f32[80,128]{1,0:T(8,128)S(1)}, u32[]{:S(2)}, u32[]{:S(2)}) collective-permute-start(f32[80,128]{1,0:T(8,128)S(1)} %get-tuple-element.45), channel_id=1, source_target_pairs={{0,2},{1,3},{2,0},{3,1},{4,6},{5,7},{6,4},{7,5},{8,10},{9,11},{10,... | collective-permute-start | bytes 122888 | tf_op jit(solution)/shard_map/ppermute | solution.py:440
  33.7 4.8 %collective-permute-start.9 = (f32[144,128]{1,0:T(8,128)S(1)}, f32[144,128]{1,0:T(8,128)S(1)}, u32[]{:S(2)}, u32[]{:S(2)}) collective-permute-start(f32[144,128]{1,0:T(8,128)S(1)} %get-tuple-element.46), channel_id=1, source_target_pairs={{0,1},{1,0},{2,3},{3,2},{4,5},{5,4},{6,7},{7,6},{8,9},{9,8},{10,11... | collective-permute-start | bytes 221192 | tf_op jit(solution)/shard_map/ppermute | solution.py:440

commit v2 on v1

--- a/solution.py
+++ b/solution.py
@@ -16,6 +16,7 @@
 F32 = jnp.float32
 BF16 = jnp.bfloat16
 VMEM_LIMIT = 24 << 20
+TABLE_LIMIT = 50 << 20
 
 
 def wide(column, count):
@@ -308,19 +309,36 @@
     lift_inner(out, face_high, face_low, lift_table)
 
 
-def first_kernel(count, fields, wave, ops_any, density_any, lame_any, shear_any, cell_any, orient_any, cells_any,
-                 flags_any, q, w_high, w_low, par, index, face_table, lift_table, *rest):
+def table_kernel(ops_any, w_high, w_low, face_table, lift_table, ops, sems):
+    dims, nodes = ops.shape[:2]
+    step = nodes // 2
+    parts = [(dim, slice(start, start + step)) for dim in range(dims) for start in range(0, nodes, step)]
+    waits = fetch([(ops_any.at[dim, rows], ops.at[dim, rows], sems.at[k]) for k, (dim, rows) in enumerate(parts)])
+
+    def on_face(node, column):
+        i, j, k = node // 64, node // 8 % 8, node % 8
+        plus = column // 64 % 2 * 7
+        p, r = column % 64 // 8, column % 8
+        along_y = (column < 128) & (j == plus) & (i == p) & (k == r)
+        along_z = (column >= 128) & (k == plus) & (i == p) & (j == r)
+        return jnp.where(along_y | along_z, 1.0, 0.0).astype(BF16)
+
+    table = face_table.shape
+    face_table[...] = on_face(lax.broadcasted_iota(jnp.int32, table, 0), lax.broadcasted_iota(jnp.int32, table, 1))
+    table = table[::-1]
+    lift_table[...] = on_face(lax.broadcasted_iota(jnp.int32, table, 1), lax.broadcasted_iota(jnp.int32, table, 0))
+    for wait, (dim, rows) in zip(waits, parts):
+        wait.wait()
+        w_high[dim, rows, :], w_low[dim, rows, :] = split(ops[dim, rows, :])
+
+
+def first_kernel(count, fields, wave, density, lame, shear, cell, orient_code, cells_any, flags_any,
+                 w_high, w_low, face_table, q, par, index, *rest):
     outs, scratch = rest[:8], rest[8:18]
-    ops, density, lame, shear, cell, orient_code, cell_sm, flag_sm, sems = rest[18:]
+    cell_sm, flag_sm, sems = rest[18:]
+    waits = fetch([(cells_any, cell_sm, sems.at[0]), (flags_any, flag_sm, sems.at[1])])
     staged = scratch[4]
-    tiles_of_node = q.shape[0]
-    pairs = [(density_any, density), (lame_any, lame), (shear_any, shear), (cell_any, cell)]
-    pairs += [(orient_any, orient_code), (cells_any, cell_sm), (flags_any, flag_sm)]
-    pairs += [(wave.at[:, t * 128 : (t + 1) * 128], staged.at[t]) for t in range(tiles_of_node)]
-    pairs += [(ops_any.at[dim], ops.at[dim]) for dim in range(3)]
-    waits = fetch([(*pair, sems.at[k]) for k, pair in enumerate(pairs)])
-    for wait in waits[:7]:
-        wait.wait()
+    put(staged, slice(0, fields * count), slice(0, wave.shape[1]), wave[...])
     fills = cell[...] == lax.broadcasted_iota(jnp.int32, (count, count), 0)
     in_cell = lambda row: jnp.broadcast_to(
         jnp.sum(jnp.where(fills, row, 0.0), axis=1, keepdims=True), (count, 128)
@@ -344,29 +362,11 @@
         r_from = jnp.where(code // 2 % 2 == 1, 7 - r_lane, r_lane)
         source = jnp.where(code >= 4, r_from * 8 + p_from, p_from * 8 + r_from)
         index[dim * count : (dim + 1) * count] = source + jnp.where(lanes < 64, 64, 0)
-
-    def on_face(node, column):
-        i, j, k = node // 64, node // 8 % 8, node % 8
-        plus = column // 64 % 2 * 7
-        p, r = column % 64 // 8, column % 8
-        along_y = (column < 128) & (j == plus) & (i == p) & (k == r)
-        along_z = (column >= 128) & (k == plus) & (i == p) & (j == r)
-        return jnp.where(along_y | along_z, 1.0, 0.0).astype(BF16)
-
-    table = (face_table.shape[0], face_table.shape[1])
-    face_table[...] = on_face(lax.broadcasted_iota(jnp.int32, table, 0), lax.broadcasted_iota(jnp.int32, table, 1))
-    table = table[::-1]
-    lift_table[...] = on_face(lax.broadcasted_iota(jnp.int32, table, 1), lax.broadcasted_iota(jnp.int32, table, 0))
-    for wait in waits[7 : 7 + tiles_of_node]:
+    for wait in waits:
         wait.wait()
     for e in range(count):
-        for t in range(tiles_of_node):
+        for t in range(q.shape[0]):
             q[t, pl.ds(cell_sm[e], fields, stride=count), :] = staged[t, pl.ds(e, fields, stride=count), :]
-    for dim in range(3):
-        waits[7 + tiles_of_node + dim].wait()
-        for start in range(0, ops.shape[1], 128):
-            rows = slice(start, start + 128)
-            w_high[dim, rows, :], w_low[dim, rows, :] = split(ops[dim, rows, :])
     predict(count, fields, q, par, w_high, w_low, face_table, cell_sm, flag_sm, outs, scratch)
 
 
@@ -479,9 +479,8 @@
     ]
     face_scratch = [pltpu.VMEM((rows, 256), BF16), pltpu.VMEM((rows, 256), BF16)]
     halo_scratch = [pltpu.VMEM((rows, 128), F32)] + face_scratch
-    params = pltpu.CompilerParams(vmem_limit_bytes=VMEM_LIMIT)
-
-    def call(kernel, operands, in_specs, out_shape, scratch, products, name, out_spec=vmem):
+
+    def call(kernel, operands, in_specs, out_shape, scratch, products, name, out_spec=vmem, limit=VMEM_LIMIT):
         single = not isinstance(out_shape, list)
         return pl.pallas_call(
             kernel,
@@ -489,39 +488,35 @@
             in_specs=in_specs,
             out_specs=out_spec if single else [out_spec] * len(out_shape),
             scratch_shapes=scratch,
-            compiler_params=params,
+            compiler_params=pltpu.CompilerParams(vmem_limit_bytes=limit),
             cost_estimate=pl.CostEstimate(
                 flops=products * 6 * rows * nodes * nodes * 4, bytes_accessed=4 * rows * nodes * 4, transcendentals=0
             ),
             name=name,
         )(*operands)
 
-    q, w_high, w_low, par, index, face_table, lift_table, *ahead = call(
-        functools.partial(first_kernel, count, fields),
-        [wave, deriv_ops, row(density), row(lame_first), row(shear_modulus), row(element_cell), codes, cell_sm, flag_sm],
-        [hbm] * 9,
+    w_high, w_low, face_table, lift_table = call(
+        table_kernel,
+        [deriv_ops],
+        [hbm],
         [
-            field_shape,
             shape(deriv_ops.shape, BF16),
             shape(deriv_ops.shape, BF16),
-            shape((4 * count, 128), F32),
-            shape((3 * count, 128), jnp.int32),
             shape((nodes, 256), BF16),
             shape((256, nodes), BF16),
-        ]
-        + predicted,
-        predict_scratch
-        + [
-            pltpu.VMEM(deriv_ops.shape, F32),
-            pltpu.VMEM((1, count), F32),
-            pltpu.VMEM((1, count), F32),
-            pltpu.VMEM((1, count), F32),
-            pltpu.VMEM((1, count), jnp.int32),
-            pltpu.VMEM((6, 1, count), jnp.int32),
-            index_scratch,
-            index_scratch,
-            pltpu.SemaphoreType.DMA((10 + nodes // 128,)),
         ],
+        [pltpu.VMEM(deriv_ops.shape, F32), pltpu.SemaphoreType.DMA((2 * deriv_ops.shape[0],))],
+        2,
+        "split_operators",
+        limit=TABLE_LIMIT,
+    )
+    q, par, index, *ahead = call(
+        functools.partial(first_kernel, count, fields),
+        [wave, row(density), row(lame_first), row(shear_modulus), row(element_cell), codes, cell_sm, flag_sm]
+        + [w_high, w_low, face_table],
+        [vmem] * 6 + [hbm] * 2 + [vmem] * 3,
+        [field_shape, shape((4 * count, 128), F32), shape((3 * count, 128), jnp.int32)] + predicted,
+        predict_scratch + [index_scratch, index_scratch, pltpu.SemaphoreType.DMA((2,))],
         4,
         "first_predictor",
     )

time: 40.8 us -> 34.6 us (0.85)
  local copies, waits for them, and re-layouts: 6.92 us -> 0.03 us
  Pallas kernels: 13 us -> 13.9 us
  starting transfers between devices: 18.2 us -> 17.5 us
    unnamed x20 -> x14, local copies, waits for them, and re-layouts: 6.92 us -> 0.03 us
    pallas_call x5 -> x6, Pallas kernels: 13 us -> 13.9 us  [call(): pl.pallas_call(kernel, out_shape=out_shape, in_specs=in_specs, out_specs=...]
    ppermute x10, starting transfers between devices: 18.2 us -> 17.5 us  [exchange(): got.append(lax.ppermute(edge, axes, swaps(sizes, dim, parity)))]
  transfers between devices with their start and end apart: 10 -> 10, of which waited for: 2 -> 2; matrix products, arithmetic and copies ran while one was open for 0% -> 0% of each run, Pallas kernels for 6% -> 7%
where the time goes in v2:
time: 34.6 us; the launch traced here: 34.3 us
  starting transfers between devices  17.5 us (51%)
  Pallas kernels  13.9 us (40%)
  waiting for transfers between devices  2.45 us (7%)
  between operations  0.35 us (1%)
    ppermute x10, starting transfers between devices, exchange(): got.append(lax.ppermute(edge, axes, swaps(sizes, dim, parity)))  17.5 us
    pallas_call x6, Pallas kernels, call(): pl.pallas_call(kernel, out_shape=out_shape, in_specs=in_specs, out_specs=...  13.9 us
    ppermute x10, waiting for transfers between devices, exchange(): got.append(lax.ppermute(edge, axes, swaps(sizes, dim, parity)))  2.45 us
  transfers between devices with their start and end apart: 10, of which 2 were waited for; matrix products, arithmetic and copies ran while one was open for 0% of the time, Pallas kernels for 7%

profile of v2, /device:TPU:0, one launch (start us, length us, event | category | flops | bytes accessed | tf_op | source)
XLA Modules:
  0.0 34.3 jit_solution(4038893738074261690)
XLA Ops:
  0.0 0.0 copy-start.6
  0.0 0.0 copy-start.1
  0.0 0.0 copy-start.5
  0.0 0.0 copy-start.4
  0.0 0.0 copy-start.3
  0.0 0.0 copy-start.2
  0.0 0.0 copy-start
  0.0 2.0 %split_operators.1 = (bf16[3,512,512]{2,1,0:T(8,128)(2,1)S(1)}, bf16[3,512,512]{2,1,0:T(8,128)(2,1)S(1)}, bf16[512,256]{1,0:T(8,128)(2,1)S(1)}, bf16[256,512]{1,0:T(8,128)(2,1)S(1)}) custom-call(f32[3,512,512]{2,1,0:T(8,128)} %ops_any.1), custom_call_target="tpu_custom_call" | custom-call | flops 3623878656 | bytes 2359296 | tf_op jit(solution)/shard_map/split_operators/pallas_call | solution.py:485
  2.1 0.0 copy-done.6
  2.1 0.0 copy-done.1
  2.1 0.0 copy-done.5
  2.1 0.0 copy-done.4
  2.1 0.0 copy-done.3
  2.1 0.0 copy-done.2
  2.2 0.0 copy-done
  2.2 3.9 %first_predictor.1 = (f32[4,288,128]{2,1,0:T(8,128)S(1)}, f32[128,128]{1,0:T(8,128)S(1)}, s32[96,128]{1,0:T(8,128)S(1)}, bf16[288,512]{1,0:T(8,128)(2,1)S(1)}, b...) custom-call(f32[288,512]{1,0:T(8,128)S(1)} %bitcast.17, ...), custom_call_target="tpu_custom_call" | custom-call | flops 7247757312 | bytes 2359296 | tf_op jit(solution)/shard_map/first_predictor/pallas_call | solution.py:485
  6.1 0.5 %collective-permute-start.1 = (f32[72,128]{1,0:T(8,128)S(1)}, f32[72,128]{1,0:T(8,128)S(1)}, u32[]{:S(2)}, u32[]{:S(2)}) collective-permute-start(f32[72,128]{1,0:T(8,128)S(1)} %get-tuple-element.32), channel_id=1, source_target_pairs={{0,2},{1,3},{2,0},{3,1},{4,6},{5,7},{6,4},{7,5},{8,16},{9,17},{10,... | collective-permute-start | bytes 110600 | tf_op jit(solution)/shard_map/ppermute | solution.py:440
  6.6 5.6 %collective-permute-start = (f32[72,128]{1,0:T(8,128)S(1)}, f32[72,128]{1,0:T(8,128)S(1)}, u32[]{:S(2)}, u32[]{:S(2)}) collective-permute-start(f32[72,128]{1,0:T(8,128)S(1)} %get-tuple-element.32), channel_id=1, source_target_pairs={{0,8},{1,9},{2,10},{3,11},{4,12},{5,13},{6,14},{7,15},{8,0},{9,1},... | collective-permute-start | bytes 110600 | tf_op jit(solution)/shard_map/ppermute | solution.py:440
  12.2 0.7 %collective-permute-start.3 = (f32[80,128]{1,0:T(8,128)S(1)}, f32[80,128]{1,0:T(8,128)S(1)}, u32[]{:S(2)}, u32[]{:S(2)}) collective-permute-start(f32[80,128]{1,0:T(8,128)S(1)} %get-tuple-element.33), channel_id=1, source_target_pairs={{0,6},{1,7},{2,4},{3,5},{4,2},{5,3},{6,0},{7,1},{8,14},{9,15},{10,... | collective-permute-start | bytes 122888 | tf_op jit(solution)/shard_map/ppermute | solution.py:440
  12.9 0.0 collective-permute-start.2
  12.9 4.0 %collective-permute-start.4 = (f32[144,128]{1,0:T(8,128)S(1)}, f32[144,128]{1,0:T(8,128)S(1)}, u32[]{:S(2)}, u32[]{:S(2)}) collective-permute-start(f32[144,128]{1,0:T(8,128)S(1)} %get-tuple-element.34), channel_id=1, source_target_pairs={{0,1},{1,0},{2,3},{3,2},{4,5},{5,4},{6,7},{7,6},{8,9},{9,8},{10,11... | collective-permute-start | bytes 221192 | tf_op jit(solution)/shard_map/ppermute | solution.py:440
  16.8 1.3 %inner_update.2.refs_5_ = f32[4,288,128]{2,1,0:T(8,128)S(1)} custom-call(f32[4,288,128]{2,1,0:T(8,128)S(1)} %get-tuple-element.35.refs_0_, bf16[288,512]{1,0:T(8,128)(2,1)S(1)} %get-tuple-element.36.refs_1_, bf16[288,512]{1,0:T(8,128)(2,1)S(1)} %get-tuple-element.37.refs_2_, f32[288,128]{1,0:T(8,128)S(1)} %get-tuple-element.38.refs_3_, ...), custom_call_target="tpu_custom_call" | custom-call | flops 1811939328 | bytes 2359296 | tf_op jit(solution)/shard_map/inner_update/pallas_call | solution.py:485
  18.1 0.0 collective-permute-done.1.refs_1_
  18.1 0.0 collective-permute-done.refs_0_
  18.1 0.0 collective-permute-done.3.refs_3_
  18.1 0.0 collective-permute-done.2.refs_2_
  18.2 1.1 %collective-permute-done.4.refs_4_ = f32[144,128]{1,0:T(8,128)S(1)} collective-permute-done((f32[144,128]{1,0:T(8,128)S(1)}, f32[144,128]{1,0:T(8,128)S(1)}, u32[]{:S(2)}, u32[]{:S(2)}) %collective-permute-start.4) | collective-permute-done | bytes 73760 | tf_op jit(solution)/shard_map/ppermute | solution.py:440
  19.3 3.6 %outer_update_predictor.1 = (f32[4,288,128]{2,1,0:T(8,128)S(1)}, bf16[288,512]{1,0:T(8,128)(2,1)S(1)}, bf16[288,512]{1,0:T(8,128)(2,1)S(1)}, f32[288,128]{1,0:T(...) custom-call(f32[72,128]{1,0:T(8,128)S(1)} %collective-permute-done.r, ...), custom_call_target="tpu_custom_call" | custom-call | flops 7247757312 | bytes 2359296 | tf_op jit(solution)/shard_map/outer_update_predictor/pallas_call | solution.py:485
  22.8 0.1 collective-permute-start.6
  22.9 3.1 %collective-permute-start.5 = (f32[72,128]{1,0:T(8,128)S(1)}, f32[72,128]{1,0:T(8,128)S(1)}, u32[]{:S(2)}, u32[]{:S(2)}) collective-permute-start(f32[72,128]{1,0:T(8,128)S(1)} %get-tuple-element.44), channel_id=1, source_target_pairs={{0,8},{1,9},{2,10},{3,11},{4,12},{5,13},{6,14},{7,15},{8,0},{9,1},... | collective-permute-start | bytes 110600 | tf_op jit(solution)/shard_map/ppermute | solution.py:440
  26.0 0.6 %collective-permute-start.8 = (f32[80,128]{1,0:T(8,128)S(1)}, f32[80,128]{1,0:T(8,128)S(1)}, u32[]{:S(2)}, u32[]{:S(2)}) collective-permute-start(f32[80,128]{1,0:T(8,128)S(1)} %get-tuple-element.45), channel_id=1, source_target_pairs={{0,6},{1,7},{2,4},{3,5},{4,2},{5,3},{6,0},{7,1},{8,14},{9,15},{10,... | collective-permute-start | bytes 122888 | tf_op jit(solution)/shard_map/ppermute | solution.py:440
  26.6 0.2 collective-permute-start.7
  26.7 2.9 %collective-permute-start.9 = (f32[144,128]{1,0:T(8,128)S(1)}, f32[144,128]{1,0:T(8,128)S(1)}, u32[]{:S(2)}, u32[]{:S(2)}) collective-permute-start(f32[144,128]{1,0:T(8,128)S(1)} %get-tuple-element.46), channel_id=1, source_target_pairs={{0,1},{1,0},{2,3},{3,2},{4,5},{5,4},{6,7},{7,6},{8,9},{9,8},{10,11... | collective-permute-start | bytes 221192 | tf_op jit(solution)/shard_map/ppermute | solution.py:440
  29.6 1.2 %inner_update.3.refs_5_ = f32[4,288,128]{2,1,0:T(8,128)S(1)} custom-call(f32[4,288,128]{2,1,0:T(8,128)S(1)} %get-tuple-element.47.refs_0_, bf16[288,512]{1,0:T(8,128)(2,1)S(1)} %get-tuple-element.48.refs_1_, bf16[288,512]{1,0:T(8,128)(2,1)S(1)} %get-tuple-element.49.refs_2_, f32[288,128]{1,0:T(8,128)S(1)} %get-tuple-element.50.refs_3_, ...), custom_call_target="tpu_custom_call" | custom-call | flops 1811939328 | bytes 2359296 | tf_op jit(solution)/shard_map/inner_update/pallas_call | solution.py:485
  30.8 0.0 collective-permute-done.6.refs_1_
  30.9 0.0 collective-permute-done.5.refs_0_
  30.9 0.0 collective-permute-done.8.refs_3_
  30.9 0.0 collective-permute-done.7.refs_2_
  30.9 1.3 %collective-permute-done.9.refs_4_ = f32[144,128]{1,0:T(8,128)S(1)} collective-permute-done((f32[144,128]{1,0:T(8,128)S(1)}, f32[144,128]{1,0:T(8,128)S(1)}, u32[]{:S(2)}, u32[]{:S(2)}) %collective-permute-start.9) | collective-permute-done | bytes 73760 | tf_op jit(solution)/shard_map/ppermute | solution.py:440
  32.2 1.9 %outer_update.1 = f32[288,512]{1,0:T(8,128)} custom-call(f32[72,128]{1,0:T(8,128)S(1)} %collective-permute-done.5.refs_0_, f32[72,128]{1,0:T(8,128)S(1)} %collective-permute-done.6.refs_1_, f32[80,128]{1,0:T(8,128)S(1)} %collective-permute-done.7.refs_2_, f32[80,128]{1,0:T(8,128)S(1)} %collective-permute-done.8.refs_3_, ...), custom_call_target="tpu_custom_call" | custom-call | flops 1811939328 | bytes 2359296 | tf_op jit(solution)/shard_map/outer_update/pallas_call | solution.py:485
Async XLA Ops:
  0.0 2.1 %copy-start.6 = (s32[1,1,1,32]{3,2,1,0:T(1,128)S(1)}, s32[1,1,1,32]{3,2,1,0:T(1,128)}, u32[]{:S(2)}) copy-start(s32[1,1,1,32]{3,2,1,0:T(1,128)} %param.14) | copy-start | bytes 388
  0.0 2.1 %copy-start.1 = (s32[1,1,1,6,32]{4,2,3,1,0:T(1,128)S(1)}, s32[1,1,1,6,32]{4,2,3,1,0:T(1,128)}, u32[]{:S(2)}) copy-start(s32[1,1,1,6,32]{4,2,3,1,0:T(1,128)} %param.15) | copy-start | bytes 2308
  0.0 2.1 %copy-start.5 = (s32[1,1,1,32]{3,2,1,0:T(1,128)S(1)}, s32[1,1,1,32]{3,2,1,0:T(1,128)}, u32[]{:S(2)}) copy-start(s32[1,1,1,32]{3,2,1,0:T(1,128)} %param.13) | copy-start | bytes 388
  0.0 2.1 %copy-start.4 = (f32[1,1,1,32]{3,2,1,0:T(1,128)S(1)}, f32[1,1,1,32]{3,2,1,0:T(1,128)}, u32[]{:S(2)}) copy-start(f32[1,1,1,32]{3,2,1,0:T(1,128)} %param.12) | copy-start | bytes 388
  0.0 2.1 %copy-start.3 = (f32[1,1,1,32]{3,2,1,0:T(1,128)S(1)}, f32[1,1,1,32]{3,2,1,0:T(1,128)}, u32[]{:S(2)}) copy-start(f32[1,1,1,32]{3,2,1,0:T(1,128)} %param.11) | copy-start | bytes 388
  0.0 2.1 %copy-start.2 = (f32[1,1,1,32]{3,2,1,0:T(1,128)S(1)}, f32[1,1,1,32]{3,2,1,0:T(1,128)}, u32[]{:S(2)}) copy-start(f32[1,1,1,32]{3,2,1,0:T(1,128)} %param.10) | copy-start | bytes 388
  0.0 2.1 %copy-start = (f32[1,1,1,32,9,512]{5,3,4,2,1,0:T(8,128)S(1)}, f32[1,1,1,32,9,512]{5,3,4,2,1,0:T(8,128)}, u32[]{:S(2)}) copy-start(f32[1,1,1,32,9,512]{5,3,4,2,1,0:T(8,128)} %param.8) | copy-start | bytes 1769476
  6.1 12.1 %collective-permute-start.1 = (f32[72,128]{1,0:T(8,128)S(1)}, f32[72,128]{1,0:T(8,128)S(1)}, u32[]{:S(2)}, u32[]{:S(2)}) collective-permute-start(f32[72,128]{1,0:T(8,128)S(1)} %get-tuple-element.32), channel_id=1, source_target_pairs={{0,2},{1,3},{2,0},{3,1},{4,6},{5,7},{6,4},{7,5},{8,16},{9,17},{10,... | collective-permute-start | bytes 110600 | tf_op jit(solution)/shard_map/ppermute | solution.py:440
  6.6 11.6 %collective-permute-start = (f32[72,128]{1,0:T(8,128)S(1)}, f32[72,128]{1,0:T(8,128)S(1)}, u32[]{:S(2)}, u32[]{:S(2)}) collective-permute-start(f32[72,128]{1,0:T(8,128)S(1)} %get-tuple-element.32), channel_id=1, source_target_pairs={{0,8},{1,9},{2,10},{3,11},{4,12},{5,13},{6,14},{7,15},{8,0},{9,1},... | collective-permute-start | bytes 110600 | tf_op jit(solution)/shard_map/ppermute | solution.py:440
  12.2 5.9 %collective-permute-start.3 = (f32[80,128]{1,0:T(8,128)S(1)}, f32[80,128]{1,0:T(8,128)S(1)}, u32[]{:S(2)}, u32[]{:S(2)}) collective-permute-start(f32[80,128]{1,0:T(8,128)S(1)} %get-tuple-element.33), channel_id=1, source_target_pairs={{0,6},{1,7},{2,4},{3,5},{4,2},{5,3},{6,0},{7,1},{8,14},{9,15},{10,... | collective-permute-start | bytes 122888 | tf_op jit(solution)/shard_map/ppermute | solution.py:440
  12.9 5.3 %collective-permute-start.2 = (f32[80,128]{1,0:T(8,128)S(1)}, f32[80,128]{1,0:T(8,128)S(1)}, u32[]{:S(2)}, u32[]{:S(2)}) collective-permute-start(f32[80,128]{1,0:T(8,128)S(1)} %get-tuple-element.33), channel_id=1, source_target_pairs={{0,2},{1,3},{2,0},{3,1},{4,6},{5,7},{6,4},{7,5},{8,10},{9,11},{10,... | collective-permute-start | bytes 122888 | tf_op jit(solution)/shard_map/ppermute | solution.py:440
  12.9 6.4 %collective-permute-start.4 = (f32[144,128]{1,0:T(8,128)S(1)}, f32[144,128]{1,0:T(8,128)S(1)}, u32[]{:S(2)}, u32[]{:S(2)}) collective-permute-start(f32[144,128]{1,0:T(8,128)S(1)} %get-tuple-element.34), channel_id=1, source_target_pairs={{0,1},{1,0},{2,3},{3,2},{4,5},{5,4},{6,7},{7,6},{8,9},{9,8},{10,11... | collective-permute-start | bytes 221192 | tf_op jit(solution)/shard_map/ppermute | solution.py:440
  22.8 8.0 %collective-permute-start.6 = (f32[72,128]{1,0:T(8,128)S(1)}, f32[72,128]{1,0:T(8,128)S(1)}, u32[]{:S(2)}, u32[]{:S(2)}) collective-permute-start(f32[72,128]{1,0:T(8,128)S(1)} %get-tuple-element.44), channel_id=1, source_target_pairs={{0,2},{1,3},{2,0},{3,1},{4,6},{5,7},{6,4},{7,5},{8,16},{9,17},{10,... | collective-permute-start | bytes 110600 | tf_op jit(solution)/shard_map/ppermute | solution.py:440
  22.9 7.9 %collective-permute-start.5 = (f32[72,128]{1,0:T(8,128)S(1)}, f32[72,128]{1,0:T(8,128)S(1)}, u32[]{:S(2)}, u32[]{:S(2)}) collective-permute-start(f32[72,128]{1,0:T(8,128)S(1)} %get-tuple-element.44), channel_id=1, source_target_pairs={{0,8},{1,9},{2,10},{3,11},{4,12},{5,13},{6,14},{7,15},{8,0},{9,1},... | collective-permute-start | bytes 110600 | tf_op jit(solution)/shard_map/ppermute | solution.py:440
  26.0 4.9 %collective-permute-start.8 = (f32[80,128]{1,0:T(8,128)S(1)}, f32[80,128]{1,0:T(8,128)S(1)}, u32[]{:S(2)}, u32[]{:S(2)}) collective-permute-start(f32[80,128]{1,0:T(8,128)S(1)} %get-tuple-element.45), channel_id=1, source_target_pairs={{0,6},{1,7},{2,4},{3,5},{4,2},{5,3},{6,0},{7,1},{8,14},{9,15},{10,... | collective-permute-start | bytes 122888 | tf_op jit(solution)/shard_map/ppermute | solution.py:440
  26.6 4.3 %collective-permute-start.7 = (f32[80,128]{1,0:T(8,128)S(1)}, f32[80,128]{1,0:T(8,128)S(1)}, u32[]{:S(2)}, u32[]{:S(2)}) collective-permute-start(f32[80,128]{1,0:T(8,128)S(1)} %get-tuple-element.45), channel_id=1, source_target_pairs={{0,2},{1,3},{2,0},{3,1},{4,6},{5,7},{6,4},{7,5},{8,10},{9,11},{10,... | collective-permute-start | bytes 122888 | tf_op jit(solution)/shard_map/ppermute | solution.py:440
  26.7 5.5 %collective-permute-start.9 = (f32[144,128]{1,0:T(8,128)S(1)}, f32[144,128]{1,0:T(8,128)S(1)}, u32[]{:S(2)}, u32[]{:S(2)}) collective-permute-start(f32[144,128]{1,0:T(8,128)S(1)} %get-tuple-element.46), channel_id=1, source_target_pairs={{0,1},{1,0},{2,3},{3,2},{4,5},{5,4},{6,7},{7,6},{8,9},{9,8},{10,11... | collective-permute-start | bytes 221192 | tf_op jit(solution)/shard_map/ppermute | solution.py:440

commit v3 on v2

--- a/solution.py
+++ b/solution.py
@@ -12,6 +12,7 @@
 STEPS = 2
 DT = 0.8
 LIFT = 2.0
+EXCHANGED = (2, 0, 1)
 PICKED = ((0, 1, 2, 3, 6, 8), (0, 1, 2, 6, 4, 7), (0, 1, 2, 8, 7, 5))
 F32 = jnp.float32
 BF16 = jnp.bfloat16
@@ -43,6 +44,13 @@
 
 def dot(left, right):
     return jnp.dot(left, right, preferred_element_type=F32)
+
+
+def moved(table, source, cols, rows_in, rows_out):
+    body, whole = table.shape[1], source.shape[0]
+    first = dot(table[...], source[0:body, cols])
+    rest = dot(table[0:rows_out, 0:rows_in], source[body:whole, cols])
+    return jnp.concatenate([first, rest], axis=0)
 
 
 def lanes_of(rows):
@@ -130,15 +138,38 @@
     return started
 
 
-def predict(count, fields, q, par, w_high, w_low, face_table, cell_sm, flag_sm, outs, scratch):
-    int_high, int_low, trace_x, trace_y, trace_z, edge_x, edge_y, edge_z = outs
-    h0, l0, h1, l1, total, second, packed, packed_par, series, hot_rows = scratch
+def send(low, high, up, targets):
+    minus = lanes_of(low.shape[0]) < 64
+    plus_face = jnp.where(minus, pltpu.roll(low, 64, 1), high)
+    minus_face = jnp.where(minus, low, pltpu.roll(high, 64, 1))
+    targets[0][...] = jnp.where(up, plus_face, minus_face)
+    if len(targets) > 1:
+        targets[1][...] = jnp.where(up, minus_face, plus_face)
+
+
+def received(pair, axis, size):
+    here = lax.axis_index(axis)
+    odd = here % 2 == 1
+    first = pair[0][...]
+    second = first if pair[1] is None else pair[1][...]
+    minus = lanes_of(first.shape[0]) < 64
+    lower = jnp.where(odd, first, second)
+    upper = jnp.where(odd, second, first)
+    plus_lane = jnp.logical_and(here > 0, jnp.logical_not(minus))
+    minus_lane = jnp.logical_and(here < size - 1, minus)
+    return (
+        (jnp.where(plus_lane, pltpu.roll(lower, 64, 1), 0.0), jnp.where(plus_lane, lower, 0.0)),
+        (jnp.where(minus_lane, upper, 0.0), jnp.where(minus_lane, pltpu.roll(upper, 64, 1), 0.0)),
+    )
+
+
+def predict(count, fields, sizes, q, par, hot_par, pack, unpack, w_high, w_low, face_table, outs, scratch):
+    int_high, int_low, trace_x, trace_y, trace_z, *edges = outs
+    h0, l0, h1, l1, total, p0, p1, p2, p3, series = scratch
     nodes = h0.shape[1]
     tiles_of_node = nodes // 128
     every = slice(0, nodes)
-    for f in range(fields):
-        rows = slice(f * count, (f + 1) * count)
-        h0[rows], l0[rows] = split(get(q, rows, every))
+    half = count // 2
 
     def first(f, cols, value):
         rows = slice(f * count, (f + 1) * count)
@@ -150,43 +181,36 @@
     def then(f, cols, value):
         rows = slice(f * count, (f + 1) * count)
         add(total, rows, cols, DT**2 / 6.0 * value)
-        put(second, rows, cols, value)
+        h0[rows, cols], l0[rows, cols] = split(value)
 
     rate(h1, l1, w_high, w_low, par, count, count, then)
 
-    slot = jnp.int32(0)
-    for e in range(count):
-        hot_rows[slot] = cell_sm[e]
-        slot = slot + flag_sm[e]
-    half = count // 2
-
-    @pl.when(slot > 0)
+    @pl.when(jnp.max(hot_par[3 * half : 3 * half + 8]) > 0.0)
     def _():
-        for k in range(half):
-            row = hot_rows[k]
-            for t in range(tiles_of_node):
-                packed[t, pl.ds(k, fields, stride=count), :] = second[t, pl.ds(row, fields, stride=count), :]
-            packed_par[pl.ds(k, 3, stride=count), :] = par[pl.ds(row, 3, stride=count), :]
-        for f in range(fields):
-            rows = slice(f * count, f * count + half)
-            h0[rows], l0[rows] = split(get(packed, rows, every))
-        buffers = [(h0, l0), (h1, l1)]
+        for start in range(0, nodes, 256):
+            cols = slice(start, start + 256)
+            p0[:, cols] = moved(pack, h0, cols, count, half).astype(BF16)
+            p1[:, cols] = moved(pack, l0, cols, count, half).astype(BF16)
+        buffers = [(p0, p1), (p2, p3)]
         for order in (3, 4, 5):
             weight = DT**order / math.factorial(order + 1)
             source, target = buffers[(order - 3) % 2], buffers[(order - 2) % 2]
 
             def more(f, cols, value, order=order, weight=weight, target=target):
-                rows = slice(f * count, f * count + half)
-                (put if order == 3 else add)(series, rows, cols, weight * value)
+                rows = slice(f * half, (f + 1) * half)
+                part = weight * value
+                if order > 3:
+                    part = part + series[rows, cols]
                 if order < 5:
-                    target[0][rows, cols], target[1][rows, cols] = split(value)
-
-            rate(source[0], source[1], w_high, w_low, packed_par, count, half, more)
-        for k in range(half):
-            row = hot_rows[k]
-            spot = pl.ds(row, fields, stride=count)
-            for t in range(tiles_of_node):
-                total[t, spot, :] = total[t, spot, :] + series[t, pl.ds(k, fields, stride=count), :]
+                    series[rows, cols] = part
+                    part = value
+                target[0][rows, cols], target[1][rows, cols] = split(part)
+
+            rate(source[0], source[1], w_high, w_low, hot_par, half, half, more)
+        for start in range(0, nodes, 256):
+            cols = slice(start, start + 256)
+            extra = moved(unpack, p2, cols, half, count) + moved(unpack, p3, cols, half, count)
+            add(total, slice(0, fields * count), cols, extra)
 
     for f in range(fields):
         rows = slice(f * count, (f + 1) * count)
@@ -195,23 +219,36 @@
     faces = dot(int_high[...], face_table[...]) + dot(int_low[...], face_table[...])
     trace_y[...] = faces[:, 0:128]
     trace_z[...] = faces[:, 128:256]
+    targets, at = {}, 0
+    for dim in EXCHANGED:
+        number = 1 if sizes[dim][1] == 2 else 2
+        targets[dim] = edges[at : at + number]
+        at += number
+    ups = [lax.axis_index(axis) % 2 == 0 for axis, _ in sizes]
+    ends = []
     for f in range(fields):
-        edge_x[f * 8 : f * 8 + 8] = jnp.where(
-            lanes_of(8) < 64, trace_x[f * count : f * count + 8], trace_x[(f + 1) * count - 8 : (f + 1) * count]
+        low, high = trace_x[f * count : f * count + 8], trace_x[(f + 1) * count - 8 : (f + 1) * count]
+        ends.append(jnp.where(lanes_of(8) < 64, low, high))
+    middle = (fields + 1) // 2
+    ends.append(ends[-1])
+    send(jnp.concatenate(ends[:middle]), jnp.concatenate(ends[middle : 2 * middle]), ups[0], targets[0])
+    tiles = fields * count // 8
+    pad = targets[1][0].shape[0] - tiles
+    minus = lanes_of(tiles) < 64
+    ends = []
+    for m in range(2):
+        value = jnp.where(minus, trace_y[pl.ds(m, tiles, stride=8), :], trace_y[pl.ds(6 + m, tiles, stride=8), :])
+        ends.append(jnp.concatenate([value, jnp.zeros((pad, 128), F32)]) if pad else value)
+    send(ends[0], ends[1], ups[1], targets[1])
+    pairs = fields * count // 4
+    minus = lanes_of(pairs) < 64
+    ends = []
+    for start in (0, 2 * pairs):
+        value = jnp.where(
+            minus, trace_z[pl.ds(start, pairs, stride=2), :], trace_z[pl.ds(start + 1, pairs, stride=2), :]
         )
-    tiles = fields * count // 8
-    minus = lanes_of(tiles) < 64
-    pad = edge_y.shape[0] // 2
-    for m in range(2):
-        edge_y[m * pad : m * pad + tiles] = jnp.where(
-            minus, trace_y[pl.ds(m, tiles, stride=8), :], trace_y[pl.ds(6 + m, tiles, stride=8), :]
-        )
-        if pad > tiles:
-            edge_y[m * pad + tiles : (m + 1) * pad] = jnp.zeros((pad - tiles, 128), F32)
-    pairs = fields * count // 2
-    edge_z[...] = jnp.where(
-        lanes_of(pairs) < 64, trace_z[pl.ds(0, pairs, stride=2), :], trace_z[pl.ds(1, pairs, stride=2), :]
-    )
+        ends.append(value)
+    send(ends[0], ends[1], ups[2], targets[2])
 
 
 def inner(count, fields, q, int_high, int_low, trace_x, trace_y, trace_z, par, index, w_high, w_low, lift_table,
@@ -252,52 +289,31 @@
 
 
 def outer(count, fields, sizes, got, base, par, index, lift_table, out, halo, face_high, face_low):
-    lower, upper = [], []
-    for dim, (axis, size) in enumerate(sizes):
-        here = lax.axis_index(axis)
-        odd = here % 2 == 1
-        first, second = got[dim]
-        second = first if second is None else second
-        lower.append((jnp.logical_and(odd, here > 0) if size == 2 else None, odd, here > 0, first, second))
-        upper.append((None, odd, here < size - 1, first, second))
-
-    def from_lower(dim, rows, minus):
-        _, odd, there, first, second = lower[dim]
-        value = jnp.where(odd, first[rows], second[rows])
-        return jnp.where(jnp.logical_and(there, jnp.logical_not(minus)), value, 0.0)
-
-    def from_upper(dim, rows, minus):
-        _, odd, there, first, second = upper[dim]
-        value = jnp.where(odd, second[rows], first[rows])
-        return jnp.where(jnp.logical_and(there, minus), value, 0.0)
-
+    middle = (fields + 1) // 2
+    lower, upper = received(got[0], *sizes[0])
     out[...] = base[...]
-    minus8 = lanes_of(8) < 64
-    for end in range(2):
+    for end, (low, high) in enumerate((lower, upper)):
         rows = slice(0, 8) if end == 0 else slice(count - 8, count)
         jump = []
         for f in range(fields):
-            here = slice(f * 8, f * 8 + 8)
-            value = from_lower(0, here, minus8) if end == 0 else from_upper(0, here, minus8)
-            jump.append(orient(value, index[rows]))
+            part, at = (low, f) if f < middle else (high, f - middle)
+            jump.append(orient(part[at * 8 : at * 8 + 8], index[rows]))
         fixed = correction(jump, par, count, 0, rows)
         for f in range(fields):
             lift_edges(out, fixed[f], f, rows, count)
     tiles = fields * count // 8
-    pad = got[1][0].shape[0] // 2
-    pairs = fields * count // 2
+    pairs = fields * count // 4
     for dim in (1, 2):
+        lower, upper = received(got[dim], *sizes[dim])
         if dim == 1:
             halo[...] = jnp.zeros_like(halo)
-            minus = lanes_of(tiles) < 64
             for m in range(2):
-                here = slice(m * pad, m * pad + tiles)
-                halo[pl.ds(m, tiles, stride=8), :] = from_lower(1, here, minus)
-                halo[pl.ds(6 + m, tiles, stride=8), :] = from_upper(1, here, minus)
+                halo[pl.ds(m, tiles, stride=8), :] = lower[m][0:tiles]
+                halo[pl.ds(6 + m, tiles, stride=8), :] = upper[m][0:tiles]
         else:
-            minus = lanes_of(pairs) < 64
-            halo[pl.ds(0, pairs, stride=2), :] = from_lower(2, slice(0, pairs), minus)
-            halo[pl.ds(1, pairs, stride=2), :] = from_upper(2, slice(0, pairs), minus)
+            for part in range(2):
+                halo[pl.ds(2 * part * pairs, pairs, stride=2), :] = lower[part]
+                halo[pl.ds(2 * part * pairs + 1, pairs, stride=2), :] = upper[part]
         jump = [
             orient(halo[f * count : (f + 1) * count], index[dim * count : (dim + 1) * count]) for f in range(fields)
         ]
@@ -332,24 +348,68 @@
         w_high[dim, rows, :], w_low[dim, rows, :] = split(ops[dim, rows, :])
 
 
-def first_kernel(count, fields, wave, density, lame, shear, cell, orient_code, cells_any, flags_any,
-                 w_high, w_low, face_table, q, par, index, *rest):
-    outs, scratch = rest[:8], rest[8:18]
-    cell_sm, flag_sm, sems = rest[18:]
-    waits = fetch([(cells_any, cell_sm, sems.at[0]), (flags_any, flag_sm, sems.at[1])])
-    staged = scratch[4]
-    put(staged, slice(0, fields * count), slice(0, wave.shape[1]), wave[...])
-    fills = cell[...] == lax.broadcasted_iota(jnp.int32, (count, count), 0)
-    in_cell = lambda row: jnp.broadcast_to(
-        jnp.sum(jnp.where(fills, row, 0.0), axis=1, keepdims=True), (count, 128)
-    )
-    inv_rho = in_cell(1.0 / density[...])
+def first_kernel(count, fields, sizes, wave, density, lame, shear, cell, flag, orient_code, w_high, w_low, face_table,
+                 q, par, index, hot_par, place, place_back, pack, unpack, *rest):
+    outs, scratch = rest[:-10], rest[-10:]
+    h0, l0, h1, l1 = scratch[:4]
+    half, blocks = count // 2, fields - 1
+    iota = lambda shape, axis: lax.broadcasted_iota(jnp.int32, shape, axis)
+    ones = lambda mask: jnp.where(mask, 1.0, 0.0).astype(BF16)
+    cells = cell[...]
+    square = (count, count)
+    tiled = dot(
+        jnp.broadcast_to(cells.astype(F32).astype(BF16), (8, count)),
+        ones(iota((count, blocks * count), 1) % count == iota((count, blocks * count), 0)),
+    )[0:1].astype(jnp.int32)
+    shape = place.shape
+    target = tiled + iota((1, shape[1]), 1) // count * count
+    place[...] = ones(iota(shape, 0) == target)
+    for f in range(fields):
+        rows = slice(f * count, (f + 1) * count)
+        h1[rows], l1[rows] = split(wave[rows])
+    for start in range(0, h0.shape[1], 256):
+        cols = slice(start, start + 256)
+        high = moved(place, h1, cols, count, count)
+        low = moved(place, l1, cols, count, count)
+        h0[:, cols], l0[:, cols] = high.astype(BF16), low.astype(BF16)
+        put(q, slice(0, fields * count), cols, high + low)
+
+    fills = cells == iota(square, 0)
+    gather = lambda mask, row: jnp.sum(jnp.where(mask, row, 0.0), axis=1, keepdims=True)
+    in_cell = lambda row: jnp.broadcast_to(gather(fills, row), (count, 128))
+    inv_row = 1.0 / density[...]
+    inv_rho = in_cell(inv_row)
     lame_col = in_cell(lame[...])
     shear_col = in_cell(shear[...])
     par[0:count] = inv_rho
     par[count : 2 * count] = lame_col
     par[2 * count : 3 * count] = shear_col
     par[3 * count : 4 * count] = 0.5 * jnp.sqrt((lame_col + 2.0 * shear_col) * inv_rho)
+
+    flags = flag[...].astype(F32)
+    before = ones(iota(square, 0) < iota(square, 1))
+    rank = dot(jnp.broadcast_to(flags.astype(BF16), (8, count)), before)[0:1]
+    slots = (rank.astype(jnp.int32) == iota((half, count), 0)) & (flags > 0.0)
+    in_slot = lambda row: jnp.broadcast_to(gather(slots, row), (half, 128))
+    hot_par[0:half] = in_slot(inv_row)
+    hot_par[half : 2 * half] = in_slot(lame[...])
+    hot_par[2 * half : 3 * half] = in_slot(shear[...])
+    hot_par[3 * half : 4 * half] = in_slot(flags)
+    twice = lambda column, times: jnp.concatenate([column] * times, axis=0).astype(jnp.int32)
+    shape = pack.shape
+    target = twice(in_slot(cells.astype(F32)), blocks) + iota((shape[0], 128), 0) // half * count
+    used = twice(in_slot(flags), blocks) > 0
+    target = jnp.where(used, target, -1)
+    pack[...] = ones(iota(shape, 1) == wide(target, shape[1] // 128))
+    shape = unpack.shape
+    target = twice(in_cell(rank), blocks) + iota((shape[0], 128), 0) // count * half
+    target = jnp.where(twice(in_cell(flags), blocks) > 0, target, -1)
+    unpack[...] = ones(iota(shape, 1) == wide(target, shape[1] // 128))
+    own = gather(iota(square, 0) == iota(square, 1), cells.astype(F32))
+    shape = place_back.shape
+    target = twice(jnp.broadcast_to(own, (count, 128)), blocks) + iota((shape[0], 128), 0) // count * count
+    place_back[...] = ones(iota(shape, 1) == wide(target, shape[1] // 128))
+
     lanes = lanes_of(count)
     p_lane, r_lane = lanes % 64 // 8, lanes % 8
     for dim in range(3):
@@ -362,12 +422,7 @@
         r_from = jnp.where(code // 2 % 2 == 1, 7 - r_lane, r_lane)
         source = jnp.where(code >= 4, r_from * 8 + p_from, p_from * 8 + r_from)
         index[dim * count : (dim + 1) * count] = source + jnp.where(lanes < 64, 64, 0)
-    for wait in waits:
-        wait.wait()
-    for e in range(count):
-        for t in range(q.shape[0]):
-            q[t, pl.ds(cell_sm[e], fields, stride=count), :] = staged[t, pl.ds(e, fields, stride=count), :]
-    predict(count, fields, q, par, w_high, w_low, face_table, cell_sm, flag_sm, outs, scratch)
+    predict(count, fields, sizes, q, par, hot_par, pack, unpack, w_high, w_low, face_table, outs, scratch)
 
 
 def inner_kernel(count, fields, *refs):
@@ -375,41 +430,38 @@
 
 
 def unpack_got(sizes, refs):
-    got, at = [], 0
-    for _, size in sizes:
-        pair = [None, None]
-        for k in range(1 if size == 2 else 2):
-            pair[k] = refs[at]
+    got, at = [[None, None] for _ in sizes], 0
+    for dim in EXCHANGED:
+        for k in range(1 if sizes[dim][1] == 2 else 2):
+            got[dim][k] = refs[at]
             at += 1
-        got.append(pair)
     return got, refs[at:]
 
 
 def middle_kernel(count, fields, sizes, *refs):
     got, refs = unpack_got(sizes, refs)
-    base, par, index, w_high, w_low, face_table, lift_table, cells_any, flags_any = refs[:9]
-    q, outs = refs[9], refs[10:18]
-    halo, face_high, face_low = refs[18:21]
-    scratch, (cell_sm, flag_sm, sems) = refs[21:31], refs[31:]
-    waits = fetch([(cells_any, cell_sm, sems.at[0]), (flags_any, flag_sm, sems.at[1])])
+    base, par, index, hot_par, pack, unpack, w_high, w_low, face_table, lift_table, q = refs[:11]
+    outs, (halo, face_high, face_low), scratch = refs[11:-13], refs[-13:-10], refs[-10:]
     outer(count, fields, sizes, got, base, par, index, lift_table, q, halo, face_high, face_low)
-    for wait in waits:
-        wait.wait()
-    predict(count, fields, q, par, w_high, w_low, face_table, cell_sm, flag_sm, outs, scratch)
+    h0, l0 = scratch[:2]
+    for f in range(fields):
+        rows = slice(f * count, (f + 1) * count)
+        h0[rows], l0[rows] = split(get(q, rows, slice(0, h0.shape[1])))
+    predict(count, fields, sizes, q, par, hot_par, pack, unpack, w_high, w_low, face_table, outs, scratch)
 
 
 def last_kernel(count, fields, sizes, *refs):
     got, refs = unpack_got(sizes, refs)
-    base, par, index, lift_table, cells_any, out, q, staged, halo, face_high, face_low, cell_sm, sems = refs
-    tiles_of_node = q.shape[0]
-    waits = fetch([(cells_any, cell_sm, sems.at[tiles_of_node])])
+    base, par, index, place_back, lift_table, out, q, high, low, staged, halo, face_high, face_low, sems = refs
     outer(count, fields, sizes, got, base, par, index, lift_table, q, halo, face_high, face_low)
-    waits[0].wait()
     done = []
-    for t in range(tiles_of_node):
-        for e in range(count):
-            staged[t, pl.ds(e, fields, stride=count), :] = q[t, pl.ds(cell_sm[e], fields, stride=count), :]
-        done += fetch([(staged.at[t], out.at[:, t * 128 : (t + 1) * 128], sems.at[t])])
+    for k, start in enumerate(range(0, staged.shape[1], 256)):
+        cols = slice(start, start + 256)
+        for f in range(fields):
+            rows = slice(f * count, (f + 1) * count)
+            high[rows, cols], low[rows, cols] = split(get(q, rows, cols))
+        staged[:, cols] = moved(place_back, high, cols, count, count) + moved(place_back, low, cols, count, count)
+        done += fetch([(staged.at[:, cols], out.at[:, cols], sems.at[k])])
     for wait in done:
         wait.wait()
 
@@ -435,9 +487,9 @@
 def exchange(edges, sizes):
     axes = tuple(axis for axis, _ in sizes)
     got = []
-    for dim, edge in enumerate(edges):
+    for dim in EXCHANGED:
         for parity in range(1 if sizes[dim][1] == 2 else 2):
-            got.append(lax.ppermute(edge, axes, swaps(sizes, dim, parity)))
+            got.append(lax.ppermute(edges[len(got)], axes, swaps(sizes, dim, parity)))
     return got
 
 
@@ -445,38 +497,26 @@
     count, fields, nodes = wavefield.shape[-3:]
     rows = fields * count
     wave = wavefield[0, 0, 0].swapaxes(0, 1).reshape(rows, nodes)
+    half, blocks = count // 2, fields - 1
     row = lambda value: value.reshape(1, count)
-    cell_sm = element_cell.reshape(count)
-    flag_sm = high_order.reshape(count)
     codes = face_orient.reshape(6, 1, count)
     vmem = pl.BlockSpec(memory_space=pltpu.VMEM)
     hbm = pl.BlockSpec(memory_space=pltpu.HBM)
-    index_scratch = pltpu.SMEM((count,), jnp.int32)
     shape = jax.ShapeDtypeStruct
     field_shape = shape((nodes // 128, rows, 128), F32)
-    pad = -(-(rows // 8) // 8) * 8
+    edge_rows = {0: (fields + 1) // 2 * 8, 1: -(-(rows // 8) // 8) * 8, 2: rows // 4}
     predicted = [
         shape((rows, nodes), BF16),
         shape((rows, nodes), BF16),
         shape((rows, 128), F32),
         shape((rows, 128), F32),
         shape((rows, 128), F32),
-        shape((fields * 8, 128), F32),
-        shape((2 * pad, 128), F32),
-        shape((rows // 2, 128), F32),
     ]
-    predict_scratch = [
-        pltpu.VMEM((rows, nodes), BF16),
-        pltpu.VMEM((rows, nodes), BF16),
-        pltpu.VMEM((rows, nodes), BF16),
-        pltpu.VMEM((rows, nodes), BF16),
-        pltpu.VMEM(field_shape.shape, F32),
-        pltpu.VMEM(field_shape.shape, F32),
-        pltpu.VMEM(field_shape.shape, F32),
-        pltpu.VMEM((3 * count, 128), F32),
-        pltpu.VMEM(field_shape.shape, F32),
-        pltpu.SMEM((count + 1,), jnp.int32),
-    ]
+    for dim in EXCHANGED:
+        predicted += [shape((edge_rows[dim], 128), F32)] * (1 if sizes[dim][1] == 2 else 2)
+    hot_rows = half * fields
+    predict_scratch = [pltpu.VMEM((rows, nodes), BF16)] * 4 + [pltpu.VMEM(field_shape.shape, F32)]
+    predict_scratch += [pltpu.VMEM((hot_rows, nodes), BF16)] * 4 + [pltpu.VMEM((hot_rows, nodes), F32)]
     face_scratch = [pltpu.VMEM((rows, 256), BF16), pltpu.VMEM((rows, 256), BF16)]
     halo_scratch = [pltpu.VMEM((rows, 128), F32)] + face_scratch
 
@@ -510,13 +550,23 @@
         "split_operators",
         limit=TABLE_LIMIT,
     )
-    q, par, index, *ahead = call(
-        functools.partial(first_kernel, count, fields),
-        [wave, row(density), row(lame_first), row(shear_modulus), row(element_cell), codes, cell_sm, flag_sm]
+    q, par, index, hot_par, place, place_back, pack, unpack, *ahead = call(
+        functools.partial(first_kernel, count, fields, sizes),
+        [wave, row(density), row(lame_first), row(shear_modulus), row(element_cell), row(high_order), codes]
         + [w_high, w_low, face_table],
-        [vmem] * 6 + [hbm] * 2 + [vmem] * 3,
-        [field_shape, shape((4 * count, 128), F32), shape((3 * count, 128), jnp.int32)] + predicted,
-        predict_scratch + [index_scratch, index_scratch, pltpu.SemaphoreType.DMA((2,))],
+        [vmem] * 10,
+        [
+            field_shape,
+            shape((4 * count, 128), F32),
+            shape((3 * count, 128), jnp.int32),
+            shape((4 * half, 128), F32),
+            shape((blocks * count, blocks * count), BF16),
+            shape((blocks * count, blocks * count), BF16),
+            shape((blocks * half, blocks * count), BF16),
+            shape((blocks * count, blocks * half), BF16),
+        ]
+        + predicted,
+        predict_scratch,
         4,
         "first_predictor",
     )
@@ -535,22 +585,24 @@
         if step < STEPS - 1:
             q, *ahead = call(
                 functools.partial(middle_kernel, count, fields, sizes),
-                [*got, base, par, index, w_high, w_low, face_table, lift_table, cell_sm, flag_sm],
-                [vmem] * (len(got) + 7) + [hbm] * 2,
+                [*got, base, par, index, hot_par, pack, unpack, w_high, w_low, face_table, lift_table],
+                [vmem] * (len(got) + 10),
                 [field_shape] + predicted,
-                halo_scratch + predict_scratch + [index_scratch, index_scratch, pltpu.SemaphoreType.DMA((2,))],
+                halo_scratch + predict_scratch,
                 4,
                 "outer_update_predictor",
             )
         else:
             out = call(
                 functools.partial(last_kernel, count, fields, sizes),
-                [*got, base, par, index, lift_table, cell_sm],
-                [vmem] * (len(got) + 4) + [hbm],
+                [*got, base, par, index, place_back, lift_table],
+                [vmem] * (len(got) + 5),
                 shape((rows, nodes), F32),
-                [pltpu.VMEM(field_shape.shape, F32)] * 2
+                [pltpu.VMEM(field_shape.shape, F32)]
+                + [pltpu.VMEM((rows, nodes), BF16)] * 2
+                + [pltpu.VMEM((rows, nodes), F32)]
                 + halo_scratch
-                + [index_scratch, pltpu.SemaphoreType.DMA((nodes // 128 + 1,))],
+                + [pltpu.SemaphoreType.DMA((nodes // 256,))],
                 1,
                 "outer_update",
                 hbm,

time: 34.6 us -> 31.7 us (0.916)
  starting transfers between devices: 17.5 us -> 8 us
  Pallas kernels: 13.9 us -> 18.1 us
  waiting for transfers between devices: 2.45 us -> 5.34 us
    ppermute x10, starting transfers between devices: 17.5 us -> 8 us  [exchange(): got.append(lax.ppermute(edges[len(got)], axes, swaps(sizes, dim, parity)))]
    pallas_call x6, Pallas kernels: 13.9 us -> 18.1 us  [call(): pl.pallas_call(kernel, out_shape=out_shape, in_specs=in_specs, out_specs=...]
    ppermute x10, waiting for transfers between devices: 2.45 us -> 5.34 us  [exchange(): got.append(lax.ppermute(edges[len(got)], axes, swaps(sizes, dim, parity)))]
  transfers between devices with their start and end apart: 10 -> 10, of which waited for: 2 -> 4; matrix products, arithmetic and copies ran while one was open for 0% -> 0% of each run, Pallas kernels for 7% -> 8%
where the time goes in v3:
time: 31.7 us; the launch traced here: 31.6 us
  Pallas kernels  18.1 us (57%)
  starting transfers between devices  8 us (25%)
  waiting for transfers between devices  5.34 us (17%)
    pallas_call x6, Pallas kernels, call(): pl.pallas_call(kernel, out_shape=out_shape, in_specs=in_specs, out_specs=...  18.1 us
    ppermute x10, starting transfers between devices, exchange(): got.append(lax.ppermute(edges[len(got)], axes, swaps(sizes, dim, parity)))  8 us
    ppermute x10, waiting for transfers between devices, exchange(): got.append(lax.ppermute(edges[len(got)], axes, swaps(sizes, dim, parity)))  5.34 us
  transfers between devices with their start and end apart: 10, of which 4 were waited for; matrix products, arithmetic and copies ran while one was open for 0% of the time, Pallas kernels for 8%

profile of v3, /device:TPU:0, one launch (start us, length us, event | category | flops | bytes accessed | tf_op | source)
XLA Modules:
  0.0 31.6 jit_solution(8266854519890597302)
XLA Ops:
  0.0 0.0 copy-start.1
  0.0 0.0 copy-start.5
  0.0 0.0 copy-start.6
  0.0 0.0 copy-start.4
  0.0 0.0 copy-start.3
  0.0 0.0 copy-start.2
  0.0 0.0 copy-start
  0.0 2.0 %split_operators.1 = (bf16[3,512,512]{2,1,0:T(8,128)(2,1)S(1)}, bf16[3,512,512]{2,1,0:T(8,128)(2,1)S(1)}, bf16[512,256]{1,0:T(8,128)(2,1)S(1)}, bf16[256,512]{1,0:T(8,128)(2,1)S(1)}) custom-call(f32[3,512,512]{2,1,0:T(8,128)} %ops_any.1), custom_call_target="tpu_custom_call" | custom-call | flops 3623878656 | bytes 2359296 | tf_op jit(solution)/shard_map/split_operators/pallas_call | solution.py:525
  2.1 0.0 copy-done.1
  2.1 0.0 copy-done.5
  2.1 0.0 copy-done.6
  2.1 0.0 copy-done.4
  2.1 0.0 copy-done.3
  2.1 0.0 copy-done.2
  2.2 0.0 copy-done
  2.2 6.1 %first_predictor.1 = (f32[4,288,128]{2,1,0:T(8,128)S(1)}, f32[128,128]{1,0:T(8,128)S(1)}, s32[96,128]{1,0:T(8,128)S(1)}, f32[64,128]{1,0:T(8,128)S(1)}, bf16[256...) custom-call(f32[288,512]{1,0:T(8,128)S(1)} %bitcast.16, ...), custom_call_target="tpu_custom_call" | custom-call | flops 7247757312 | bytes 2359296 | tf_op jit(solution)/shard_map/first_predictor/pallas_call | solution.py:525
  8.2 3.0 %collective-permute-start.1 = (f32[40,128]{1,0:T(8,128)S(1)}, f32[40,128]{1,0:T(8,128)S(1)}, u32[]{:S(2)}, u32[]{:S(2)}) collective-permute-start(f32[40,128]{1,0:T(8,128)S(1)} %get-tuple-element.41), channel_id=1, source_target_pairs={{0,8},{1,9},{2,10},{3,11},{4,12},{5,13},{6,14},{7,15},{8,0},{9,1},... | collective-permute-start | bytes 61448 | tf_op jit(solution)/shard_map/ppermute | solution.py:492
  11.3 0.0 collective-permute-start.2
  11.3 0.5 %collective-permute-start.3 = (f32[40,128]{1,0:T(8,128)S(1)}, f32[40,128]{1,0:T(8,128)S(1)}, u32[]{:S(2)}, u32[]{:S(2)}) collective-permute-start(f32[40,128]{1,0:T(8,128)S(1)} %get-tuple-element.43), channel_id=1, source_target_pairs={{0,2},{1,3},{2,0},{3,1},{4,6},{5,7},{6,4},{7,5},{8,10},{9,11},{10,... | collective-permute-start | bytes 61448 | tf_op jit(solution)/shard_map/ppermute | solution.py:492
  11.8 1.1 %collective-permute-start.4 = (f32[40,128]{1,0:T(8,128)S(1)}, f32[40,128]{1,0:T(8,128)S(1)}, u32[]{:S(2)}, u32[]{:S(2)}) collective-permute-start(f32[40,128]{1,0:T(8,128)S(1)} %get-tuple-element.44), channel_id=1, source_target_pairs={{0,6},{1,7},{2,4},{3,5},{4,2},{5,3},{6,0},{7,1},{8,14},{9,15},{10,... | collective-permute-start | bytes 61448 | tf_op jit(solution)/shard_map/ppermute | solution.py:492
  12.9 0.0 collective-permute-start
  12.9 1.2 %inner_update.2.refs_5_ = f32[4,288,128]{2,1,0:T(8,128)S(1)} custom-call(f32[4,288,128]{2,1,0:T(8,128)S(1)} %get-tuple-element.45.refs_0_, bf16[288,512]{1,0:T(8,128)(2,1)S(1)} %get-tuple-element.46.refs_1_, bf16[288,512]{1,0:T(8,128)(2,1)S(1)} %get-tuple-element.47.refs_2_, f32[288,128]{1,0:T(8,128)S(1)} %get-tuple-element.48.refs_3_, ...), custom_call_target="tpu_custom_call" | custom-call | flops 1811939328 | bytes 2359296 | tf_op jit(solution)/shard_map/inner_update/pallas_call | solution.py:525
  14.1 0.0 collective-permute-done.1.refs_1_
  14.2 0.0 collective-permute-done.2.refs_2_
  14.2 0.0 collective-permute-done.3.refs_3_
  14.2 0.8 %collective-permute-done.4.refs_4_ = f32[40,128]{1,0:T(8,128)S(1)} collective-permute-done((f32[40,128]{1,0:T(8,128)S(1)}, f32[40,128]{1,0:T(8,128)S(1)}, u32[]{:S(2)}, u32[]{:S(2)}) %collective-permute-start.4) | collective-permute-done | bytes 20512 | tf_op jit(solution)/shard_map/ppermute | solution.py:492
  15.0 1.8 %collective-permute-done.refs_0_ = f32[72,128]{1,0:T(8,128)S(1)} collective-permute-done((f32[72,128]{1,0:T(8,128)S(1)}, f32[72,128]{1,0:T(8,128)S(1)}, u32[]{:S(2)}, u32[]{:S(2)}) %collective-permute-start) | collective-permute-done | bytes 36896 | tf_op jit(solution)/shard_map/ppermute | solution.py:492
  16.8 5.8 %outer_update_predictor.1 = (f32[4,288,128]{2,1,0:T(8,128)S(1)}, bf16[288,512]{1,0:T(8,128)(2,1)S(1)}, bf16[288,512]{1,0:T(8,128)(2,1)S(1)}, f32[288,128]{1,0:T(...) custom-call(f32[72,128]{1,0:T(8,128)S(1)} %collective-permute-done.r, ...), custom_call_target="tpu_custom_call" | custom-call | flops 7247757312 | bytes 2359296 | tf_op jit(solution)/shard_map/outer_update_predictor/pallas_call | solution.py:525
  22.6 2.7 %collective-permute-start.6 = (f32[40,128]{1,0:T(8,128)S(1)}, f32[40,128]{1,0:T(8,128)S(1)}, u32[]{:S(2)}, u32[]{:S(2)}) collective-permute-start(f32[40,128]{1,0:T(8,128)S(1)} %get-tuple-element.58), channel_id=1, source_target_pairs={{0,8},{1,9},{2,10},{3,11},{4,12},{5,13},{6,14},{7,15},{8,0},{9,1},... | collective-permute-start | bytes 61448 | tf_op jit(solution)/shard_map/ppermute | solution.py:492
  25.3 0.0 collective-permute-start.7
  25.3 0.5 %collective-permute-start.8 = (f32[40,128]{1,0:T(8,128)S(1)}, f32[40,128]{1,0:T(8,128)S(1)}, u32[]{:S(2)}, u32[]{:S(2)}) collective-permute-start(f32[40,128]{1,0:T(8,128)S(1)} %get-tuple-element.60), channel_id=1, source_target_pairs={{0,2},{1,3},{2,0},{3,1},{4,6},{5,7},{6,4},{7,5},{8,10},{9,11},{10,... | collective-permute-start | bytes 61448 | tf_op jit(solution)/shard_map/ppermute | solution.py:492
  25.9 0.1 collective-permute-start.9
  26.0 0.0 collective-permute-start.5
  26.0 1.3 %inner_update.3.refs_5_ = f32[4,288,128]{2,1,0:T(8,128)S(1)} custom-call(f32[4,288,128]{2,1,0:T(8,128)S(1)} %get-tuple-element.62.refs_0_, bf16[288,512]{1,0:T(8,128)(2,1)S(1)} %get-tuple-element.63.refs_1_, bf16[288,512]{1,0:T(8,128)(2,1)S(1)} %get-tuple-element.64.refs_2_, f32[288,128]{1,0:T(8,128)S(1)} %get-tuple-element.65.refs_3_, ...), custom_call_target="tpu_custom_call" | custom-call | flops 1811939328 | bytes 2359296 | tf_op jit(solution)/shard_map/inner_update/pallas_call | solution.py:525
  27.3 0.0 collective-permute-done.6.refs_1_
  27.3 0.0 collective-permute-done.7.refs_2_
  27.3 0.0 collective-permute-done.8.refs_3_
  27.3 1.8 %collective-permute-done.9.refs_4_ = f32[40,128]{1,0:T(8,128)S(1)} collective-permute-done((f32[40,128]{1,0:T(8,128)S(1)}, f32[40,128]{1,0:T(8,128)S(1)}, u32[]{:S(2)}, u32[]{:S(2)}) %collective-permute-start.9) | collective-permute-done | bytes 20512 | tf_op jit(solution)/shard_map/ppermute | solution.py:492
  29.1 0.8 %collective-permute-done.5.refs_0_ = f32[72,128]{1,0:T(8,128)S(1)} collective-permute-done((f32[72,128]{1,0:T(8,128)S(1)}, f32[72,128]{1,0:T(8,128)S(1)}, u32[]{:S(2)}, u32[]{:S(2)}) %collective-permute-start.5) | collective-permute-done | bytes 36896 | tf_op jit(solution)/shard_map/ppermute | solution.py:492
  29.9 1.7 %outer_update.1 = f32[288,512]{1,0:T(8,128)} custom-call(f32[72,128]{1,0:T(8,128)S(1)} %collective-permute-done.5.refs_0_, f32[40,128]{1,0:T(8,128)S(1)} %collective-permute-done.6.refs_1_, f32[40,128]{1,0:T(8,128)S(1)} %collective-permute-done.7.refs_2_, f32[40,128]{1,0:T(8,128)S(1)} %collective-permute-done.8.refs_3_, ...), custom_call_target="tpu_custom_call" | custom-call | flops 1811939328 | bytes 2359296 | tf_op jit(solution)/shard_map/outer_update/pallas_call | solution.py:525
Async XLA Ops:
  0.0 2.1 %copy-start.1 = (s32[1,1,1,6,32]{4,2,3,1,0:T(1,128)S(1)}, s32[1,1,1,6,32]{4,2,3,1,0:T(1,128)}, u32[]{:S(2)}) copy-start(s32[1,1,1,6,32]{4,2,3,1,0:T(1,128)} %param.15) | copy-start | bytes 2308
  0.0 2.1 %copy-start.5 = (s32[1,1,1,32]{3,2,1,0:T(1,128)S(1)}, s32[1,1,1,32]{3,2,1,0:T(1,128)}, u32[]{:S(2)}) copy-start(s32[1,1,1,32]{3,2,1,0:T(1,128)} %param.14) | copy-start | bytes 388
  0.0 2.1 %copy-start.6 = (s32[1,1,1,32]{3,2,1,0:T(1,128)S(1)}, s32[1,1,1,32]{3,2,1,0:T(1,128)}, u32[]{:S(2)}) copy-start(s32[1,1,1,32]{3,2,1,0:T(1,128)} %param.13) | copy-start | bytes 388
  0.0 2.1 %copy-start.4 = (f32[1,1,1,32]{3,2,1,0:T(1,128)S(1)}, f32[1,1,1,32]{3,2,1,0:T(1,128)}, u32[]{:S(2)}) copy-start(f32[1,1,1,32]{3,2,1,0:T(1,128)} %param.12) | copy-start | bytes 388
  0.0 2.1 %copy-start.3 = (f32[1,1,1,32]{3,2,1,0:T(1,128)S(1)}, f32[1,1,1,32]{3,2,1,0:T(1,128)}, u32[]{:S(2)}) copy-start(f32[1,1,1,32]{3,2,1,0:T(1,128)} %param.11) | copy-start | bytes 388
  0.0 2.1 %copy-start.2 = (f32[1,1,1,32]{3,2,1,0:T(1,128)S(1)}, f32[1,1,1,32]{3,2,1,0:T(1,128)}, u32[]{:S(2)}) copy-start(f32[1,1,1,32]{3,2,1,0:T(1,128)} %param.10) | copy-start | bytes 388
  0.0 2.1 %copy-start = (f32[1,1,1,32,9,512]{5,3,4,2,1,0:T(8,128)S(1)}, f32[1,1,1,32,9,512]{5,3,4,2,1,0:T(8,128)}, u32[]{:S(2)}) copy-start(f32[1,1,1,32,9,512]{5,3,4,2,1,0:T(8,128)} %param.8) | copy-start | bytes 1769476
  8.2 5.9 %collective-permute-start.1 = (f32[40,128]{1,0:T(8,128)S(1)}, f32[40,128]{1,0:T(8,128)S(1)}, u32[]{:S(2)}, u32[]{:S(2)}) collective-permute-start(f32[40,128]{1,0:T(8,128)S(1)} %get-tuple-element.41), channel_id=1, source_target_pairs={{0,8},{1,9},{2,10},{3,11},{4,12},{5,13},{6,14},{7,15},{8,0},{9,1},... | collective-permute-start | bytes 61448 | tf_op jit(solution)/shard_map/ppermute | solution.py:492
  11.3 2.9 %collective-permute-start.2 = (f32[40,128]{1,0:T(8,128)S(1)}, f32[40,128]{1,0:T(8,128)S(1)}, u32[]{:S(2)}, u32[]{:S(2)}) collective-permute-start(f32[40,128]{1,0:T(8,128)S(1)} %get-tuple-element.42), channel_id=1, source_target_pairs={{0,2},{1,3},{2,0},{3,1},{4,6},{5,7},{6,4},{7,5},{8,16},{9,17},{10,... | collective-permute-start | bytes 61448 | tf_op jit(solution)/shard_map/ppermute | solution.py:492
  11.3 2.9 %collective-permute-start.3 = (f32[40,128]{1,0:T(8,128)S(1)}, f32[40,128]{1,0:T(8,128)S(1)}, u32[]{:S(2)}, u32[]{:S(2)}) collective-permute-start(f32[40,128]{1,0:T(8,128)S(1)} %get-tuple-element.43), channel_id=1, source_target_pairs={{0,2},{1,3},{2,0},{3,1},{4,6},{5,7},{6,4},{7,5},{8,10},{9,11},{10,... | collective-permute-start | bytes 61448 | tf_op jit(solution)/shard_map/ppermute | solution.py:492
  11.8 3.2 %collective-permute-start.4 = (f32[40,128]{1,0:T(8,128)S(1)}, f32[40,128]{1,0:T(8,128)S(1)}, u32[]{:S(2)}, u32[]{:S(2)}) collective-permute-start(f32[40,128]{1,0:T(8,128)S(1)} %get-tuple-element.44), channel_id=1, source_target_pairs={{0,6},{1,7},{2,4},{3,5},{4,2},{5,3},{6,0},{7,1},{8,14},{9,15},{10,... | collective-permute-start | bytes 61448 | tf_op jit(solution)/shard_map/ppermute | solution.py:492
  12.9 4.0 %collective-permute-start = (f32[72,128]{1,0:T(8,128)S(1)}, f32[72,128]{1,0:T(8,128)S(1)}, u32[]{:S(2)}, u32[]{:S(2)}) collective-permute-start(f32[72,128]{1,0:T(8,128)S(1)} %get-tuple-element.40), channel_id=1, source_target_pairs={{0,1},{1,0},{2,3},{3,2},{4,5},{5,4},{6,7},{7,6},{8,9},{9,8},{10,11... | collective-permute-start | bytes 110600 | tf_op jit(solution)/shard_map/ppermute | solution.py:492
  22.6 4.6 %collective-permute-start.6 = (f32[40,128]{1,0:T(8,128)S(1)}, f32[40,128]{1,0:T(8,128)S(1)}, u32[]{:S(2)}, u32[]{:S(2)}) collective-permute-start(f32[40,128]{1,0:T(8,128)S(1)} %get-tuple-element.58), channel_id=1, source_target_pairs={{0,8},{1,9},{2,10},{3,11},{4,12},{5,13},{6,14},{7,15},{8,0},{9,1},... | collective-permute-start | bytes 61448 | tf_op jit(solution)/shard_map/ppermute | solution.py:492
  25.3 1.9 %collective-permute-start.7 = (f32[40,128]{1,0:T(8,128)S(1)}, f32[40,128]{1,0:T(8,128)S(1)}, u32[]{:S(2)}, u32[]{:S(2)}) collective-permute-start(f32[40,128]{1,0:T(8,128)S(1)} %get-tuple-element.59), channel_id=1, source_target_pairs={{0,2},{1,3},{2,0},{3,1},{4,6},{5,7},{6,4},{7,5},{8,16},{9,17},{10,... | collective-permute-start | bytes 61448 | tf_op jit(solution)/shard_map/ppermute | solution.py:492
  25.3 1.9 %collective-permute-start.8 = (f32[40,128]{1,0:T(8,128)S(1)}, f32[40,128]{1,0:T(8,128)S(1)}, u32[]{:S(2)}, u32[]{:S(2)}) collective-permute-start(f32[40,128]{1,0:T(8,128)S(1)} %get-tuple-element.60), channel_id=1, source_target_pairs={{0,2},{1,3},{2,0},{3,1},{4,6},{5,7},{6,4},{7,5},{8,10},{9,11},{10,... | collective-permute-start | bytes 61448 | tf_op jit(solution)/shard_map/ppermute | solution.py:492
  25.9 3.2 %collective-permute-start.9 = (f32[40,128]{1,0:T(8,128)S(1)}, f32[40,128]{1,0:T(8,128)S(1)}, u32[]{:S(2)}, u32[]{:S(2)}) collective-permute-start(f32[40,128]{1,0:T(8,128)S(1)} %get-tuple-element.61), channel_id=1, source_target_pairs={{0,6},{1,7},{2,4},{3,5},{4,2},{5,3},{6,0},{7,1},{8,14},{9,15},{10,... | collective-permute-start | bytes 61448 | tf_op jit(solution)/shard_map/ppermute | solution.py:492
  26.0 4.0 %collective-permute-start.5 = (f32[72,128]{1,0:T(8,128)S(1)}, f32[72,128]{1,0:T(8,128)S(1)}, u32[]{:S(2)}, u32[]{:S(2)}) collective-permute-start(f32[72,128]{1,0:T(8,128)S(1)} %get-tuple-element.57), channel_id=1, source_target_pairs={{0,1},{1,0},{2,3},{3,2},{4,5},{5,4},{6,7},{7,6},{8,9},{9,8},{10,11... | collective-permute-start | bytes 110600 | tf_op jit(solution)/shard_map/ppermute | solution.py:492

commit v4 on v3

--- a/solution.py
+++ b/solution.py
@@ -57,6 +57,20 @@
     return lax.broadcasted_iota(jnp.int32, (rows, 128), 1)
 
 
+def combine(deriv, rows, inv_rho, lame, shear, shear2, cols, emit):
+    part = lambda dim, row: deriv[dim][row * rows : (row + 1) * rows]
+    div = lame * (part(0, 0) + part(1, 1) + part(2, 2))
+    emit(0, cols, inv_rho * (part(0, 3) + part(1, 3) + part(2, 3)))
+    emit(1, cols, inv_rho * (part(0, 4) + part(1, 4) + part(2, 4)))
+    emit(2, cols, inv_rho * (part(0, 5) + part(1, 5) + part(2, 5)))
+    emit(3, cols, div + shear2 * part(0, 0))
+    emit(4, cols, div + shear2 * part(1, 1))
+    emit(5, cols, div + shear2 * part(2, 2))
+    emit(6, cols, shear * (part(0, 1) + part(1, 0)))
+    emit(7, cols, shear * (part(1, 2) + part(2, 1)))
+    emit(8, cols, shear * (part(0, 2) + part(2, 0)))
+
+
 def rate(high, low, w_high, w_low, par, stride, rows, emit, block=256):
     nodes = w_high.shape[-1]
     inv_rho = wide(par[0:rows], block // 128)
@@ -65,23 +79,16 @@
     shear2 = 2.0 * shear
     for start in range(0, nodes, block):
         cols = slice(start, start + block)
-        deriv = []
-        for dim in range(3):
-            top = jnp.concatenate([high[f * stride : f * stride + rows] for f in PICKED[dim]], axis=0)
-            rest = jnp.concatenate([low[f * stride : f * stride + rows] for f in PICKED[dim]], axis=0)
-            both = dot(jnp.concatenate([top, rest], axis=0), w_high[dim, :, cols])
-            deriv.append(both[: 6 * rows] + both[6 * rows :] + dot(top, w_low[dim, :, cols]))
-        part = lambda dim, row: deriv[dim][row * rows : (row + 1) * rows]
-        div = lame * (part(0, 0) + part(1, 1) + part(2, 2))
-        emit(0, cols, inv_rho * (part(0, 3) + part(1, 3) + part(2, 3)))
-        emit(1, cols, inv_rho * (part(0, 4) + part(1, 4) + part(2, 4)))
-        emit(2, cols, inv_rho * (part(0, 5) + part(1, 5) + part(2, 5)))
-        emit(3, cols, div + shear2 * part(0, 0))
-        emit(4, cols, div + shear2 * part(1, 1))
-        emit(5, cols, div + shear2 * part(2, 2))
-        emit(6, cols, shear * (part(0, 1) + part(1, 0)))
-        emit(7, cols, shear * (part(1, 2) + part(2, 1)))
-        emit(8, cols, shear * (part(0, 2) + part(2, 0)))
+        deriv = [None] * 3
+        for k in range(0, nodes, 256):
+            depth = slice(k, k + 256)
+            for dim in range(3):
+                top = jnp.concatenate([high[f * stride : f * stride + rows, depth] for f in PICKED[dim]], axis=0)
+                rest = jnp.concatenate([low[f * stride : f * stride + rows, depth] for f in PICKED[dim]], axis=0)
+                both = dot(jnp.concatenate([top, rest], axis=0), w_high[dim, depth, cols])
+                part = both[: 6 * rows] + both[6 * rows :] + dot(top, w_low[dim, depth, cols])
+                deriv[dim] = part if deriv[dim] is None else deriv[dim] + part
+        combine(deriv, rows, inv_rho, lame, shear, shear2, cols, emit)
 
 
 def correction(jump, par, count, dim, rows):
@@ -123,12 +130,12 @@
     target[last, top] = target[last, top] + jnp.where(lanes < 64, 0.0, scaled)
 
 
-def lift_inner(target, face_high, face_low, lift_table):
+def lift_inner(target, source, face_high, face_low, lift_table):
     rows, nodes = target.shape[1], lift_table.shape[1]
     for start in range(0, nodes, 256):
         cols = slice(start, start + 256)
         lifted = dot(face_high[...], lift_table[:, cols]) + dot(face_low[...], lift_table[:, cols])
-        add(target, slice(0, rows), cols, DT * LIFT * lifted)
+        put(target, slice(0, rows), cols, get(source, slice(0, rows), cols) + DT * LIFT * lifted)
 
 
 def fetch(copies):
@@ -167,8 +174,6 @@
     int_high, int_low, trace_x, trace_y, trace_z, *edges = outs
     h0, l0, h1, l1, total, p0, p1, p2, p3, series = scratch
     nodes = h0.shape[1]
-    tiles_of_node = nodes // 128
-    every = slice(0, nodes)
     half = count // 2
 
     def first(f, cols, value):
@@ -185,37 +190,34 @@
 
     rate(h1, l1, w_high, w_low, par, count, count, then)
 
-    @pl.when(jnp.max(hot_par[3 * half : 3 * half + 8]) > 0.0)
-    def _():
-        for start in range(0, nodes, 256):
-            cols = slice(start, start + 256)
-            p0[:, cols] = moved(pack, h0, cols, count, half).astype(BF16)
-            p1[:, cols] = moved(pack, l0, cols, count, half).astype(BF16)
-        buffers = [(p0, p1), (p2, p3)]
-        for order in (3, 4, 5):
-            weight = DT**order / math.factorial(order + 1)
-            source, target = buffers[(order - 3) % 2], buffers[(order - 2) % 2]
-
-            def more(f, cols, value, order=order, weight=weight, target=target):
-                rows = slice(f * half, (f + 1) * half)
-                part = weight * value
-                if order > 3:
-                    part = part + series[rows, cols]
-                if order < 5:
-                    series[rows, cols] = part
-                    part = value
-                target[0][rows, cols], target[1][rows, cols] = split(part)
-
-            rate(source[0], source[1], w_high, w_low, hot_par, half, half, more)
-        for start in range(0, nodes, 256):
-            cols = slice(start, start + 256)
-            extra = moved(unpack, p2, cols, half, count) + moved(unpack, p3, cols, half, count)
-            add(total, slice(0, fields * count), cols, extra)
-
+    for start in range(0, nodes, 256):
+        cols = slice(start, start + 256)
+        p0[:, cols] = moved(pack, h0, cols, count, half).astype(BF16)
+        p1[:, cols] = moved(pack, l0, cols, count, half).astype(BF16)
+    buffers = [(p0, p1), (p2, p3)]
+    for order in (3, 4, 5):
+        weight = DT**order / math.factorial(order + 1)
+        source, target = buffers[(order - 3) % 2], buffers[(order - 2) % 2]
+
+        def more(f, cols, value, order=order, weight=weight, target=target):
+            rows = slice(f * half, (f + 1) * half)
+            part = weight * value
+            if order > 3:
+                part = part + series[rows, cols]
+            if order < 5:
+                series[rows, cols] = part
+                part = value
+            target[0][rows, cols], target[1][rows, cols] = split(part)
+
+        rate(source[0], source[1], w_high, w_low, hot_par, half, half, more)
+    for start in range(0, nodes, 256):
+        cols = slice(start, start + 256)
+        extra = moved(unpack, p2, cols, half, count) + moved(unpack, p3, cols, half, count)
+        add(total, slice(0, fields * count), cols, extra)
     for f in range(fields):
         rows = slice(f * count, (f + 1) * count)
-        int_high[rows], int_low[rows] = split(get(total, rows, every))
-        trace_x[rows] = jnp.where(lanes_of(count) < 64, total[0, rows], total[tiles_of_node - 1, rows])
+        int_high[rows], int_low[rows] = split(get(total, rows, slice(0, nodes)))
+        trace_x[rows] = jnp.where(lanes_of(count) < 64, total[0, rows], total[total.shape[0] - 1, rows])
     faces = dot(int_high[...], face_table[...]) + dot(int_low[...], face_table[...])
     trace_y[...] = faces[:, 0:128]
     trace_z[...] = faces[:, 128:256]
@@ -285,22 +287,10 @@
                 cols = slice((dim - 1) * 128, dim * 128)
                 rows = slice(f * count, (f + 1) * count)
                 face_high[rows, cols], face_low[rows, cols] = split(fixed[f])
-    lift_inner(base, face_high, face_low, lift_table)
+    lift_inner(base, base, face_high, face_low, lift_table)
 
 
 def outer(count, fields, sizes, got, base, par, index, lift_table, out, halo, face_high, face_low):
-    middle = (fields + 1) // 2
-    lower, upper = received(got[0], *sizes[0])
-    out[...] = base[...]
-    for end, (low, high) in enumerate((lower, upper)):
-        rows = slice(0, 8) if end == 0 else slice(count - 8, count)
-        jump = []
-        for f in range(fields):
-            part, at = (low, f) if f < middle else (high, f - middle)
-            jump.append(orient(part[at * 8 : at * 8 + 8], index[rows]))
-        fixed = correction(jump, par, count, 0, rows)
-        for f in range(fields):
-            lift_edges(out, fixed[f], f, rows, count)
     tiles = fields * count // 8
     pairs = fields * count // 4
     for dim in (1, 2):
@@ -322,7 +312,18 @@
             cols = slice((dim - 1) * 128, dim * 128)
             rows = slice(f * count, (f + 1) * count)
             face_high[rows, cols], face_low[rows, cols] = split(fixed[f])
-    lift_inner(out, face_high, face_low, lift_table)
+    lift_inner(out, base, face_high, face_low, lift_table)
+    middle = (fields + 1) // 2
+    lower, upper = received(got[0], *sizes[0])
+    for end, (low, high) in enumerate((lower, upper)):
+        rows = slice(0, 8) if end == 0 else slice(count - 8, count)
+        jump = []
+        for f in range(fields):
+            part, at = (low, f) if f < middle else (high, f - middle)
+            jump.append(orient(part[at * 8 : at * 8 + 8], index[rows]))
+        fixed = correction(jump, par, count, 0, rows)
+        for f in range(fields):
+            lift_edges(out, fixed[f], f, rows, count)
 
 
 def table_kernel(ops_any, w_high, w_low, face_table, lift_table, ops, sems):

time: 31.7 us -> 31.9 us (level)
  starting transfers between devices: 8 us -> 11.5 us
  waiting for transfers between devices: 5.34 us -> 2.3 us
  Pallas kernels: 18.1 us -> 17.7 us
    ppermute x10, starting transfers between devices: 8 us -> 11.5 us  [exchange(): got.append(lax.ppermute(edges[len(got)], axes, swaps(sizes, dim, parity)))]
    ppermute x10, waiting for transfers between devices: 5.34 us -> 2.3 us  [exchange(): got.append(lax.ppermute(edges[len(got)], axes, swaps(sizes, dim, parity)))]
    pallas_call x6, Pallas kernels: 18.1 us -> 17.7 us  [call(): pl.pallas_call(kernel, out_shape=out_shape, in_specs=in_specs, out_specs=...]
  transfers between devices with their start and end apart: 10 -> 10, of which waited for: 4 -> 3; matrix products, arithmetic and copies ran while one was open for 0% -> 0% of each run, Pallas kernels for 8% -> 8%
where the time goes in v4:
time: 31.9 us; the launch traced here: 31.7 us
  Pallas kernels  17.7 us (55%)
  starting transfers between devices  11.5 us (36%)
  waiting for transfers between devices  2.3 us (7%)
    pallas_call x6, Pallas kernels, call(): pl.pallas_call(kernel, out_shape=out_shape, in_specs=in_specs, out_specs=...  17.7 us
    ppermute x10, starting transfers between devices, exchange(): got.append(lax.ppermute(edges[len(got)], axes, swaps(sizes, dim, parity)))  11.5 us
    ppermute x10, waiting for transfers between devices, exchange(): got.append(lax.ppermute(edges[len(got)], axes, swaps(sizes, dim, parity)))  2.3 us
  transfers between devices with their start and end apart: 10, of which 3 were waited for; matrix products, arithmetic and copies ran while one was open for 0% of the time, Pallas kernels for 8%

profile of v4, /device:TPU:0, one launch (start us, length us, event | category | flops | bytes accessed | tf_op | source)
XLA Modules:
  0.0 31.7 jit_solution(13144790902754677535)
XLA Ops:
  0.0 0.0 copy-start.1
  0.0 0.0 copy-start.5
  0.0 0.0 copy-start.6
  0.0 0.0 copy-start.4
  0.0 0.0 copy-start.3
  0.0 0.0 copy-start.2
  0.0 0.0 copy-start
  0.0 2.0 %split_operators.1 = (bf16[3,512,512]{2,1,0:T(8,128)(2,1)S(1)}, bf16[3,512,512]{2,1,0:T(8,128)(2,1)S(1)}, bf16[512,256]{1,0:T(8,128)(2,1)S(1)}, bf16[256,512]{1,0:T(8,128)(2,1)S(1)}) custom-call(f32[3,512,512]{2,1,0:T(8,128)} %ops_any.1), custom_call_target="tpu_custom_call" | custom-call | flops 3623878656 | bytes 2359296 | tf_op jit(solution)/shard_map/split_operators/pallas_call | solution.py:526
  2.1 0.0 copy-done.1
  2.1 0.0 copy-done.5
  2.1 0.0 copy-done.6
  2.1 0.0 copy-done.4
  2.1 0.0 copy-done.3
  2.1 0.0 copy-done.2
  2.2 0.0 copy-done
  2.2 5.9 %first_predictor.1 = (f32[4,288,128]{2,1,0:T(8,128)S(1)}, f32[128,128]{1,0:T(8,128)S(1)}, s32[96,128]{1,0:T(8,128)S(1)}, f32[64,128]{1,0:T(8,128)S(1)}, bf16[256...) custom-call(f32[288,512]{1,0:T(8,128)S(1)} %bitcast.16, ...), custom_call_target="tpu_custom_call" | custom-call | flops 7247757312 | bytes 2359296 | tf_op jit(solution)/shard_map/first_predictor/pallas_call | solution.py:526
  8.1 3.0 %collective-permute-start.1 = (f32[40,128]{1,0:T(8,128)S(1)}, f32[40,128]{1,0:T(8,128)S(1)}, u32[]{:S(2)}, u32[]{:S(2)}) collective-permute-start(f32[40,128]{1,0:T(8,128)S(1)} %get-tuple-element.41), channel_id=1, source_target_pairs={{0,8},{1,9},{2,10},{3,11},{4,12},{5,13},{6,14},{7,15},{8,0},{9,1},... | collective-permute-start | bytes 61448 | tf_op jit(solution)/shard_map/ppermute | solution.py:493
  11.1 0.0 collective-permute-start.2
  11.1 0.5 %collective-permute-start.3 = (f32[40,128]{1,0:T(8,128)S(1)}, f32[40,128]{1,0:T(8,128)S(1)}, u32[]{:S(2)}, u32[]{:S(2)}) collective-permute-start(f32[40,128]{1,0:T(8,128)S(1)} %get-tuple-element.43), channel_id=1, source_target_pairs={{0,2},{1,3},{2,0},{3,1},{4,6},{5,7},{6,4},{7,5},{8,10},{9,11},{10,... | collective-permute-start | bytes 61448 | tf_op jit(solution)/shard_map/ppermute | solution.py:493
  11.6 1.1 %collective-permute-start.4 = (f32[40,128]{1,0:T(8,128)S(1)}, f32[40,128]{1,0:T(8,128)S(1)}, u32[]{:S(2)}, u32[]{:S(2)}) collective-permute-start(f32[40,128]{1,0:T(8,128)S(1)} %get-tuple-element.44), channel_id=1, source_target_pairs={{0,6},{1,7},{2,4},{3,5},{4,2},{5,3},{6,0},{7,1},{8,14},{9,15},{10,... | collective-permute-start | bytes 61448 | tf_op jit(solution)/shard_map/ppermute | solution.py:493
  12.7 1.5 %collective-permute-start = (f32[72,128]{1,0:T(8,128)S(1)}, f32[72,128]{1,0:T(8,128)S(1)}, u32[]{:S(2)}, u32[]{:S(2)}) collective-permute-start(f32[72,128]{1,0:T(8,128)S(1)} %get-tuple-element.40), channel_id=1, source_target_pairs={{0,1},{1,0},{2,3},{3,2},{4,5},{5,4},{6,7},{7,6},{8,9},{9,8},{10,11... | collective-permute-start | bytes 110600 | tf_op jit(solution)/shard_map/ppermute | solution.py:493
  14.3 1.3 %inner_update.2.refs_5_ = f32[4,288,128]{2,1,0:T(8,128)S(1)} custom-call(f32[4,288,128]{2,1,0:T(8,128)S(1)} %get-tuple-element.45.refs_0_, bf16[288,512]{1,0:T(8,128)(2,1)S(1)} %get-tuple-element.46.refs_1_, bf16[288,512]{1,0:T(8,128)(2,1)S(1)} %get-tuple-element.47.refs_2_, f32[288,128]{1,0:T(8,128)S(1)} %get-tuple-element.48.refs_3_, ...), custom_call_target="tpu_custom_call" | custom-call | flops 1811939328 | bytes 2359296 | tf_op jit(solution)/shard_map/inner_update/pallas_call | solution.py:526
  15.5 0.0 collective-permute-done.1.refs_1_
  15.5 0.0 collective-permute-done.2.refs_2_
  15.5 0.0 collective-permute-done.3.refs_3_
  15.6 0.0 collective-permute-done.4.refs_4_
  15.6 1.1 %collective-permute-done.refs_0_ = f32[72,128]{1,0:T(8,128)S(1)} collective-permute-done((f32[72,128]{1,0:T(8,128)S(1)}, f32[72,128]{1,0:T(8,128)S(1)}, u32[]{:S(2)}, u32[]{:S(2)}) %collective-permute-start) | collective-permute-done | bytes 36896 | tf_op jit(solution)/shard_map/ppermute | solution.py:493
  16.7 5.5 %outer_update_predictor.1 = (f32[4,288,128]{2,1,0:T(8,128)S(1)}, bf16[288,512]{1,0:T(8,128)(2,1)S(1)}, bf16[288,512]{1,0:T(8,128)(2,1)S(1)}, f32[288,128]{1,0:T(...) custom-call(f32[72,128]{1,0:T(8,128)S(1)} %collective-permute-done.r, ...), custom_call_target="tpu_custom_call" | custom-call | flops 7247757312 | bytes 2359296 | tf_op jit(solution)/shard_map/outer_update_predictor/pallas_call | solution.py:526
  22.2 3.2 %collective-permute-start.6 = (f32[40,128]{1,0:T(8,128)S(1)}, f32[40,128]{1,0:T(8,128)S(1)}, u32[]{:S(2)}, u32[]{:S(2)}) collective-permute-start(f32[40,128]{1,0:T(8,128)S(1)} %get-tuple-element.58), channel_id=1, source_target_pairs={{0,8},{1,9},{2,10},{3,11},{4,12},{5,13},{6,14},{7,15},{8,0},{9,1},... | collective-permute-start | bytes 61448 | tf_op jit(solution)/shard_map/ppermute | solution.py:493
  25.4 0.0 collective-permute-start.7
  25.4 0.5 %collective-permute-start.8 = (f32[40,128]{1,0:T(8,128)S(1)}, f32[40,128]{1,0:T(8,128)S(1)}, u32[]{:S(2)}, u32[]{:S(2)}) collective-permute-start(f32[40,128]{1,0:T(8,128)S(1)} %get-tuple-element.60), channel_id=1, source_target_pairs={{0,2},{1,3},{2,0},{3,1},{4,6},{5,7},{6,4},{7,5},{8,10},{9,11},{10,... | collective-permute-start | bytes 61448 | tf_op jit(solution)/shard_map/ppermute | solution.py:493
  25.9 0.2 collective-permute-start.9
  26.1 1.5 %collective-permute-start.5 = (f32[72,128]{1,0:T(8,128)S(1)}, f32[72,128]{1,0:T(8,128)S(1)}, u32[]{:S(2)}, u32[]{:S(2)}) collective-permute-start(f32[72,128]{1,0:T(8,128)S(1)} %get-tuple-element.57), channel_id=1, source_target_pairs={{0,1},{1,0},{2,3},{3,2},{4,5},{5,4},{6,7},{7,6},{8,9},{9,8},{10,11... | collective-permute-start | bytes 110600 | tf_op jit(solution)/shard_map/ppermute | solution.py:493
  27.6 1.3 %inner_update.3.refs_5_ = f32[4,288,128]{2,1,0:T(8,128)S(1)} custom-call(f32[4,288,128]{2,1,0:T(8,128)S(1)} %get-tuple-element.62.refs_0_, bf16[288,512]{1,0:T(8,128)(2,1)S(1)} %get-tuple-element.63.refs_1_, bf16[288,512]{1,0:T(8,128)(2,1)S(1)} %get-tuple-element.64.refs_2_, f32[288,128]{1,0:T(8,128)S(1)} %get-tuple-element.65.refs_3_, ...), custom_call_target="tpu_custom_call" | custom-call | flops 1811939328 | bytes 2359296 | tf_op jit(solution)/shard_map/inner_update/pallas_call | solution.py:526
  28.9 0.0 collective-permute-done.6.refs_1_
  28.9 0.0 collective-permute-done.7.refs_2_
  28.9 0.0 collective-permute-done.8.refs_3_
  28.9 0.3 collective-permute-done.9.refs_4_
  29.2 0.9 %collective-permute-done.5.refs_0_ = f32[72,128]{1,0:T(8,128)S(1)} collective-permute-done((f32[72,128]{1,0:T(8,128)S(1)}, f32[72,128]{1,0:T(8,128)S(1)}, u32[]{:S(2)}, u32[]{:S(2)}) %collective-permute-start.5) | collective-permute-done | bytes 36896 | tf_op jit(solution)/shard_map/ppermute | solution.py:493
  30.1 1.7 %outer_update.1 = f32[288,512]{1,0:T(8,128)} custom-call(f32[72,128]{1,0:T(8,128)S(1)} %collective-permute-done.5.refs_0_, f32[40,128]{1,0:T(8,128)S(1)} %collective-permute-done.6.refs_1_, f32[40,128]{1,0:T(8,128)S(1)} %collective-permute-done.7.refs_2_, f32[40,128]{1,0:T(8,128)S(1)} %collective-permute-done.8.refs_3_, ...), custom_call_target="tpu_custom_call" | custom-call | flops 1811939328 | bytes 2359296 | tf_op jit(solution)/shard_map/outer_update/pallas_call | solution.py:526
Async XLA Ops:
  0.0 2.1 %copy-start.1 = (s32[1,1,1,6,32]{4,2,3,1,0:T(1,128)S(1)}, s32[1,1,1,6,32]{4,2,3,1,0:T(1,128)}, u32[]{:S(2)}) copy-start(s32[1,1,1,6,32]{4,2,3,1,0:T(1,128)} %param.15) | copy-start | bytes 2308
  0.0 2.1 %copy-start.5 = (s32[1,1,1,32]{3,2,1,0:T(1,128)S(1)}, s32[1,1,1,32]{3,2,1,0:T(1,128)}, u32[]{:S(2)}) copy-start(s32[1,1,1,32]{3,2,1,0:T(1,128)} %param.14) | copy-start | bytes 388
  0.0 2.1 %copy-start.6 = (s32[1,1,1,32]{3,2,1,0:T(1,128)S(1)}, s32[1,1,1,32]{3,2,1,0:T(1,128)}, u32[]{:S(2)}) copy-start(s32[1,1,1,32]{3,2,1,0:T(1,128)} %param.13) | copy-start | bytes 388
  0.0 2.1 %copy-start.4 = (f32[1,1,1,32]{3,2,1,0:T(1,128)S(1)}, f32[1,1,1,32]{3,2,1,0:T(1,128)}, u32[]{:S(2)}) copy-start(f32[1,1,1,32]{3,2,1,0:T(1,128)} %param.12) | copy-start | bytes 388
  0.0 2.1 %copy-start.3 = (f32[1,1,1,32]{3,2,1,0:T(1,128)S(1)}, f32[1,1,1,32]{3,2,1,0:T(1,128)}, u32[]{:S(2)}) copy-start(f32[1,1,1,32]{3,2,1,0:T(1,128)} %param.11) | copy-start | bytes 388
  0.0 2.1 %copy-start.2 = (f32[1,1,1,32]{3,2,1,0:T(1,128)S(1)}, f32[1,1,1,32]{3,2,1,0:T(1,128)}, u32[]{:S(2)}) copy-start(f32[1,1,1,32]{3,2,1,0:T(1,128)} %param.10) | copy-start | bytes 388
  0.0 2.1 %copy-start = (f32[1,1,1,32,9,512]{5,3,4,2,1,0:T(8,128)S(1)}, f32[1,1,1,32,9,512]{5,3,4,2,1,0:T(8,128)}, u32[]{:S(2)}) copy-start(f32[1,1,1,32,9,512]{5,3,4,2,1,0:T(8,128)} %param.8) | copy-start | bytes 1769476
  8.1 7.4 %collective-permute-start.1 = (f32[40,128]{1,0:T(8,128)S(1)}, f32[40,128]{1,0:T(8,128)S(1)}, u32[]{:S(2)}, u32[]{:S(2)}) collective-permute-start(f32[40,128]{1,0:T(8,128)S(1)} %get-tuple-element.41), channel_id=1, source_target_pairs={{0,8},{1,9},{2,10},{3,11},{4,12},{5,13},{6,14},{7,15},{8,0},{9,1},... | collective-permute-start | bytes 61448 | tf_op jit(solution)/shard_map/ppermute | solution.py:493
  11.1 4.4 %collective-permute-start.2 = (f32[40,128]{1,0:T(8,128)S(1)}, f32[40,128]{1,0:T(8,128)S(1)}, u32[]{:S(2)}, u32[]{:S(2)}) collective-permute-start(f32[40,128]{1,0:T(8,128)S(1)} %get-tuple-element.42), channel_id=1, source_target_pairs={{0,2},{1,3},{2,0},{3,1},{4,6},{5,7},{6,4},{7,5},{8,16},{9,17},{10,... | collective-permute-start | bytes 61448 | tf_op jit(solution)/shard_map/ppermute | solution.py:493
  11.1 4.4 %collective-permute-start.3 = (f32[40,128]{1,0:T(8,128)S(1)}, f32[40,128]{1,0:T(8,128)S(1)}, u32[]{:S(2)}, u32[]{:S(2)}) collective-permute-start(f32[40,128]{1,0:T(8,128)S(1)} %get-tuple-element.43), channel_id=1, source_target_pairs={{0,2},{1,3},{2,0},{3,1},{4,6},{5,7},{6,4},{7,5},{8,10},{9,11},{10,... | collective-permute-start | bytes 61448 | tf_op jit(solution)/shard_map/ppermute | solution.py:493
  11.6 3.9 %collective-permute-start.4 = (f32[40,128]{1,0:T(8,128)S(1)}, f32[40,128]{1,0:T(8,128)S(1)}, u32[]{:S(2)}, u32[]{:S(2)}) collective-permute-start(f32[40,128]{1,0:T(8,128)S(1)} %get-tuple-element.44), channel_id=1, source_target_pairs={{0,6},{1,7},{2,4},{3,5},{4,2},{5,3},{6,0},{7,1},{8,14},{9,15},{10,... | collective-permute-start | bytes 61448 | tf_op jit(solution)/shard_map/ppermute | solution.py:493
  12.7 4.0 %collective-permute-start = (f32[72,128]{1,0:T(8,128)S(1)}, f32[72,128]{1,0:T(8,128)S(1)}, u32[]{:S(2)}, u32[]{:S(2)}) collective-permute-start(f32[72,128]{1,0:T(8,128)S(1)} %get-tuple-element.40), channel_id=1, source_target_pairs={{0,1},{1,0},{2,3},{3,2},{4,5},{5,4},{6,7},{7,6},{8,9},{9,8},{10,11... | collective-permute-start | bytes 110600 | tf_op jit(solution)/shard_map/ppermute | solution.py:493
  22.2 6.7 %collective-permute-start.6 = (f32[40,128]{1,0:T(8,128)S(1)}, f32[40,128]{1,0:T(8,128)S(1)}, u32[]{:S(2)}, u32[]{:S(2)}) collective-permute-start(f32[40,128]{1,0:T(8,128)S(1)} %get-tuple-element.58), channel_id=1, source_target_pairs={{0,8},{1,9},{2,10},{3,11},{4,12},{5,13},{6,14},{7,15},{8,0},{9,1},... | collective-permute-start | bytes 61448 | tf_op jit(solution)/shard_map/ppermute | solution.py:493
  25.4 3.5 %collective-permute-start.7 = (f32[40,128]{1,0:T(8,128)S(1)}, f32[40,128]{1,0:T(8,128)S(1)}, u32[]{:S(2)}, u32[]{:S(2)}) collective-permute-start(f32[40,128]{1,0:T(8,128)S(1)} %get-tuple-element.59), channel_id=1, source_target_pairs={{0,2},{1,3},{2,0},{3,1},{4,6},{5,7},{6,4},{7,5},{8,16},{9,17},{10,... | collective-permute-start | bytes 61448 | tf_op jit(solution)/shard_map/ppermute | solution.py:493
  25.4 3.5 %collective-permute-start.8 = (f32[40,128]{1,0:T(8,128)S(1)}, f32[40,128]{1,0:T(8,128)S(1)}, u32[]{:S(2)}, u32[]{:S(2)}) collective-permute-start(f32[40,128]{1,0:T(8,128)S(1)} %get-tuple-element.60), channel_id=1, source_target_pairs={{0,2},{1,3},{2,0},{3,1},{4,6},{5,7},{6,4},{7,5},{8,10},{9,11},{10,... | collective-permute-start | bytes 61448 | tf_op jit(solution)/shard_map/ppermute | solution.py:493
  25.9 3.2 %collective-permute-start.9 = (f32[40,128]{1,0:T(8,128)S(1)}, f32[40,128]{1,0:T(8,128)S(1)}, u32[]{:S(2)}, u32[]{:S(2)}) collective-permute-start(f32[40,128]{1,0:T(8,128)S(1)} %get-tuple-element.61), channel_id=1, source_target_pairs={{0,6},{1,7},{2,4},{3,5},{4,2},{5,3},{6,0},{7,1},{8,14},{9,15},{10,... | collective-permute-start | bytes 61448 | tf_op jit(solution)/shard_map/ppermute | solution.py:493
  26.1 4.0 %collective-permute-start.5 = (f32[72,128]{1,0:T(8,128)S(1)}, f32[72,128]{1,0:T(8,128)S(1)}, u32[]{:S(2)}, u32[]{:S(2)}) collective-permute-start(f32[72,128]{1,0:T(8,128)S(1)} %get-tuple-element.57), channel_id=1, source_target_pairs={{0,1},{1,0},{2,3},{3,2},{4,5},{5,4},{6,7},{7,6},{8,9},{9,8},{10,11... | collective-permute-start | bytes 110600 | tf_op jit(solution)/shard_map/ppermute | solution.py:493

commit v5 on v4

--- a/solution.py
+++ b/solution.py
@@ -149,16 +149,18 @@
     minus = lanes_of(low.shape[0]) < 64
     plus_face = jnp.where(minus, pltpu.roll(low, 64, 1), high)
     minus_face = jnp.where(minus, low, pltpu.roll(high, 64, 1))
-    targets[0][...] = jnp.where(up, plus_face, minus_face)
-    if len(targets) > 1:
-        targets[1][...] = jnp.where(up, minus_face, plus_face)
-
-
-def received(pair, axis, size):
+    rows = low.shape[0]
+    for parity, target in enumerate(targets):
+        target[0:rows] = jnp.where(up, plus_face, minus_face) if parity == 0 else jnp.where(up, minus_face, plus_face)
+        if target.shape[0] > rows:
+            target[rows:] = jnp.zeros((target.shape[0] - rows, 128), F32)
+
+
+def received(pair, rows, axis, size):
     here = lax.axis_index(axis)
     odd = here % 2 == 1
-    first = pair[0][...]
-    second = first if pair[1] is None else pair[1][...]
+    first = pair[0][0:rows]
+    second = first if pair[1] is None else pair[1][0:rows]
     minus = lanes_of(first.shape[0]) < 64
     lower = jnp.where(odd, first, second)
     upper = jnp.where(odd, second, first)
@@ -235,7 +237,7 @@
     ends.append(ends[-1])
     send(jnp.concatenate(ends[:middle]), jnp.concatenate(ends[middle : 2 * middle]), ups[0], targets[0])
     tiles = fields * count // 8
-    pad = targets[1][0].shape[0] - tiles
+    pad = -tiles % 8
     minus = lanes_of(tiles) < 64
     ends = []
     for m in range(2):
@@ -294,7 +296,7 @@
     tiles = fields * count // 8
     pairs = fields * count // 4
     for dim in (1, 2):
-        lower, upper = received(got[dim], *sizes[dim])
+        lower, upper = received(got[dim], pairs if dim == 2 else tiles + -tiles % 8, *sizes[dim])
         if dim == 1:
             halo[...] = jnp.zeros_like(halo)
             for m in range(2):
@@ -314,7 +316,7 @@
             face_high[rows, cols], face_low[rows, cols] = split(fixed[f])
     lift_inner(out, base, face_high, face_low, lift_table)
     middle = (fields + 1) // 2
-    lower, upper = received(got[0], *sizes[0])
+    lower, upper = received(got[0], middle * 8, *sizes[0])
     for end, (low, high) in enumerate((lower, upper)):
         rows = slice(0, 8) if end == 0 else slice(count - 8, count)
         jump = []
@@ -350,8 +352,8 @@
 
 
 def first_kernel(count, fields, sizes, wave, density, lame, shear, cell, flag, orient_code, w_high, w_low, face_table,
-                 q, par, index, hot_par, place, place_back, pack, unpack, *rest):
-    outs, scratch = rest[:-10], rest[-10:]
+                 q, par, index, hot_par, place_back, pack, unpack, *rest):
+    outs, place, scratch = rest[:-11], rest[-11], rest[-10:]
     h0, l0, h1, l1 = scratch[:4]
     half, blocks = count // 2, fields - 1
     iota = lambda shape, axis: lax.broadcasted_iota(jnp.int32, shape, axis)
@@ -514,7 +516,9 @@
         shape((rows, 128), F32),
     ]
     for dim in EXCHANGED:
-        predicted += [shape((edge_rows[dim], 128), F32)] * (1 if sizes[dim][1] == 2 else 2)
+        for parity in range(1 if sizes[dim][1] == 2 else 2):
+            padded = edge_rows[dim] if (dim, parity) == (1, 1) else max(edge_rows.values())
+            predicted.append(shape((padded, 128), F32))
     hot_rows = half * fields
     predict_scratch = [pltpu.VMEM((rows, nodes), BF16)] * 4 + [pltpu.VMEM(field_shape.shape, F32)]
     predict_scratch += [pltpu.VMEM((hot_rows, nodes), BF16)] * 4 + [pltpu.VMEM((hot_rows, nodes), F32)]
@@ -551,7 +555,7 @@
         "split_operators",
         limit=TABLE_LIMIT,
     )
-    q, par, index, hot_par, place, place_back, pack, unpack, *ahead = call(
+    q, par, index, hot_par, place_back, pack, unpack, *ahead = call(
         functools.partial(first_kernel, count, fields, sizes),
         [wave, row(density), row(lame_first), row(shear_modulus), row(element_cell), row(high_order), codes]
         + [w_high, w_low, face_table],
@@ -562,12 +566,11 @@
             shape((3 * count, 128), jnp.int32),
             shape((4 * half, 128), F32),
             shape((blocks * count, blocks * count), BF16),
-            shape((blocks * count, blocks * count), BF16),
             shape((blocks * half, blocks * count), BF16),
             shape((blocks * count, blocks * half), BF16),
         ]
         + predicted,
-        predict_scratch,
+        [pltpu.VMEM((blocks * count, blocks * count), BF16)] + predict_scratch,
         4,
         "first_predictor",
     )

time: 31.9 us -> 28.2 us (0.88)
  starting transfers between devices: 11.5 us -> 9.96 us
  waiting for transfers between devices: 2.3 us -> 0.79 us
  Pallas kernels: 17.7 us -> 17.1 us
    ppermute x10, starting transfers between devices: 11.5 us -> 9.96 us  [exchange(): got.append(lax.ppermute(edges[len(got)], axes, swaps(sizes, dim, parity)))]
    ppermute x10, waiting for transfers between devices: 2.3 us -> 0.79 us  [exchange(): got.append(lax.ppermute(edges[len(got)], axes, swaps(sizes, dim, parity)))]
    pallas_call x6, Pallas kernels: 17.7 us -> 17.1 us  [call(): pl.pallas_call(kernel, out_shape=out_shape, in_specs=in_specs, out_specs=...]
  transfers between devices with their start and end apart: 10 -> 10, of which waited for: 3 -> 2; matrix products, arithmetic and copies ran while one was open for 0% -> 0% of each run, Pallas kernels for 8% -> 9%
where the time goes in v5:
time: 28.2 us; the launch traced here: 28 us
  Pallas kernels  17.1 us (61%)
  starting transfers between devices  9.96 us (35%)
  waiting for transfers between devices  0.79 us (3%)
    pallas_call x6, Pallas kernels, call(): pl.pallas_call(kernel, out_shape=out_shape, in_specs=in_specs, out_specs=...  17.1 us
    ppermute x10, starting transfers between devices, exchange(): got.append(lax.ppermute(edges[len(got)], axes, swaps(sizes, dim, parity)))  9.96 us
    ppermute x10, waiting for transfers between devices, exchange(): got.append(lax.ppermute(edges[len(got)], axes, swaps(sizes, dim, parity)))  0.79 us
  transfers between devices with their start and end apart: 10, of which 2 were waited for; matrix products, arithmetic and copies ran while one was open for 0% of the time, Pallas kernels for 9%

profile of v5, /device:TPU:0, one launch (start us, length us, event | category | flops | bytes accessed | tf_op | source)
XLA Modules:
  0.0 28.0 jit_solution(10365802297465455773)
XLA Ops:
  0.0 0.0 copy-start.1
  0.0 0.0 copy-start.5
  0.0 0.0 copy-start.6
  0.0 0.0 copy-start.4
  0.0 0.0 copy-start.3
  0.0 0.0 copy-start.2
  0.0 0.0 copy-start
  0.0 2.0 %split_operators.1 = (bf16[3,512,512]{2,1,0:T(8,128)(2,1)S(1)}, bf16[3,512,512]{2,1,0:T(8,128)(2,1)S(1)}, bf16[512,256]{1,0:T(8,128)(2,1)S(1)}, bf16[256,512]{1,0:T(8,128)(2,1)S(1)}) custom-call(f32[3,512,512]{2,1,0:T(8,128)} %ops_any.1), custom_call_target="tpu_custom_call" | custom-call | flops 3623878656 | bytes 2359296 | tf_op jit(solution)/shard_map/split_operators/pallas_call | solution.py:530
  2.1 0.0 copy-done.1
  2.1 0.0 copy-done.5
  2.1 0.0 copy-done.6
  2.1 0.0 copy-done.4
  2.1 0.0 copy-done.3
  2.1 0.0 copy-done.2
  2.2 0.0 copy-done
  2.2 5.3 %first_predictor.1 = (f32[4,288,128]{2,1,0:T(8,128)S(1)}, f32[128,128]{1,0:T(8,128)S(1)}, s32[96,128]{1,0:T(8,128)S(1)}, f32[64,128]{1,0:T(8,128)S(1)}, bf16[256...) custom-call(f32[288,512]{1,0:T(8,128)S(1)} %bitcast.16, ...), custom_call_target="tpu_custom_call" | custom-call | flops 7247757312 | bytes 2359296 | tf_op jit(solution)/shard_map/first_predictor/pallas_call | solution.py:530
  7.5 2.5 %collective-permute-start.4 = (f32[40,128]{1,0:T(8,128)S(1)}, f32[40,128]{1,0:T(8,128)S(1)}, u32[]{:S(2)}, u32[]{:S(2)}) collective-permute-start(f32[40,128]{1,0:T(8,128)S(1)} %get-tuple-element.44), channel_id=1, source_target_pairs={{0,6},{1,7},{2,4},{3,5},{4,2},{5,3},{6,0},{7,1},{8,14},{9,15},{10,... | collective-permute-start | bytes 61448 | tf_op jit(solution)/shard_map/ppermute | solution.py:495
  10.0 1.5 %collective-permute-start = (f32[72,128]{1,0:T(8,128)S(1)}, f32[72,128]{1,0:T(8,128)S(1)}, u32[]{:S(2)}, u32[]{:S(2)}) collective-permute-start(f32[72,128]{1,0:T(8,128)S(1)} %get-tuple-element.40), channel_id=1, source_target_pairs={{0,1},{1,0},{2,3},{3,2},{4,5},{5,4},{6,7},{7,6},{8,9},{9,8},{10,11... | collective-permute-start | bytes 110600 | tf_op jit(solution)/shard_map/ppermute | solution.py:495
  11.5 1.6 %collective-permute-start.1 = (f32[72,128]{1,0:T(8,128)S(1)}, f32[72,128]{1,0:T(8,128)S(1)}, u32[]{:S(2)}, u32[]{:S(2)}) collective-permute-start(f32[72,128]{1,0:T(8,128)S(1)} %get-tuple-element.41), channel_id=1, source_target_pairs={{0,8},{1,9},{2,10},{3,11},{4,12},{5,13},{6,14},{7,15},{8,0},{9,1},... | collective-permute-start | bytes 110600 | tf_op jit(solution)/shard_map/ppermute | solution.py:495
  13.1 0.1 collective-permute-start.2
  13.2 0.4 %collective-permute-start.3 = (f32[72,128]{1,0:T(8,128)S(1)}, f32[72,128]{1,0:T(8,128)S(1)}, u32[]{:S(2)}, u32[]{:S(2)}) collective-permute-start(f32[72,128]{1,0:T(8,128)S(1)} %get-tuple-element.43), channel_id=1, source_target_pairs={{0,2},{1,3},{2,0},{3,1},{4,6},{5,7},{6,4},{7,5},{8,10},{9,11},{10,... | collective-permute-start | bytes 110600 | tf_op jit(solution)/shard_map/ppermute | solution.py:495
  13.6 1.3 %inner_update.2.refs_5_ = f32[4,288,128]{2,1,0:T(8,128)S(1)} custom-call(f32[4,288,128]{2,1,0:T(8,128)S(1)} %get-tuple-element.45.refs_0_, bf16[288,512]{1,0:T(8,128)(2,1)S(1)} %get-tuple-element.46.refs_1_, bf16[288,512]{1,0:T(8,128)(2,1)S(1)} %get-tuple-element.47.refs_2_, f32[288,128]{1,0:T(8,128)S(1)} %get-tuple-element.48.refs_3_, ...), custom_call_target="tpu_custom_call" | custom-call | flops 1811939328 | bytes 2359296 | tf_op jit(solution)/shard_map/inner_update/pallas_call | solution.py:530
  14.9 0.0 collective-permute-done.4.refs_4_
  14.9 0.0 collective-permute-done.refs_0_
  14.9 0.6 %collective-permute-done.1.refs_1_ = f32[72,128]{1,0:T(8,128)S(1)} collective-permute-done((f32[72,128]{1,0:T(8,128)S(1)}, f32[72,128]{1,0:T(8,128)S(1)}, u32[]{:S(2)}, u32[]{:S(2)}) %collective-permute-start.1) | collective-permute-done | bytes 36896 | tf_op jit(solution)/shard_map/ppermute | solution.py:495
  15.5 0.0 collective-permute-done.2.refs_2_
  15.5 0.0 collective-permute-done.3.refs_3_
  15.5 5.5 %outer_update_predictor.1 = (f32[4,288,128]{2,1,0:T(8,128)S(1)}, bf16[288,512]{1,0:T(8,128)(2,1)S(1)}, bf16[288,512]{1,0:T(8,128)(2,1)S(1)}, f32[288,128]{1,0:T(...) custom-call(f32[72,128]{1,0:T(8,128)S(1)} %collective-permute-done.r, ...), custom_call_target="tpu_custom_call" | custom-call | flops 7247757312 | bytes 2359296 | tf_op jit(solution)/shard_map/outer_update_predictor/pallas_call | solution.py:530
  21.0 0.1 collective-permute-start.9
  21.1 0.6 %collective-permute-start.5 = (f32[72,128]{1,0:T(8,128)S(1)}, f32[72,128]{1,0:T(8,128)S(1)}, u32[]{:S(2)}, u32[]{:S(2)}) collective-permute-start(f32[72,128]{1,0:T(8,128)S(1)} %get-tuple-element.57), channel_id=1, source_target_pairs={{0,1},{1,0},{2,3},{3,2},{4,5},{5,4},{6,7},{7,6},{8,9},{9,8},{10,11... | collective-permute-start | bytes 110600 | tf_op jit(solution)/shard_map/ppermute | solution.py:495
  21.6 2.7 %collective-permute-start.6 = (f32[72,128]{1,0:T(8,128)S(1)}, f32[72,128]{1,0:T(8,128)S(1)}, u32[]{:S(2)}, u32[]{:S(2)}) collective-permute-start(f32[72,128]{1,0:T(8,128)S(1)} %get-tuple-element.58), channel_id=1, source_target_pairs={{0,8},{1,9},{2,10},{3,11},{4,12},{5,13},{6,14},{7,15},{8,0},{9,1},... | collective-permute-start | bytes 110600 | tf_op jit(solution)/shard_map/ppermute | solution.py:495
  24.4 0.1 collective-permute-start.7
  24.4 0.5 %collective-permute-start.8 = (f32[72,128]{1,0:T(8,128)S(1)}, f32[72,128]{1,0:T(8,128)S(1)}, u32[]{:S(2)}, u32[]{:S(2)}) collective-permute-start(f32[72,128]{1,0:T(8,128)S(1)} %get-tuple-element.60), channel_id=1, source_target_pairs={{0,2},{1,3},{2,0},{3,1},{4,6},{5,7},{6,4},{7,5},{8,10},{9,11},{10,... | collective-permute-start | bytes 110600 | tf_op jit(solution)/shard_map/ppermute | solution.py:495
  24.9 1.2 %inner_update.3.refs_5_ = f32[4,288,128]{2,1,0:T(8,128)S(1)} custom-call(f32[4,288,128]{2,1,0:T(8,128)S(1)} %get-tuple-element.62.refs_0_, bf16[288,512]{1,0:T(8,128)(2,1)S(1)} %get-tuple-element.63.refs_1_, bf16[288,512]{1,0:T(8,128)(2,1)S(1)} %get-tuple-element.64.refs_2_, f32[288,128]{1,0:T(8,128)S(1)} %get-tuple-element.65.refs_3_, ...), custom_call_target="tpu_custom_call" | custom-call | flops 1811939328 | bytes 2359296 | tf_op jit(solution)/shard_map/inner_update/pallas_call | solution.py:530
  26.1 0.0 collective-permute-done.9.refs_4_
  26.1 0.0 collective-permute-done.5.refs_0_
  26.2 0.2 collective-permute-done.6.refs_1_
  26.3 0.0 collective-permute-done.7.refs_2_
  26.3 0.0 collective-permute-done.8.refs_3_
  26.3 1.7 %outer_update.1 = f32[288,512]{1,0:T(8,128)} custom-call(f32[72,128]{1,0:T(8,128)S(1)} %collective-permute-done.5.refs_0_, f32[72,128]{1,0:T(8,128)S(1)} %collective-permute-done.6.refs_1_, f32[72,128]{1,0:T(8,128)S(1)} %collective-permute-done.7.refs_2_, f32[72,128]{1,0:T(8,128)S(1)} %collective-permute-done.8.refs_3_, ...), custom_call_target="tpu_custom_call" | custom-call | flops 1811939328 | bytes 2359296 | tf_op jit(solution)/shard_map/outer_update/pallas_call | solution.py:530
Async XLA Ops:
  0.0 2.1 %copy-start.1 = (s32[1,1,1,6,32]{4,2,3,1,0:T(1,128)S(1)}, s32[1,1,1,6,32]{4,2,3,1,0:T(1,128)}, u32[]{:S(2)}) copy-start(s32[1,1,1,6,32]{4,2,3,1,0:T(1,128)} %param.15) | copy-start | bytes 2308
  0.0 2.1 %copy-start.5 = (s32[1,1,1,32]{3,2,1,0:T(1,128)S(1)}, s32[1,1,1,32]{3,2,1,0:T(1,128)}, u32[]{:S(2)}) copy-start(s32[1,1,1,32]{3,2,1,0:T(1,128)} %param.14) | copy-start | bytes 388
  0.0 2.1 %copy-start.6 = (s32[1,1,1,32]{3,2,1,0:T(1,128)S(1)}, s32[1,1,1,32]{3,2,1,0:T(1,128)}, u32[]{:S(2)}) copy-start(s32[1,1,1,32]{3,2,1,0:T(1,128)} %param.13) | copy-start | bytes 388
  0.0 2.1 %copy-start.4 = (f32[1,1,1,32]{3,2,1,0:T(1,128)S(1)}, f32[1,1,1,32]{3,2,1,0:T(1,128)}, u32[]{:S(2)}) copy-start(f32[1,1,1,32]{3,2,1,0:T(1,128)} %param.12) | copy-start | bytes 388
  0.0 2.1 %copy-start.3 = (f32[1,1,1,32]{3,2,1,0:T(1,128)S(1)}, f32[1,1,1,32]{3,2,1,0:T(1,128)}, u32[]{:S(2)}) copy-start(f32[1,1,1,32]{3,2,1,0:T(1,128)} %param.11) | copy-start | bytes 388
  0.0 2.1 %copy-start.2 = (f32[1,1,1,32]{3,2,1,0:T(1,128)S(1)}, f32[1,1,1,32]{3,2,1,0:T(1,128)}, u32[]{:S(2)}) copy-start(f32[1,1,1,32]{3,2,1,0:T(1,128)} %param.10) | copy-start | bytes 388
  0.0 2.1 %copy-start = (f32[1,1,1,32,9,512]{5,3,4,2,1,0:T(8,128)S(1)}, f32[1,1,1,32,9,512]{5,3,4,2,1,0:T(8,128)}, u32[]{:S(2)}) copy-start(f32[1,1,1,32,9,512]{5,3,4,2,1,0:T(8,128)} %param.8) | copy-start | bytes 1769476
  7.5 7.4 %collective-permute-start.4 = (f32[40,128]{1,0:T(8,128)S(1)}, f32[40,128]{1,0:T(8,128)S(1)}, u32[]{:S(2)}, u32[]{:S(2)}) collective-permute-start(f32[40,128]{1,0:T(8,128)S(1)} %get-tuple-element.44), channel_id=1, source_target_pairs={{0,6},{1,7},{2,4},{3,5},{4,2},{5,3},{6,0},{7,1},{8,14},{9,15},{10,... | collective-permute-start | bytes 61448 | tf_op jit(solution)/shard_map/ppermute | solution.py:495
  10.0 4.9 %collective-permute-start = (f32[72,128]{1,0:T(8,128)S(1)}, f32[72,128]{1,0:T(8,128)S(1)}, u32[]{:S(2)}, u32[]{:S(2)}) collective-permute-start(f32[72,128]{1,0:T(8,128)S(1)} %get-tuple-element.40), channel_id=1, source_target_pairs={{0,1},{1,0},{2,3},{3,2},{4,5},{5,4},{6,7},{7,6},{8,9},{9,8},{10,11... | collective-permute-start | bytes 110600 | tf_op jit(solution)/shard_map/ppermute | solution.py:495
  11.5 4.0 %collective-permute-start.1 = (f32[72,128]{1,0:T(8,128)S(1)}, f32[72,128]{1,0:T(8,128)S(1)}, u32[]{:S(2)}, u32[]{:S(2)}) collective-permute-start(f32[72,128]{1,0:T(8,128)S(1)} %get-tuple-element.41), channel_id=1, source_target_pairs={{0,8},{1,9},{2,10},{3,11},{4,12},{5,13},{6,14},{7,15},{8,0},{9,1},... | collective-permute-start | bytes 110600 | tf_op jit(solution)/shard_map/ppermute | solution.py:495
  13.1 2.4 %collective-permute-start.2 = (f32[72,128]{1,0:T(8,128)S(1)}, f32[72,128]{1,0:T(8,128)S(1)}, u32[]{:S(2)}, u32[]{:S(2)}) collective-permute-start(f32[72,128]{1,0:T(8,128)S(1)} %get-tuple-element.42), channel_id=1, source_target_pairs={{0,2},{1,3},{2,0},{3,1},{4,6},{5,7},{6,4},{7,5},{8,16},{9,17},{10,... | collective-permute-start | bytes 110600 | tf_op jit(solution)/shard_map/ppermute | solution.py:495
  13.2 2.3 %collective-permute-start.3 = (f32[72,128]{1,0:T(8,128)S(1)}, f32[72,128]{1,0:T(8,128)S(1)}, u32[]{:S(2)}, u32[]{:S(2)}) collective-permute-start(f32[72,128]{1,0:T(8,128)S(1)} %get-tuple-element.43), channel_id=1, source_target_pairs={{0,2},{1,3},{2,0},{3,1},{4,6},{5,7},{6,4},{7,5},{8,10},{9,11},{10,... | collective-permute-start | bytes 110600 | tf_op jit(solution)/shard_map/ppermute | solution.py:495
  21.0 5.1 %collective-permute-start.9 = (f32[40,128]{1,0:T(8,128)S(1)}, f32[40,128]{1,0:T(8,128)S(1)}, u32[]{:S(2)}, u32[]{:S(2)}) collective-permute-start(f32[40,128]{1,0:T(8,128)S(1)} %get-tuple-element.61), channel_id=1, source_target_pairs={{0,6},{1,7},{2,4},{3,5},{4,2},{5,3},{6,0},{7,1},{8,14},{9,15},{10,... | collective-permute-start | bytes 61448 | tf_op jit(solution)/shard_map/ppermute | solution.py:495
  21.1 5.1 %collective-permute-start.5 = (f32[72,128]{1,0:T(8,128)S(1)}, f32[72,128]{1,0:T(8,128)S(1)}, u32[]{:S(2)}, u32[]{:S(2)}) collective-permute-start(f32[72,128]{1,0:T(8,128)S(1)} %get-tuple-element.57), channel_id=1, source_target_pairs={{0,1},{1,0},{2,3},{3,2},{4,5},{5,4},{6,7},{7,6},{8,9},{9,8},{10,11... | collective-permute-start | bytes 110600 | tf_op jit(solution)/shard_map/ppermute | solution.py:495
  21.6 4.7 %collective-permute-start.6 = (f32[72,128]{1,0:T(8,128)S(1)}, f32[72,128]{1,0:T(8,128)S(1)}, u32[]{:S(2)}, u32[]{:S(2)}) collective-permute-start(f32[72,128]{1,0:T(8,128)S(1)} %get-tuple-element.58), channel_id=1, source_target_pairs={{0,8},{1,9},{2,10},{3,11},{4,12},{5,13},{6,14},{7,15},{8,0},{9,1},... | collective-permute-start | bytes 110600 | tf_op jit(solution)/shard_map/ppermute | solution.py:495
  24.4 2.0 %collective-permute-start.7 = (f32[72,128]{1,0:T(8,128)S(1)}, f32[72,128]{1,0:T(8,128)S(1)}, u32[]{:S(2)}, u32[]{:S(2)}) collective-permute-start(f32[72,128]{1,0:T(8,128)S(1)} %get-tuple-element.59), channel_id=1, source_target_pairs={{0,2},{1,3},{2,0},{3,1},{4,6},{5,7},{6,4},{7,5},{8,16},{9,17},{10,... | collective-permute-start | bytes 110600 | tf_op jit(solution)/shard_map/ppermute | solution.py:495
  24.4 1.9 %collective-permute-start.8 = (f32[72,128]{1,0:T(8,128)S(1)}, f32[72,128]{1,0:T(8,128)S(1)}, u32[]{:S(2)}, u32[]{:S(2)}) collective-permute-start(f32[72,128]{1,0:T(8,128)S(1)} %get-tuple-element.60), channel_id=1, source_target_pairs={{0,2},{1,3},{2,0},{3,1},{4,6},{5,7},{6,4},{7,5},{8,10},{9,11},{10,... | collective-permute-start | bytes 110600 | tf_op jit(solution)/shard_map/ppermute | solution.py:495

commit v6 on v5

--- a/solution.py
+++ b/solution.py
@@ -12,7 +12,7 @@
 STEPS = 2
 DT = 0.8
 LIFT = 2.0
-EXCHANGED = (2, 0, 1)
+ORDER = ((1, 1), (2, 0), (2, 1), (0, 0), (0, 1), (1, 0))
 PICKED = ((0, 1, 2, 3, 6, 8), (0, 1, 2, 6, 4, 7), (0, 1, 2, 8, 7, 5))
 F32 = jnp.float32
 BF16 = jnp.bfloat16
@@ -138,6 +138,10 @@
         put(target, slice(0, rows), cols, get(source, slice(0, rows), cols) + DT * LIFT * lifted)
 
 
+def exchanges(sizes):
+    return [(dim, parity) for dim, parity in ORDER if parity == 0 or sizes[dim][1] > 2]
+
+
 def fetch(copies):
     started = [pltpu.make_async_copy(*copy) for copy in copies]
     for copy in started:
@@ -151,6 +155,8 @@
     minus_face = jnp.where(minus, low, pltpu.roll(high, 64, 1))
     rows = low.shape[0]
     for parity, target in enumerate(targets):
+        if target is None:
+            continue
         target[0:rows] = jnp.where(up, plus_face, minus_face) if parity == 0 else jnp.where(up, minus_face, plus_face)
         if target.shape[0] > rows:
             target[rows:] = jnp.zeros((target.shape[0] - rows, 128), F32)
@@ -223,11 +229,9 @@
     faces = dot(int_high[...], face_table[...]) + dot(int_low[...], face_table[...])
     trace_y[...] = faces[:, 0:128]
     trace_z[...] = faces[:, 128:256]
-    targets, at = {}, 0
-    for dim in EXCHANGED:
-        number = 1 if sizes[dim][1] == 2 else 2
-        targets[dim] = edges[at : at + number]
-        at += number
+    targets = [[None, None] for _ in sizes]
+    for (dim, parity), edge in zip(exchanges(sizes), edges):
+        targets[dim][parity] = edge
     ups = [lax.axis_index(axis) % 2 == 0 for axis, _ in sizes]
     ends = []
     for f in range(fields):
@@ -330,7 +334,7 @@
 
 def table_kernel(ops_any, w_high, w_low, face_table, lift_table, ops, sems):
     dims, nodes = ops.shape[:2]
-    step = nodes // 2
+    step = nodes // 4
     parts = [(dim, slice(start, start + step)) for dim in range(dims) for start in range(0, nodes, step)]
     waits = fetch([(ops_any.at[dim, rows], ops.at[dim, rows], sems.at[k]) for k, (dim, rows) in enumerate(parts)])
 
@@ -433,12 +437,11 @@
 
 
 def unpack_got(sizes, refs):
-    got, at = [[None, None] for _ in sizes], 0
-    for dim in EXCHANGED:
-        for k in range(1 if sizes[dim][1] == 2 else 2):
-            got[dim][k] = refs[at]
-            at += 1
-    return got, refs[at:]
+    got = [[None, None] for _ in sizes]
+    places = exchanges(sizes)
+    for (dim, parity), ref in zip(places, refs):
+        got[dim][parity] = ref
+    return got, refs[len(places) :]
 
 
 def middle_kernel(count, fields, sizes, *refs):
@@ -489,11 +492,7 @@
 
 def exchange(edges, sizes):
     axes = tuple(axis for axis, _ in sizes)
-    got = []
-    for dim in EXCHANGED:
-        for parity in range(1 if sizes[dim][1] == 2 else 2):
-            got.append(lax.ppermute(edges[len(got)], axes, swaps(sizes, dim, parity)))
-    return got
+    return [lax.ppermute(edge, axes, swaps(sizes, *place)) for edge, place in zip(edges, exchanges(sizes))]
 
 
 def shards(sizes, wavefield, deriv_ops, density, lame_first, shear_modulus, high_order, element_cell, face_orient):
@@ -515,10 +514,9 @@
         shape((rows, 128), F32),
         shape((rows, 128), F32),
     ]
-    for dim in EXCHANGED:
-        for parity in range(1 if sizes[dim][1] == 2 else 2):
-            padded = edge_rows[dim] if (dim, parity) == (1, 1) else max(edge_rows.values())
-            predicted.append(shape((padded, 128), F32))
+    for place in exchanges(sizes):
+        padded = edge_rows[place[0]] if place == ORDER[0] else max(edge_rows.values())
+        predicted.append(shape((padded, 128), F32))
     hot_rows = half * fields
     predict_scratch = [pltpu.VMEM((rows, nodes), BF16)] * 4 + [pltpu.VMEM(field_shape.shape, F32)]
     predict_scratch += [pltpu.VMEM((hot_rows, nodes), BF16)] * 4 + [pltpu.VMEM((hot_rows, nodes), F32)]
@@ -550,7 +548,7 @@
             shape((nodes, 256), BF16),
             shape((256, nodes), BF16),
         ],
-        [pltpu.VMEM(deriv_ops.shape, F32), pltpu.SemaphoreType.DMA((2 * deriv_ops.shape[0],))],
+        [pltpu.VMEM(deriv_ops.shape, F32), pltpu.SemaphoreType.DMA((4 * deriv_ops.shape[0],))],
         2,
         "split_operators",
         limit=TABLE_LIMIT,

time: 28.2 us -> 28.2 us (level)
  no operation moved by 1% of the time
where the time goes in v6:
time: 28.2 us; the launch traced here: 28 us
  Pallas kernels  17.1 us (61%)
  starting transfers between devices  9.92 us (35%)
  waiting for transfers between devices  0.82 us (3%)
    pallas_call x6, Pallas kernels, call(): pl.pallas_call(kernel, out_shape=out_shape, in_specs=in_specs, out_specs=...  17.1 us
    ppermute x10, starting transfers between devices, exchange(): lax.ppermute(edge, axes, swaps(sizes, *place))  9.92 us
    ppermute x10, waiting for transfers between devices, exchange(): lax.ppermute(edge, axes, swaps(sizes, *place))  0.82 us
  transfers between devices with their start and end apart: 10, of which 2 were waited for; matrix products, arithmetic and copies ran while one was open for 0% of the time, Pallas kernels for 9%

profile of v6, /device:TPU:0, one launch (start us, length us, event | category | flops | bytes accessed | tf_op | source)
XLA Modules:
  0.0 28.0 jit_solution(6271956428868303372)
XLA Ops:
  0.0 0.0 copy-start.1
  0.0 0.0 copy-start.5
  0.0 0.0 copy-start.6
  0.0 0.0 copy-start.4
  0.0 0.0 copy-start.3
  0.0 0.0 copy-start.2
  0.0 0.0 copy-start
  0.0 2.0 %split_operators.1 = (bf16[3,512,512]{2,1,0:T(8,128)(2,1)S(1)}, bf16[3,512,512]{2,1,0:T(8,128)(2,1)S(1)}, bf16[512,256]{1,0:T(8,128)(2,1)S(1)}, bf16[256,512]{1,0:T(8,128)(2,1)S(1)}) custom-call(f32[3,512,512]{2,1,0:T(8,128)} %ops_any.1), custom_call_target="tpu_custom_call" | custom-call | flops 3623878656 | bytes 2359296 | tf_op jit(solution)/shard_map/split_operators/pallas_call | solution.py:528
  2.1 0.0 copy-done.1
  2.1 0.0 copy-done.5
  2.1 0.0 copy-done.6
  2.1 0.0 copy-done.4
  2.1 0.0 copy-done.3
  2.1 0.0 copy-done.2
  2.1 0.0 copy-done
  2.1 5.3 %first_predictor.1 = (f32[4,288,128]{2,1,0:T(8,128)S(1)}, f32[128,128]{1,0:T(8,128)S(1)}, s32[96,128]{1,0:T(8,128)S(1)}, f32[64,128]{1,0:T(8,128)S(1)}, bf16[256...) custom-call(f32[288,512]{1,0:T(8,128)S(1)} %bitcast.16, ...), custom_call_target="tpu_custom_call" | custom-call | flops 7247757312 | bytes 2359296 | tf_op jit(solution)/shard_map/first_predictor/pallas_call | solution.py:528
  7.5 2.4 %collective-permute-start = (f32[40,128]{1,0:T(8,128)S(1)}, f32[40,128]{1,0:T(8,128)S(1)}, u32[]{:S(2)}, u32[]{:S(2)}) collective-permute-start(f32[40,128]{1,0:T(8,128)S(1)} %get-tuple-element.40), channel_id=1, source_target_pairs={{0,6},{1,7},{2,4},{3,5},{4,2},{5,3},{6,0},{7,1},{8,14},{9,15},{10,... | collective-permute-start | bytes 61448 | tf_op jit(solution)/shard_map/ppermute | solution.py:495
  9.9 1.5 %collective-permute-start.1 = (f32[72,128]{1,0:T(8,128)S(1)}, f32[72,128]{1,0:T(8,128)S(1)}, u32[]{:S(2)}, u32[]{:S(2)}) collective-permute-start(f32[72,128]{1,0:T(8,128)S(1)} %get-tuple-element.41), channel_id=1, source_target_pairs={{0,1},{1,0},{2,3},{3,2},{4,5},{5,4},{6,7},{7,6},{8,9},{9,8},{10,11... | collective-permute-start | bytes 110600 | tf_op jit(solution)/shard_map/ppermute | solution.py:495
  11.5 1.6 %collective-permute-start.2 = (f32[72,128]{1,0:T(8,128)S(1)}, f32[72,128]{1,0:T(8,128)S(1)}, u32[]{:S(2)}, u32[]{:S(2)}) collective-permute-start(f32[72,128]{1,0:T(8,128)S(1)} %get-tuple-element.42), channel_id=1, source_target_pairs={{0,8},{1,9},{2,10},{3,11},{4,12},{5,13},{6,14},{7,15},{8,0},{9,1},... | collective-permute-start | bytes 110600 | tf_op jit(solution)/shard_map/ppermute | solution.py:495
  13.0 0.1 collective-permute-start.3
  13.2 0.4 %collective-permute-start.4 = (f32[72,128]{1,0:T(8,128)S(1)}, f32[72,128]{1,0:T(8,128)S(1)}, u32[]{:S(2)}, u32[]{:S(2)}) collective-permute-start(f32[72,128]{1,0:T(8,128)S(1)} %get-tuple-element.44), channel_id=1, source_target_pairs={{0,2},{1,3},{2,0},{3,1},{4,6},{5,7},{6,4},{7,5},{8,10},{9,11},{10,... | collective-permute-start | bytes 110600 | tf_op jit(solution)/shard_map/ppermute | solution.py:495
  13.5 1.3 %inner_update.2.refs_5_ = f32[4,288,128]{2,1,0:T(8,128)S(1)} custom-call(f32[4,288,128]{2,1,0:T(8,128)S(1)} %get-tuple-element.45.refs_0_, bf16[288,512]{1,0:T(8,128)(2,1)S(1)} %get-tuple-element.46.refs_1_, bf16[288,512]{1,0:T(8,128)(2,1)S(1)} %get-tuple-element.47.refs_2_, f32[288,128]{1,0:T(8,128)S(1)} %get-tuple-element.48.refs_3_, ...), custom_call_target="tpu_custom_call" | custom-call | flops 1811939328 | bytes 2359296 | tf_op jit(solution)/shard_map/inner_update/pallas_call | solution.py:528
  14.8 0.0 collective-permute-done.refs_0_
  14.8 0.0 collective-permute-done.1.refs_1_
  14.8 0.6 %collective-permute-done.2.refs_2_ = f32[72,128]{1,0:T(8,128)S(1)} collective-permute-done((f32[72,128]{1,0:T(8,128)S(1)}, f32[72,128]{1,0:T(8,128)S(1)}, u32[]{:S(2)}, u32[]{:S(2)}) %collective-permute-start.2) | collective-permute-done | bytes 36896 | tf_op jit(solution)/shard_map/ppermute | solution.py:495
  15.5 0.0 collective-permute-done.3.refs_3_
  15.5 0.0 collective-permute-done.4.refs_4_
  15.5 5.5 %outer_update_predictor.1 = (f32[4,288,128]{2,1,0:T(8,128)S(1)}, bf16[288,512]{1,0:T(8,128)(2,1)S(1)}, bf16[288,512]{1,0:T(8,128)(2,1)S(1)}, f32[288,128]{1,0:T(...) custom-call(f32[40,128]{1,0:T(8,128)S(1)} %collective-permute-done.r, ...), custom_call_target="tpu_custom_call" | custom-call | flops 7247757312 | bytes 2359296 | tf_op jit(solution)/shard_map/outer_update_predictor/pallas_call | solution.py:528
  21.0 0.1 collective-permute-start.5
  21.0 0.5 %collective-permute-start.6 = (f32[72,128]{1,0:T(8,128)S(1)}, f32[72,128]{1,0:T(8,128)S(1)}, u32[]{:S(2)}, u32[]{:S(2)}) collective-permute-start(f32[72,128]{1,0:T(8,128)S(1)} %get-tuple-element.58), channel_id=1, source_target_pairs={{0,1},{1,0},{2,3},{3,2},{4,5},{5,4},{6,7},{7,6},{8,9},{9,8},{10,11... | collective-permute-start | bytes 110600 | tf_op jit(solution)/shard_map/ppermute | solution.py:495
  21.6 2.8 %collective-permute-start.7 = (f32[72,128]{1,0:T(8,128)S(1)}, f32[72,128]{1,0:T(8,128)S(1)}, u32[]{:S(2)}, u32[]{:S(2)}) collective-permute-start(f32[72,128]{1,0:T(8,128)S(1)} %get-tuple-element.59), channel_id=1, source_target_pairs={{0,8},{1,9},{2,10},{3,11},{4,12},{5,13},{6,14},{7,15},{8,0},{9,1},... | collective-permute-start | bytes 110600 | tf_op jit(solution)/shard_map/ppermute | solution.py:495
  24.3 0.1 collective-permute-start.8
  24.4 0.5 %collective-permute-start.9 = (f32[72,128]{1,0:T(8,128)S(1)}, f32[72,128]{1,0:T(8,128)S(1)}, u32[]{:S(2)}, u32[]{:S(2)}) collective-permute-start(f32[72,128]{1,0:T(8,128)S(1)} %get-tuple-element.61), channel_id=1, source_target_pairs={{0,2},{1,3},{2,0},{3,1},{4,6},{5,7},{6,4},{7,5},{8,10},{9,11},{10,... | collective-permute-start | bytes 110600 | tf_op jit(solution)/shard_map/ppermute | solution.py:495
  24.9 1.3 %inner_update.3.refs_5_ = f32[4,288,128]{2,1,0:T(8,128)S(1)} custom-call(f32[4,288,128]{2,1,0:T(8,128)S(1)} %get-tuple-element.62.refs_0_, bf16[288,512]{1,0:T(8,128)(2,1)S(1)} %get-tuple-element.63.refs_1_, bf16[288,512]{1,0:T(8,128)(2,1)S(1)} %get-tuple-element.64.refs_2_, f32[288,128]{1,0:T(8,128)S(1)} %get-tuple-element.65.refs_3_, ...), custom_call_target="tpu_custom_call" | custom-call | flops 1811939328 | bytes 2359296 | tf_op jit(solution)/shard_map/inner_update/pallas_call | solution.py:528
  26.1 0.0 collective-permute-done.5.refs_0_
  26.1 0.0 collective-permute-done.6.refs_1_
  26.1 0.2 collective-permute-done.7.refs_2_
  26.3 0.0 collective-permute-done.8.refs_3_
  26.3 0.0 collective-permute-done.9.refs_4_
  26.3 1.7 %outer_update.1 = f32[288,512]{1,0:T(8,128)} custom-call(f32[40,128]{1,0:T(8,128)S(1)} %collective-permute-done.5.refs_0_, f32[72,128]{1,0:T(8,128)S(1)} %collective-permute-done.6.refs_1_, f32[72,128]{1,0:T(8,128)S(1)} %collective-permute-done.7.refs_2_, f32[72,128]{1,0:T(8,128)S(1)} %collective-permute-done.8.refs_3_, ...), custom_call_target="tpu_custom_call" | custom-call | flops 1811939328 | bytes 2359296 | tf_op jit(solution)/shard_map/outer_update/pallas_call | solution.py:528
Async XLA Ops:
  0.0 2.1 %copy-start.1 = (s32[1,1,1,6,32]{4,2,3,1,0:T(1,128)S(1)}, s32[1,1,1,6,32]{4,2,3,1,0:T(1,128)}, u32[]{:S(2)}) copy-start(s32[1,1,1,6,32]{4,2,3,1,0:T(1,128)} %param.15) | copy-start | bytes 2308
  0.0 2.1 %copy-start.5 = (s32[1,1,1,32]{3,2,1,0:T(1,128)S(1)}, s32[1,1,1,32]{3,2,1,0:T(1,128)}, u32[]{:S(2)}) copy-start(s32[1,1,1,32]{3,2,1,0:T(1,128)} %param.14) | copy-start | bytes 388
  0.0 2.1 %copy-start.6 = (s32[1,1,1,32]{3,2,1,0:T(1,128)S(1)}, s32[1,1,1,32]{3,2,1,0:T(1,128)}, u32[]{:S(2)}) copy-start(s32[1,1,1,32]{3,2,1,0:T(1,128)} %param.13) | copy-start | bytes 388
  0.0 2.1 %copy-start.4 = (f32[1,1,1,32]{3,2,1,0:T(1,128)S(1)}, f32[1,1,1,32]{3,2,1,0:T(1,128)}, u32[]{:S(2)}) copy-start(f32[1,1,1,32]{3,2,1,0:T(1,128)} %param.12) | copy-start | bytes 388
  0.0 2.1 %copy-start.3 = (f32[1,1,1,32]{3,2,1,0:T(1,128)S(1)}, f32[1,1,1,32]{3,2,1,0:T(1,128)}, u32[]{:S(2)}) copy-start(f32[1,1,1,32]{3,2,1,0:T(1,128)} %param.11) | copy-start | bytes 388
  0.0 2.1 %copy-start.2 = (f32[1,1,1,32]{3,2,1,0:T(1,128)S(1)}, f32[1,1,1,32]{3,2,1,0:T(1,128)}, u32[]{:S(2)}) copy-start(f32[1,1,1,32]{3,2,1,0:T(1,128)} %param.10) | copy-start | bytes 388
  0.0 2.1 %copy-start = (f32[1,1,1,32,9,512]{5,3,4,2,1,0:T(8,128)S(1)}, f32[1,1,1,32,9,512]{5,3,4,2,1,0:T(8,128)}, u32[]{:S(2)}) copy-start(f32[1,1,1,32,9,512]{5,3,4,2,1,0:T(8,128)} %param.8) | copy-start | bytes 1769476
  7.5 7.3 %collective-permute-start = (f32[40,128]{1,0:T(8,128)S(1)}, f32[40,128]{1,0:T(8,128)S(1)}, u32[]{:S(2)}, u32[]{:S(2)}) collective-permute-start(f32[40,128]{1,0:T(8,128)S(1)} %get-tuple-element.40), channel_id=1, source_target_pairs={{0,6},{1,7},{2,4},{3,5},{4,2},{5,3},{6,0},{7,1},{8,14},{9,15},{10,... | collective-permute-start | bytes 61448 | tf_op jit(solution)/shard_map/ppermute | solution.py:495
  9.9 4.9 %collective-permute-start.1 = (f32[72,128]{1,0:T(8,128)S(1)}, f32[72,128]{1,0:T(8,128)S(1)}, u32[]{:S(2)}, u32[]{:S(2)}) collective-permute-start(f32[72,128]{1,0:T(8,128)S(1)} %get-tuple-element.41), channel_id=1, source_target_pairs={{0,1},{1,0},{2,3},{3,2},{4,5},{5,4},{6,7},{7,6},{8,9},{9,8},{10,11... | collective-permute-start | bytes 110600 | tf_op jit(solution)/shard_map/ppermute | solution.py:495
  11.5 4.0 %collective-permute-start.2 = (f32[72,128]{1,0:T(8,128)S(1)}, f32[72,128]{1,0:T(8,128)S(1)}, u32[]{:S(2)}, u32[]{:S(2)}) collective-permute-start(f32[72,128]{1,0:T(8,128)S(1)} %get-tuple-element.42), channel_id=1, source_target_pairs={{0,8},{1,9},{2,10},{3,11},{4,12},{5,13},{6,14},{7,15},{8,0},{9,1},... | collective-permute-start | bytes 110600 | tf_op jit(solution)/shard_map/ppermute | solution.py:495
  13.0 2.4 %collective-permute-start.3 = (f32[72,128]{1,0:T(8,128)S(1)}, f32[72,128]{1,0:T(8,128)S(1)}, u32[]{:S(2)}, u32[]{:S(2)}) collective-permute-start(f32[72,128]{1,0:T(8,128)S(1)} %get-tuple-element.43), channel_id=1, source_target_pairs={{0,2},{1,3},{2,0},{3,1},{4,6},{5,7},{6,4},{7,5},{8,16},{9,17},{10,... | collective-permute-start | bytes 110600 | tf_op jit(solution)/shard_map/ppermute | solution.py:495
  13.2 2.3 %collective-permute-start.4 = (f32[72,128]{1,0:T(8,128)S(1)}, f32[72,128]{1,0:T(8,128)S(1)}, u32[]{:S(2)}, u32[]{:S(2)}) collective-permute-start(f32[72,128]{1,0:T(8,128)S(1)} %get-tuple-element.44), channel_id=1, source_target_pairs={{0,2},{1,3},{2,0},{3,1},{4,6},{5,7},{6,4},{7,5},{8,10},{9,11},{10,... | collective-permute-start | bytes 110600 | tf_op jit(solution)/shard_map/ppermute | solution.py:495
  21.0 5.1 %collective-permute-start.5 = (f32[40,128]{1,0:T(8,128)S(1)}, f32[40,128]{1,0:T(8,128)S(1)}, u32[]{:S(2)}, u32[]{:S(2)}) collective-permute-start(f32[40,128]{1,0:T(8,128)S(1)} %get-tuple-element.57), channel_id=1, source_target_pairs={{0,6},{1,7},{2,4},{3,5},{4,2},{5,3},{6,0},{7,1},{8,14},{9,15},{10,... | collective-permute-start | bytes 61448 | tf_op jit(solution)/shard_map/ppermute | solution.py:495
  21.0 5.1 %collective-permute-start.6 = (f32[72,128]{1,0:T(8,128)S(1)}, f32[72,128]{1,0:T(8,128)S(1)}, u32[]{:S(2)}, u32[]{:S(2)}) collective-permute-start(f32[72,128]{1,0:T(8,128)S(1)} %get-tuple-element.58), channel_id=1, source_target_pairs={{0,1},{1,0},{2,3},{3,2},{4,5},{5,4},{6,7},{7,6},{8,9},{9,8},{10,11... | collective-permute-start | bytes 110600 | tf_op jit(solution)/shard_map/ppermute | solution.py:495
  21.6 4.7 %collective-permute-start.7 = (f32[72,128]{1,0:T(8,128)S(1)}, f32[72,128]{1,0:T(8,128)S(1)}, u32[]{:S(2)}, u32[]{:S(2)}) collective-permute-start(f32[72,128]{1,0:T(8,128)S(1)} %get-tuple-element.59), channel_id=1, source_target_pairs={{0,8},{1,9},{2,10},{3,11},{4,12},{5,13},{6,14},{7,15},{8,0},{9,1},... | collective-permute-start | bytes 110600 | tf_op jit(solution)/shard_map/ppermute | solution.py:495
  24.3 2.0 %collective-permute-start.8 = (f32[72,128]{1,0:T(8,128)S(1)}, f32[72,128]{1,0:T(8,128)S(1)}, u32[]{:S(2)}, u32[]{:S(2)}) collective-permute-start(f32[72,128]{1,0:T(8,128)S(1)} %get-tuple-element.60), channel_id=1, source_target_pairs={{0,2},{1,3},{2,0},{3,1},{4,6},{5,7},{6,4},{7,5},{8,16},{9,17},{10,... | collective-permute-start | bytes 110600 | tf_op jit(solution)/shard_map/ppermute | solution.py:495
  24.4 1.9 %collective-permute-start.9 = (f32[72,128]{1,0:T(8,128)S(1)}, f32[72,128]{1,0:T(8,128)S(1)}, u32[]{:S(2)}, u32[]{:S(2)}) collective-permute-start(f32[72,128]{1,0:T(8,128)S(1)} %get-tuple-element.61), channel_id=1, source_target_pairs={{0,2},{1,3},{2,0},{3,1},{4,6},{5,7},{6,4},{7,5},{8,10},{9,11},{10,... | collective-permute-start | bytes 110600 | tf_op jit(solution)/shard_map/ppermute | solution.py:495

commit v7 on v6

--- a/solution.py
+++ b/solution.py
@@ -227,7 +227,10 @@
         int_high[rows], int_low[rows] = split(get(total, rows, slice(0, nodes)))
         trace_x[rows] = jnp.where(lanes_of(count) < 64, total[0, rows], total[total.shape[0] - 1, rows])
     faces = dot(int_high[...], face_table[...]) + dot(int_low[...], face_table[...])
-    trace_y[...] = faces[:, 0:128]
+    whole = fields * count
+    trace_y[0:whole] = faces[:, 0:128]
+    if trace_y.shape[0] > whole:
+        trace_y[whole:] = jnp.zeros((trace_y.shape[0] - whole, 128), F32)
     trace_z[...] = faces[:, 128:256]
     targets = [[None, None] for _ in sizes]
     for (dim, parity), edge in zip(exchanges(sizes), edges):
@@ -240,13 +243,12 @@
     middle = (fields + 1) // 2
     ends.append(ends[-1])
     send(jnp.concatenate(ends[:middle]), jnp.concatenate(ends[middle : 2 * middle]), ups[0], targets[0])
-    tiles = fields * count // 8
-    pad = -tiles % 8
+    tiles = trace_y.shape[0] // 8
     minus = lanes_of(tiles) < 64
-    ends = []
-    for m in range(2):
-        value = jnp.where(minus, trace_y[pl.ds(m, tiles, stride=8), :], trace_y[pl.ds(6 + m, tiles, stride=8), :])
-        ends.append(jnp.concatenate([value, jnp.zeros((pad, 128), F32)]) if pad else value)
+    ends = [
+        jnp.where(minus, trace_y[pl.ds(m, tiles, stride=8), :], trace_y[pl.ds(6 + m, tiles, stride=8), :])
+        for m in range(2)
+    ]
     send(ends[0], ends[1], ups[1], targets[1])
     pairs = fields * count // 4
     minus = lanes_of(pairs) < 64
@@ -297,15 +299,15 @@
 
 
 def outer(count, fields, sizes, got, base, par, index, lift_table, out, halo, face_high, face_low):
-    tiles = fields * count // 8
+    tiles = halo.shape[0] // 8
     pairs = fields * count // 4
     for dim in (1, 2):
-        lower, upper = received(got[dim], pairs if dim == 2 else tiles + -tiles % 8, *sizes[dim])
+        lower, upper = received(got[dim], pairs if dim == 2 else tiles, *sizes[dim])
         if dim == 1:
             halo[...] = jnp.zeros_like(halo)
             for m in range(2):
-                halo[pl.ds(m, tiles, stride=8), :] = lower[m][0:tiles]
-                halo[pl.ds(6 + m, tiles, stride=8), :] = upper[m][0:tiles]
+                halo[pl.ds(m, tiles, stride=8), :] = lower[m]
+                halo[pl.ds(6 + m, tiles, stride=8), :] = upper[m]
         else:
             for part in range(2):
                 halo[pl.ds(2 * part * pairs, pairs, stride=2), :] = lower[part]
@@ -511,7 +513,7 @@
         shape((rows, nodes), BF16),
         shape((rows, nodes), BF16),
         shape((rows, 128), F32),
-        shape((rows, 128), F32),
+        shape((edge_rows[1] * 8, 128), F32),
         shape((rows, 128), F32),
     ]
     for place in exchanges(sizes):
@@ -521,7 +523,7 @@
     predict_scratch = [pltpu.VMEM((rows, nodes), BF16)] * 4 + [pltpu.VMEM(field_shape.shape, F32)]
     predict_scratch += [pltpu.VMEM((hot_rows, nodes), BF16)] * 4 + [pltpu.VMEM((hot_rows, nodes), F32)]
     face_scratch = [pltpu.VMEM((rows, 256), BF16), pltpu.VMEM((rows, 256), BF16)]
-    halo_scratch = [pltpu.VMEM((rows, 128), F32)] + face_scratch
+    halo_scratch = [pltpu.VMEM((edge_rows[1] * 8, 128), F32)] + face_scratch
 
     def call(kernel, operands, in_specs, out_shape, scratch, products, name, out_spec=vmem, limit=VMEM_LIMIT):
         single = not isinstance(out_shape, list)

time: 28.2 us -> 28.2 us (level)
  no operation moved by 1% of the time
where the time goes in v7:
time: 28.2 us; the launch traced here: 28.1 us
  Pallas kernels  17.1 us (61%)
  starting transfers between devices  9.97 us (35%)
  waiting for transfers between devices  0.77 us (3%)
    pallas_call x6, Pallas kernels, call(): pl.pallas_call(kernel, out_shape=out_shape, in_specs=in_specs, out_specs=...  17.1 us
    ppermute x10, starting transfers between devices, exchange(): lax.ppermute(edge, axes, swaps(sizes, *place))  9.97 us
    ppermute x10, waiting for transfers between devices, exchange(): lax.ppermute(edge, axes, swaps(sizes, *place))  0.77 us
  transfers between devices with their start and end apart: 10, of which 2 were waited for; matrix products, arithmetic and copies ran while one was open for 0% of the time, Pallas kernels for 9%

profile of v7, /device:TPU:0, one launch (start us, length us, event | category | flops | bytes accessed | tf_op | source)
XLA Modules:
  0.0 28.1 jit_solution(12483369035514782451)
XLA Ops:
  0.0 0.0 copy-start.1
  0.0 0.0 copy-start.5
  0.0 0.0 copy-start.6
  0.0 0.0 copy-start.4
  0.0 0.0 copy-start.3
  0.0 0.0 copy-start.2
  0.0 0.0 copy-start
  0.0 2.0 %split_operators.1 = (bf16[3,512,512]{2,1,0:T(8,128)(2,1)S(1)}, bf16[3,512,512]{2,1,0:T(8,128)(2,1)S(1)}, bf16[512,256]{1,0:T(8,128)(2,1)S(1)}, bf16[256,512]{1,0:T(8,128)(2,1)S(1)}) custom-call(f32[3,512,512]{2,1,0:T(8,128)} %ops_any.1), custom_call_target="tpu_custom_call" | custom-call | flops 3623878656 | bytes 2359296 | tf_op jit(solution)/shard_map/split_operators/pallas_call | solution.py:530
  2.1 0.0 copy-done.1
  2.1 0.0 copy-done.5
  2.1 0.0 copy-done.6
  2.1 0.0 copy-done.4
  2.1 0.0 copy-done.3
  2.1 0.0 copy-done.2
  2.1 0.0 copy-done
  2.1 5.4 %first_predictor.1 = (f32[4,288,128]{2,1,0:T(8,128)S(1)}, f32[128,128]{1,0:T(8,128)S(1)}, s32[96,128]{1,0:T(8,128)S(1)}, f32[64,128]{1,0:T(8,128)S(1)}, bf16[256...) custom-call(f32[288,512]{1,0:T(8,128)S(1)} %bitcast.16, ...), custom_call_target="tpu_custom_call" | custom-call | flops 7247757312 | bytes 2359296 | tf_op jit(solution)/shard_map/first_predictor/pallas_call | solution.py:530
  7.5 2.4 %collective-permute-start = (f32[40,128]{1,0:T(8,128)S(1)}, f32[40,128]{1,0:T(8,128)S(1)}, u32[]{:S(2)}, u32[]{:S(2)}) collective-permute-start(f32[40,128]{1,0:T(8,128)S(1)} %get-tuple-element.40), channel_id=1, source_target_pairs={{0,6},{1,7},{2,4},{3,5},{4,2},{5,3},{6,0},{7,1},{8,14},{9,15},{10,... | collective-permute-start | bytes 61448 | tf_op jit(solution)/shard_map/ppermute | solution.py:497
  10.0 1.5 %collective-permute-start.1 = (f32[72,128]{1,0:T(8,128)S(1)}, f32[72,128]{1,0:T(8,128)S(1)}, u32[]{:S(2)}, u32[]{:S(2)}) collective-permute-start(f32[72,128]{1,0:T(8,128)S(1)} %get-tuple-element.41), channel_id=1, source_target_pairs={{0,1},{1,0},{2,3},{3,2},{4,5},{5,4},{6,7},{7,6},{8,9},{9,8},{10,11... | collective-permute-start | bytes 110600 | tf_op jit(solution)/shard_map/ppermute | solution.py:497
  11.5 1.6 %collective-permute-start.2 = (f32[72,128]{1,0:T(8,128)S(1)}, f32[72,128]{1,0:T(8,128)S(1)}, u32[]{:S(2)}, u32[]{:S(2)}) collective-permute-start(f32[72,128]{1,0:T(8,128)S(1)} %get-tuple-element.42), channel_id=1, source_target_pairs={{0,8},{1,9},{2,10},{3,11},{4,12},{5,13},{6,14},{7,15},{8,0},{9,1},... | collective-permute-start | bytes 110600 | tf_op jit(solution)/shard_map/ppermute | solution.py:497
  13.1 0.1 collective-permute-start.3
  13.2 0.4 %collective-permute-start.4 = (f32[72,128]{1,0:T(8,128)S(1)}, f32[72,128]{1,0:T(8,128)S(1)}, u32[]{:S(2)}, u32[]{:S(2)}) collective-permute-start(f32[72,128]{1,0:T(8,128)S(1)} %get-tuple-element.44), channel_id=1, source_target_pairs={{0,2},{1,3},{2,0},{3,1},{4,6},{5,7},{6,4},{7,5},{8,10},{9,11},{10,... | collective-permute-start | bytes 110600 | tf_op jit(solution)/shard_map/ppermute | solution.py:497
  13.6 1.3 %inner_update.2.refs_5_ = f32[4,288,128]{2,1,0:T(8,128)S(1)} custom-call(f32[4,288,128]{2,1,0:T(8,128)S(1)} %get-tuple-element.45.refs_0_, bf16[288,512]{1,0:T(8,128)(2,1)S(1)} %get-tuple-element.46.refs_1_, bf16[288,512]{1,0:T(8,128)(2,1)S(1)} %get-tuple-element.47.refs_2_, f32[288,128]{1,0:T(8,128)S(1)} %get-tuple-element.48.refs_3_, ...), custom_call_target="tpu_custom_call" | custom-call | flops 1811939328 | bytes 2359296 | tf_op jit(solution)/shard_map/inner_update/pallas_call | solution.py:530
  14.9 0.0 collective-permute-done.refs_0_
  14.9 0.0 collective-permute-done.1.refs_1_
  14.9 0.6 %collective-permute-done.2.refs_2_ = f32[72,128]{1,0:T(8,128)S(1)} collective-permute-done((f32[72,128]{1,0:T(8,128)S(1)}, f32[72,128]{1,0:T(8,128)S(1)}, u32[]{:S(2)}, u32[]{:S(2)}) %collective-permute-start.2) | collective-permute-done | bytes 36896 | tf_op jit(solution)/shard_map/ppermute | solution.py:497
  15.5 0.0 collective-permute-done.3.refs_3_
  15.5 0.0 collective-permute-done.4.refs_4_
  15.5 5.5 %outer_update_predictor.1 = (f32[4,288,128]{2,1,0:T(8,128)S(1)}, bf16[288,512]{1,0:T(8,128)(2,1)S(1)}, bf16[288,512]{1,0:T(8,128)(2,1)S(1)}, f32[288,128]{1,0:T(...) custom-call(f32[40,128]{1,0:T(8,128)S(1)} %collective-permute-done.r, ...), custom_call_target="tpu_custom_call" | custom-call | flops 7247757312 | bytes 2359296 | tf_op jit(solution)/shard_map/outer_update_predictor/pallas_call | solution.py:530
  21.0 0.1 collective-permute-start.5
  21.1 0.6 %collective-permute-start.6 = (f32[72,128]{1,0:T(8,128)S(1)}, f32[72,128]{1,0:T(8,128)S(1)}, u32[]{:S(2)}, u32[]{:S(2)}) collective-permute-start(f32[72,128]{1,0:T(8,128)S(1)} %get-tuple-element.58), channel_id=1, source_target_pairs={{0,1},{1,0},{2,3},{3,2},{4,5},{5,4},{6,7},{7,6},{8,9},{9,8},{10,11... | collective-permute-start | bytes 110600 | tf_op jit(solution)/shard_map/ppermute | solution.py:497
  21.7 2.7 %collective-permute-start.7 = (f32[72,128]{1,0:T(8,128)S(1)}, f32[72,128]{1,0:T(8,128)S(1)}, u32[]{:S(2)}, u32[]{:S(2)}) collective-permute-start(f32[72,128]{1,0:T(8,128)S(1)} %get-tuple-element.59), channel_id=1, source_target_pairs={{0,8},{1,9},{2,10},{3,11},{4,12},{5,13},{6,14},{7,15},{8,0},{9,1},... | collective-permute-start | bytes 110600 | tf_op jit(solution)/shard_map/ppermute | solution.py:497
  24.4 0.0 collective-permute-start.8
  24.4 0.5 %collective-permute-start.9 = (f32[72,128]{1,0:T(8,128)S(1)}, f32[72,128]{1,0:T(8,128)S(1)}, u32[]{:S(2)}, u32[]{:S(2)}) collective-permute-start(f32[72,128]{1,0:T(8,128)S(1)} %get-tuple-element.61), channel_id=1, source_target_pairs={{0,2},{1,3},{2,0},{3,1},{4,6},{5,7},{6,4},{7,5},{8,10},{9,11},{10,... | collective-permute-start | bytes 110600 | tf_op jit(solution)/shard_map/ppermute | solution.py:497
  24.9 1.3 %inner_update.3.refs_5_ = f32[4,288,128]{2,1,0:T(8,128)S(1)} custom-call(f32[4,288,128]{2,1,0:T(8,128)S(1)} %get-tuple-element.62.refs_0_, bf16[288,512]{1,0:T(8,128)(2,1)S(1)} %get-tuple-element.63.refs_1_, bf16[288,512]{1,0:T(8,128)(2,1)S(1)} %get-tuple-element.64.refs_2_, f32[288,128]{1,0:T(8,128)S(1)} %get-tuple-element.65.refs_3_, ...), custom_call_target="tpu_custom_call" | custom-call | flops 1811939328 | bytes 2359296 | tf_op jit(solution)/shard_map/inner_update/pallas_call | solution.py:530
  26.2 0.0 collective-permute-done.5.refs_0_
  26.2 0.0 collective-permute-done.6.refs_1_
  26.2 0.2 collective-permute-done.7.refs_2_
  26.4 0.0 collective-permute-done.8.refs_3_
  26.4 0.0 collective-permute-done.9.refs_4_
  26.4 1.7 %outer_update.1 = f32[288,512]{1,0:T(8,128)} custom-call(f32[40,128]{1,0:T(8,128)S(1)} %collective-permute-done.5.refs_0_, f32[72,128]{1,0:T(8,128)S(1)} %collective-permute-done.6.refs_1_, f32[72,128]{1,0:T(8,128)S(1)} %collective-permute-done.7.refs_2_, f32[72,128]{1,0:T(8,128)S(1)} %collective-permute-done.8.refs_3_, ...), custom_call_target="tpu_custom_call" | custom-call | flops 1811939328 | bytes 2359296 | tf_op jit(solution)/shard_map/outer_update/pallas_call | solution.py:530
Async XLA Ops:
  0.0 2.1 %copy-start.1 = (s32[1,1,1,6,32]{4,2,3,1,0:T(1,128)S(1)}, s32[1,1,1,6,32]{4,2,3,1,0:T(1,128)}, u32[]{:S(2)}) copy-start(s32[1,1,1,6,32]{4,2,3,1,0:T(1,128)} %param.15) | copy-start | bytes 2308
  0.0 2.1 %copy-start.5 = (s32[1,1,1,32]{3,2,1,0:T(1,128)S(1)}, s32[1,1,1,32]{3,2,1,0:T(1,128)}, u32[]{:S(2)}) copy-start(s32[1,1,1,32]{3,2,1,0:T(1,128)} %param.14) | copy-start | bytes 388
  0.0 2.1 %copy-start.6 = (s32[1,1,1,32]{3,2,1,0:T(1,128)S(1)}, s32[1,1,1,32]{3,2,1,0:T(1,128)}, u32[]{:S(2)}) copy-start(s32[1,1,1,32]{3,2,1,0:T(1,128)} %param.13) | copy-start | bytes 388
  0.0 2.1 %copy-start.4 = (f32[1,1,1,32]{3,2,1,0:T(1,128)S(1)}, f32[1,1,1,32]{3,2,1,0:T(1,128)}, u32[]{:S(2)}) copy-start(f32[1,1,1,32]{3,2,1,0:T(1,128)} %param.12) | copy-start | bytes 388
  0.0 2.1 %copy-start.3 = (f32[1,1,1,32]{3,2,1,0:T(1,128)S(1)}, f32[1,1,1,32]{3,2,1,0:T(1,128)}, u32[]{:S(2)}) copy-start(f32[1,1,1,32]{3,2,1,0:T(1,128)} %param.11) | copy-start | bytes 388
  0.0 2.1 %copy-start.2 = (f32[1,1,1,32]{3,2,1,0:T(1,128)S(1)}, f32[1,1,1,32]{3,2,1,0:T(1,128)}, u32[]{:S(2)}) copy-start(f32[1,1,1,32]{3,2,1,0:T(1,128)} %param.10) | copy-start | bytes 388
  0.0 2.1 %copy-start = (f32[1,1,1,32,9,512]{5,3,4,2,1,0:T(8,128)S(1)}, f32[1,1,1,32,9,512]{5,3,4,2,1,0:T(8,128)}, u32[]{:S(2)}) copy-start(f32[1,1,1,32,9,512]{5,3,4,2,1,0:T(8,128)} %param.8) | copy-start | bytes 1769476
  7.5 7.4 %collective-permute-start = (f32[40,128]{1,0:T(8,128)S(1)}, f32[40,128]{1,0:T(8,128)S(1)}, u32[]{:S(2)}, u32[]{:S(2)}) collective-permute-start(f32[40,128]{1,0:T(8,128)S(1)} %get-tuple-element.40), channel_id=1, source_target_pairs={{0,6},{1,7},{2,4},{3,5},{4,2},{5,3},{6,0},{7,1},{8,14},{9,15},{10,... | collective-permute-start | bytes 61448 | tf_op jit(solution)/shard_map/ppermute | solution.py:497
  10.0 4.9 %collective-permute-start.1 = (f32[72,128]{1,0:T(8,128)S(1)}, f32[72,128]{1,0:T(8,128)S(1)}, u32[]{:S(2)}, u32[]{:S(2)}) collective-permute-start(f32[72,128]{1,0:T(8,128)S(1)} %get-tuple-element.41), channel_id=1, source_target_pairs={{0,1},{1,0},{2,3},{3,2},{4,5},{5,4},{6,7},{7,6},{8,9},{9,8},{10,11... | collective-permute-start | bytes 110600 | tf_op jit(solution)/shard_map/ppermute | solution.py:497
  11.5 4.0 %collective-permute-start.2 = (f32[72,128]{1,0:T(8,128)S(1)}, f32[72,128]{1,0:T(8,128)S(1)}, u32[]{:S(2)}, u32[]{:S(2)}) collective-permute-start(f32[72,128]{1,0:T(8,128)S(1)} %get-tuple-element.42), channel_id=1, source_target_pairs={{0,8},{1,9},{2,10},{3,11},{4,12},{5,13},{6,14},{7,15},{8,0},{9,1},... | collective-permute-start | bytes 110600 | tf_op jit(solution)/shard_map/ppermute | solution.py:497
  13.1 2.4 %collective-permute-start.3 = (f32[72,128]{1,0:T(8,128)S(1)}, f32[72,128]{1,0:T(8,128)S(1)}, u32[]{:S(2)}, u32[]{:S(2)}) collective-permute-start(f32[72,128]{1,0:T(8,128)S(1)} %get-tuple-element.43), channel_id=1, source_target_pairs={{0,2},{1,3},{2,0},{3,1},{4,6},{5,7},{6,4},{7,5},{8,16},{9,17},{10,... | collective-permute-start | bytes 110600 | tf_op jit(solution)/shard_map/ppermute | solution.py:497
  13.2 2.3 %collective-permute-start.4 = (f32[72,128]{1,0:T(8,128)S(1)}, f32[72,128]{1,0:T(8,128)S(1)}, u32[]{:S(2)}, u32[]{:S(2)}) collective-permute-start(f32[72,128]{1,0:T(8,128)S(1)} %get-tuple-element.44), channel_id=1, source_target_pairs={{0,2},{1,3},{2,0},{3,1},{4,6},{5,7},{6,4},{7,5},{8,10},{9,11},{10,... | collective-permute-start | bytes 110600 | tf_op jit(solution)/shard_map/ppermute | solution.py:497
  21.0 5.2 %collective-permute-start.5 = (f32[40,128]{1,0:T(8,128)S(1)}, f32[40,128]{1,0:T(8,128)S(1)}, u32[]{:S(2)}, u32[]{:S(2)}) collective-permute-start(f32[40,128]{1,0:T(8,128)S(1)} %get-tuple-element.57), channel_id=1, source_target_pairs={{0,6},{1,7},{2,4},{3,5},{4,2},{5,3},{6,0},{7,1},{8,14},{9,15},{10,... | collective-permute-start | bytes 61448 | tf_op jit(solution)/shard_map/ppermute | solution.py:497
  21.1 5.1 %collective-permute-start.6 = (f32[72,128]{1,0:T(8,128)S(1)}, f32[72,128]{1,0:T(8,128)S(1)}, u32[]{:S(2)}, u32[]{:S(2)}) collective-permute-start(f32[72,128]{1,0:T(8,128)S(1)} %get-tuple-element.58), channel_id=1, source_target_pairs={{0,1},{1,0},{2,3},{3,2},{4,5},{5,4},{6,7},{7,6},{8,9},{9,8},{10,11... | collective-permute-start | bytes 110600 | tf_op jit(solution)/shard_map/ppermute | solution.py:497
  21.7 4.7 %collective-permute-start.7 = (f32[72,128]{1,0:T(8,128)S(1)}, f32[72,128]{1,0:T(8,128)S(1)}, u32[]{:S(2)}, u32[]{:S(2)}) collective-permute-start(f32[72,128]{1,0:T(8,128)S(1)} %get-tuple-element.59), channel_id=1, source_target_pairs={{0,8},{1,9},{2,10},{3,11},{4,12},{5,13},{6,14},{7,15},{8,0},{9,1},... | collective-permute-start | bytes 110600 | tf_op jit(solution)/shard_map/ppermute | solution.py:497
  24.4 2.0 %collective-permute-start.8 = (f32[72,128]{1,0:T(8,128)S(1)}, f32[72,128]{1,0:T(8,128)S(1)}, u32[]{:S(2)}, u32[]{:S(2)}) collective-permute-start(f32[72,128]{1,0:T(8,128)S(1)} %get-tuple-element.60), channel_id=1, source_target_pairs={{0,2},{1,3},{2,0},{3,1},{4,6},{5,7},{6,4},{7,5},{8,16},{9,17},{10,... | collective-permute-start | bytes 110600 | tf_op jit(solution)/shard_map/ppermute | solution.py:497
  24.4 1.9 %collective-permute-start.9 = (f32[72,128]{1,0:T(8,128)S(1)}, f32[72,128]{1,0:T(8,128)S(1)}, u32[]{:S(2)}, u32[]{:S(2)}) collective-permute-start(f32[72,128]{1,0:T(8,128)S(1)} %get-tuple-element.61), channel_id=1, source_target_pairs={{0,2},{1,3},{2,0},{3,1},{4,6},{5,7},{6,4},{7,5},{8,10},{9,11},{10,... | collective-permute-start | bytes 110600 | tf_op jit(solution)/shard_map/ppermute | solution.py:497

commit v8 on v7

--- a/solution.py
+++ b/solution.py
@@ -86,7 +86,7 @@
                 top = jnp.concatenate([high[f * stride : f * stride + rows, depth] for f in PICKED[dim]], axis=0)
                 rest = jnp.concatenate([low[f * stride : f * stride + rows, depth] for f in PICKED[dim]], axis=0)
                 both = dot(jnp.concatenate([top, rest], axis=0), w_high[dim, depth, cols])
-                part = both[: 6 * rows] + both[6 * rows :] + dot(top, w_low[dim, depth, cols])
+                part = both[: 6 * rows] + (both[6 * rows :] + dot(top, w_low[dim, depth, cols]))
                 deriv[dim] = part if deriv[dim] is None else deriv[dim] + part
         combine(deriv, rows, inv_rho, lame, shear, shear2, cols, emit)
 

time: 28.2 us -> 28.2 us (level)
  no operation moved by 1% of the time
where the time goes in v8:
time: 28.2 us; the launch traced here: 28.1 us
  Pallas kernels  17.1 us (61%)
  starting transfers between devices  9.97 us (35%)
  waiting for transfers between devices  0.77 us (3%)
    pallas_call x6, Pallas kernels, call(): pl.pallas_call(kernel, out_shape=out_shape, in_specs=in_specs, out_specs=...  17.1 us
    ppermute x10, starting transfers between devices, exchange(): lax.ppermute(edge, axes, swaps(sizes, *place))  9.97 us
    ppermute x10, waiting for transfers between devices, exchange(): lax.ppermute(edge, axes, swaps(sizes, *place))  0.77 us
  transfers between devices with their start and end apart: 10, of which 2 were waited for; matrix products, arithmetic and copies ran while one was open for 0% of the time, Pallas kernels for 9%

profile of v8, /device:TPU:0, one launch (start us, length us, event | category | flops | bytes accessed | tf_op | source)
XLA Modules:
  0.0 28.1 jit_solution(12483369035514782451)
XLA Ops:
  0.0 0.0 copy-start.1
  0.0 0.0 copy-start.5
  0.0 0.0 copy-start.6
  0.0 0.0 copy-start.4
  0.0 0.0 copy-start.3
  0.0 0.0 copy-start.2
  0.0 0.0 copy-start
  0.0 2.0 %split_operators.1 = (bf16[3,512,512]{2,1,0:T(8,128)(2,1)S(1)}, bf16[3,512,512]{2,1,0:T(8,128)(2,1)S(1)}, bf16[512,256]{1,0:T(8,128)(2,1)S(1)}, bf16[256,512]{1,0:T(8,128)(2,1)S(1)}) custom-call(f32[3,512,512]{2,1,0:T(8,128)} %ops_any.1), custom_call_target="tpu_custom_call" | custom-call | flops 3623878656 | bytes 2359296 | tf_op jit(solution)/shard_map/split_operators/pallas_call | solution.py:530
  2.1 0.0 copy-done.1
  2.1 0.0 copy-done.5
  2.1 0.0 copy-done.6
  2.1 0.0 copy-done.4
  2.1 0.0 copy-done.3
  2.1 0.0 copy-done.2
  2.1 0.0 copy-done
  2.1 5.4 %first_predictor.1 = (f32[4,288,128]{2,1,0:T(8,128)S(1)}, f32[128,128]{1,0:T(8,128)S(1)}, s32[96,128]{1,0:T(8,128)S(1)}, f32[64,128]{1,0:T(8,128)S(1)}, bf16[256...) custom-call(f32[288,512]{1,0:T(8,128)S(1)} %bitcast.16, ...), custom_call_target="tpu_custom_call" | custom-call | flops 7247757312 | bytes 2359296 | tf_op jit(solution)/shard_map/first_predictor/pallas_call | solution.py:530
  7.5 2.4 %collective-permute-start = (f32[40,128]{1,0:T(8,128)S(1)}, f32[40,128]{1,0:T(8,128)S(1)}, u32[]{:S(2)}, u32[]{:S(2)}) collective-permute-start(f32[40,128]{1,0:T(8,128)S(1)} %get-tuple-element.40), channel_id=1, source_target_pairs={{0,6},{1,7},{2,4},{3,5},{4,2},{5,3},{6,0},{7,1},{8,14},{9,15},{10,... | collective-permute-start | bytes 61448 | tf_op jit(solution)/shard_map/ppermute | solution.py:497
  10.0 1.5 %collective-permute-start.1 = (f32[72,128]{1,0:T(8,128)S(1)}, f32[72,128]{1,0:T(8,128)S(1)}, u32[]{:S(2)}, u32[]{:S(2)}) collective-permute-start(f32[72,128]{1,0:T(8,128)S(1)} %get-tuple-element.41), channel_id=1, source_target_pairs={{0,1},{1,0},{2,3},{3,2},{4,5},{5,4},{6,7},{7,6},{8,9},{9,8},{10,11... | collective-permute-start | bytes 110600 | tf_op jit(solution)/shard_map/ppermute | solution.py:497
  11.5 1.6 %collective-permute-start.2 = (f32[72,128]{1,0:T(8,128)S(1)}, f32[72,128]{1,0:T(8,128)S(1)}, u32[]{:S(2)}, u32[]{:S(2)}) collective-permute-start(f32[72,128]{1,0:T(8,128)S(1)} %get-tuple-element.42), channel_id=1, source_target_pairs={{0,8},{1,9},{2,10},{3,11},{4,12},{5,13},{6,14},{7,15},{8,0},{9,1},... | collective-permute-start | bytes 110600 | tf_op jit(solution)/shard_map/ppermute | solution.py:497
  13.1 0.1 collective-permute-start.3
  13.2 0.4 %collective-permute-start.4 = (f32[72,128]{1,0:T(8,128)S(1)}, f32[72,128]{1,0:T(8,128)S(1)}, u32[]{:S(2)}, u32[]{:S(2)}) collective-permute-start(f32[72,128]{1,0:T(8,128)S(1)} %get-tuple-element.44), channel_id=1, source_target_pairs={{0,2},{1,3},{2,0},{3,1},{4,6},{5,7},{6,4},{7,5},{8,10},{9,11},{10,... | collective-permute-start | bytes 110600 | tf_op jit(solution)/shard_map/ppermute | solution.py:497
  13.6 1.3 %inner_update.2.refs_5_ = f32[4,288,128]{2,1,0:T(8,128)S(1)} custom-call(f32[4,288,128]{2,1,0:T(8,128)S(1)} %get-tuple-element.45.refs_0_, bf16[288,512]{1,0:T(8,128)(2,1)S(1)} %get-tuple-element.46.refs_1_, bf16[288,512]{1,0:T(8,128)(2,1)S(1)} %get-tuple-element.47.refs_2_, f32[288,128]{1,0:T(8,128)S(1)} %get-tuple-element.48.refs_3_, ...), custom_call_target="tpu_custom_call" | custom-call | flops 1811939328 | bytes 2359296 | tf_op jit(solution)/shard_map/inner_update/pallas_call | solution.py:530
  14.9 0.0 collective-permute-done.refs_0_
  14.9 0.0 collective-permute-done.1.refs_1_
  14.9 0.6 %collective-permute-done.2.refs_2_ = f32[72,128]{1,0:T(8,128)S(1)} collective-permute-done((f32[72,128]{1,0:T(8,128)S(1)}, f32[72,128]{1,0:T(8,128)S(1)}, u32[]{:S(2)}, u32[]{:S(2)}) %collective-permute-start.2) | collective-permute-done | bytes 36896 | tf_op jit(solution)/shard_map/ppermute | solution.py:497
  15.5 0.0 collective-permute-done.3.refs_3_
  15.5 0.0 collective-permute-done.4.refs_4_
  15.5 5.5 %outer_update_predictor.1 = (f32[4,288,128]{2,1,0:T(8,128)S(1)}, bf16[288,512]{1,0:T(8,128)(2,1)S(1)}, bf16[288,512]{1,0:T(8,128)(2,1)S(1)}, f32[288,128]{1,0:T(...) custom-call(f32[40,128]{1,0:T(8,128)S(1)} %collective-permute-done.r, ...), custom_call_target="tpu_custom_call" | custom-call | flops 7247757312 | bytes 2359296 | tf_op jit(solution)/shard_map/outer_update_predictor/pallas_call | solution.py:530
  21.0 0.1 collective-permute-start.5
  21.1 0.6 %collective-permute-start.6 = (f32[72,128]{1,0:T(8,128)S(1)}, f32[72,128]{1,0:T(8,128)S(1)}, u32[]{:S(2)}, u32[]{:S(2)}) collective-permute-start(f32[72,128]{1,0:T(8,128)S(1)} %get-tuple-element.58), channel_id=1, source_target_pairs={{0,1},{1,0},{2,3},{3,2},{4,5},{5,4},{6,7},{7,6},{8,9},{9,8},{10,11... | collective-permute-start | bytes 110600 | tf_op jit(solution)/shard_map/ppermute | solution.py:497
  21.7 2.7 %collective-permute-start.7 = (f32[72,128]{1,0:T(8,128)S(1)}, f32[72,128]{1,0:T(8,128)S(1)}, u32[]{:S(2)}, u32[]{:S(2)}) collective-permute-start(f32[72,128]{1,0:T(8,128)S(1)} %get-tuple-element.59), channel_id=1, source_target_pairs={{0,8},{1,9},{2,10},{3,11},{4,12},{5,13},{6,14},{7,15},{8,0},{9,1},... | collective-permute-start | bytes 110600 | tf_op jit(solution)/shard_map/ppermute | solution.py:497
  24.4 0.0 collective-permute-start.8
  24.4 0.5 %collective-permute-start.9 = (f32[72,128]{1,0:T(8,128)S(1)}, f32[72,128]{1,0:T(8,128)S(1)}, u32[]{:S(2)}, u32[]{:S(2)}) collective-permute-start(f32[72,128]{1,0:T(8,128)S(1)} %get-tuple-element.61), channel_id=1, source_target_pairs={{0,2},{1,3},{2,0},{3,1},{4,6},{5,7},{6,4},{7,5},{8,10},{9,11},{10,... | collective-permute-start | bytes 110600 | tf_op jit(solution)/shard_map/ppermute | solution.py:497
  24.9 1.3 %inner_update.3.refs_5_ = f32[4,288,128]{2,1,0:T(8,128)S(1)} custom-call(f32[4,288,128]{2,1,0:T(8,128)S(1)} %get-tuple-element.62.refs_0_, bf16[288,512]{1,0:T(8,128)(2,1)S(1)} %get-tuple-element.63.refs_1_, bf16[288,512]{1,0:T(8,128)(2,1)S(1)} %get-tuple-element.64.refs_2_, f32[288,128]{1,0:T(8,128)S(1)} %get-tuple-element.65.refs_3_, ...), custom_call_target="tpu_custom_call" | custom-call | flops 1811939328 | bytes 2359296 | tf_op jit(solution)/shard_map/inner_update/pallas_call | solution.py:530
  26.2 0.0 collective-permute-done.5.refs_0_
  26.2 0.0 collective-permute-done.6.refs_1_
  26.2 0.2 collective-permute-done.7.refs_2_
  26.4 0.0 collective-permute-done.8.refs_3_
  26.4 0.0 collective-permute-done.9.refs_4_
  26.4 1.7 %outer_update.1 = f32[288,512]{1,0:T(8,128)} custom-call(f32[40,128]{1,0:T(8,128)S(1)} %collective-permute-done.5.refs_0_, f32[72,128]{1,0:T(8,128)S(1)} %collective-permute-done.6.refs_1_, f32[72,128]{1,0:T(8,128)S(1)} %collective-permute-done.7.refs_2_, f32[72,128]{1,0:T(8,128)S(1)} %collective-permute-done.8.refs_3_, ...), custom_call_target="tpu_custom_call" | custom-call | flops 1811939328 | bytes 2359296 | tf_op jit(solution)/shard_map/outer_update/pallas_call | solution.py:530
Async XLA Ops:
  0.0 2.1 %copy-start.1 = (s32[1,1,1,6,32]{4,2,3,1,0:T(1,128)S(1)}, s32[1,1,1,6,32]{4,2,3,1,0:T(1,128)}, u32[]{:S(2)}) copy-start(s32[1,1,1,6,32]{4,2,3,1,0:T(1,128)} %param.15) | copy-start | bytes 2308
  0.0 2.1 %copy-start.5 = (s32[1,1,1,32]{3,2,1,0:T(1,128)S(1)}, s32[1,1,1,32]{3,2,1,0:T(1,128)}, u32[]{:S(2)}) copy-start(s32[1,1,1,32]{3,2,1,0:T(1,128)} %param.14) | copy-start | bytes 388
  0.0 2.1 %copy-start.6 = (s32[1,1,1,32]{3,2,1,0:T(1,128)S(1)}, s32[1,1,1,32]{3,2,1,0:T(1,128)}, u32[]{:S(2)}) copy-start(s32[1,1,1,32]{3,2,1,0:T(1,128)} %param.13) | copy-start | bytes 388
  0.0 2.1 %copy-start.4 = (f32[1,1,1,32]{3,2,1,0:T(1,128)S(1)}, f32[1,1,1,32]{3,2,1,0:T(1,128)}, u32[]{:S(2)}) copy-start(f32[1,1,1,32]{3,2,1,0:T(1,128)} %param.12) | copy-start | bytes 388
  0.0 2.1 %copy-start.3 = (f32[1,1,1,32]{3,2,1,0:T(1,128)S(1)}, f32[1,1,1,32]{3,2,1,0:T(1,128)}, u32[]{:S(2)}) copy-start(f32[1,1,1,32]{3,2,1,0:T(1,128)} %param.11) | copy-start | bytes 388
  0.0 2.1 %copy-start.2 = (f32[1,1,1,32]{3,2,1,0:T(1,128)S(1)}, f32[1,1,1,32]{3,2,1,0:T(1,128)}, u32[]{:S(2)}) copy-start(f32[1,1,1,32]{3,2,1,0:T(1,128)} %param.10) | copy-start | bytes 388
  0.0 2.1 %copy-start = (f32[1,1,1,32,9,512]{5,3,4,2,1,0:T(8,128)S(1)}, f32[1,1,1,32,9,512]{5,3,4,2,1,0:T(8,128)}, u32[]{:S(2)}) copy-start(f32[1,1,1,32,9,512]{5,3,4,2,1,0:T(8,128)} %param.8) | copy-start | bytes 1769476
  7.5 7.4 %collective-permute-start = (f32[40,128]{1,0:T(8,128)S(1)}, f32[40,128]{1,0:T(8,128)S(1)}, u32[]{:S(2)}, u32[]{:S(2)}) collective-permute-start(f32[40,128]{1,0:T(8,128)S(1)} %get-tuple-element.40), channel_id=1, source_target_pairs={{0,6},{1,7},{2,4},{3,5},{4,2},{5,3},{6,0},{7,1},{8,14},{9,15},{10,... | collective-permute-start | bytes 61448 | tf_op jit(solution)/shard_map/ppermute | solution.py:497
  10.0 4.9 %collective-permute-start.1 = (f32[72,128]{1,0:T(8,128)S(1)}, f32[72,128]{1,0:T(8,128)S(1)}, u32[]{:S(2)}, u32[]{:S(2)}) collective-permute-start(f32[72,128]{1,0:T(8,128)S(1)} %get-tuple-element.41), channel_id=1, source_target_pairs={{0,1},{1,0},{2,3},{3,2},{4,5},{5,4},{6,7},{7,6},{8,9},{9,8},{10,11... | collective-permute-start | bytes 110600 | tf_op jit(solution)/shard_map/ppermute | solution.py:497
  11.5 4.0 %collective-permute-start.2 = (f32[72,128]{1,0:T(8,128)S(1)}, f32[72,128]{1,0:T(8,128)S(1)}, u32[]{:S(2)}, u32[]{:S(2)}) collective-permute-start(f32[72,128]{1,0:T(8,128)S(1)} %get-tuple-element.42), channel_id=1, source_target_pairs={{0,8},{1,9},{2,10},{3,11},{4,12},{5,13},{6,14},{7,15},{8,0},{9,1},... | collective-permute-start | bytes 110600 | tf_op jit(solution)/shard_map/ppermute | solution.py:497
  13.1 2.4 %collective-permute-start.3 = (f32[72,128]{1,0:T(8,128)S(1)}, f32[72,128]{1,0:T(8,128)S(1)}, u32[]{:S(2)}, u32[]{:S(2)}) collective-permute-start(f32[72,128]{1,0:T(8,128)S(1)} %get-tuple-element.43), channel_id=1, source_target_pairs={{0,2},{1,3},{2,0},{3,1},{4,6},{5,7},{6,4},{7,5},{8,16},{9,17},{10,... | collective-permute-start | bytes 110600 | tf_op jit(solution)/shard_map/ppermute | solution.py:497
  13.2 2.3 %collective-permute-start.4 = (f32[72,128]{1,0:T(8,128)S(1)}, f32[72,128]{1,0:T(8,128)S(1)}, u32[]{:S(2)}, u32[]{:S(2)}) collective-permute-start(f32[72,128]{1,0:T(8,128)S(1)} %get-tuple-element.44), channel_id=1, source_target_pairs={{0,2},{1,3},{2,0},{3,1},{4,6},{5,7},{6,4},{7,5},{8,10},{9,11},{10,... | collective-permute-start | bytes 110600 | tf_op jit(solution)/shard_map/ppermute | solution.py:497
  21.0 5.2 %collective-permute-start.5 = (f32[40,128]{1,0:T(8,128)S(1)}, f32[40,128]{1,0:T(8,128)S(1)}, u32[]{:S(2)}, u32[]{:S(2)}) collective-permute-start(f32[40,128]{1,0:T(8,128)S(1)} %get-tuple-element.57), channel_id=1, source_target_pairs={{0,6},{1,7},{2,4},{3,5},{4,2},{5,3},{6,0},{7,1},{8,14},{9,15},{10,... | collective-permute-start | bytes 61448 | tf_op jit(solution)/shard_map/ppermute | solution.py:497
  21.1 5.1 %collective-permute-start.6 = (f32[72,128]{1,0:T(8,128)S(1)}, f32[72,128]{1,0:T(8,128)S(1)}, u32[]{:S(2)}, u32[]{:S(2)}) collective-permute-start(f32[72,128]{1,0:T(8,128)S(1)} %get-tuple-element.58), channel_id=1, source_target_pairs={{0,1},{1,0},{2,3},{3,2},{4,5},{5,4},{6,7},{7,6},{8,9},{9,8},{10,11... | collective-permute-start | bytes 110600 | tf_op jit(solution)/shard_map/ppermute | solution.py:497
  21.7 4.7 %collective-permute-start.7 = (f32[72,128]{1,0:T(8,128)S(1)}, f32[72,128]{1,0:T(8,128)S(1)}, u32[]{:S(2)}, u32[]{:S(2)}) collective-permute-start(f32[72,128]{1,0:T(8,128)S(1)} %get-tuple-element.59), channel_id=1, source_target_pairs={{0,8},{1,9},{2,10},{3,11},{4,12},{5,13},{6,14},{7,15},{8,0},{9,1},... | collective-permute-start | bytes 110600 | tf_op jit(solution)/shard_map/ppermute | solution.py:497
  24.4 2.0 %collective-permute-start.8 = (f32[72,128]{1,0:T(8,128)S(1)}, f32[72,128]{1,0:T(8,128)S(1)}, u32[]{:S(2)}, u32[]{:S(2)}) collective-permute-start(f32[72,128]{1,0:T(8,128)S(1)} %get-tuple-element.60), channel_id=1, source_target_pairs={{0,2},{1,3},{2,0},{3,1},{4,6},{5,7},{6,4},{7,5},{8,16},{9,17},{10,... | collective-permute-start | bytes 110600 | tf_op jit(solution)/shard_map/ppermute | solution.py:497
  24.4 1.9 %collective-permute-start.9 = (f32[72,128]{1,0:T(8,128)S(1)}, f32[72,128]{1,0:T(8,128)S(1)}, u32[]{:S(2)}, u32[]{:S(2)}) collective-permute-start(f32[72,128]{1,0:T(8,128)S(1)} %get-tuple-element.61), channel_id=1, source_target_pairs={{0,2},{1,3},{2,0},{3,1},{4,6},{5,7},{6,4},{7,5},{8,10},{9,11},{10,... | collective-permute-start | bytes 110600 | tf_op jit(solution)/shard_map/ppermute | solution.py:497
